TPU v7x, 32 devices: a whole 2x2x4 slice. The times are simulated.
32 devices in a mesh: dp: 8 (over y, x, core), mp: 4 (over z).
Axes of the slice: x: 2, y: 2, z: 4, core: 2. Of those that a mesh axis runs over, the one named last changes fastest.
Arguments:
- tokens: bfloat16 [27648, 768], P(('dp', 'mp')), may hold values from -6 to 6
- scene_ids: int32 [27648], P('dp'), may hold values from -1 to 3, as said below
- gain_one: float32 [768], replicated, may hold values from 0.25 to 1.75
- shift_one: float32 [768], replicated, may hold values from -4 to 4
- w_qkv: bfloat16 [3, 768, 768], P(None, None, 'mp'), may hold values from -0.3125 to 0.3125
- w_out: bfloat16 [768, 768], P('mp'), may hold values from -0.875 to 0.875
- b_out: float32 [768], replicated, may hold values from -4 to 4
- gain_two: float32 [768], replicated, may hold values from 0.25 to 1.75
- shift_two: float32 [768], replicated, may hold values from -4 to 4
- w_up: bfloat16 [768, 1536], P(None, 'mp'), may hold values from -0.21875 to 0.21875
- b_up: float32 [1536], P('mp'), may hold values from -6 to 6
- w_down: bfloat16 [1536, 768], P('mp'), may hold values from -0.15625 to 0.15625
- b_down: float32 [768], replicated, may hold values from -4 to 4
- cotangent: bfloat16 [27648, 768], P(('dp', 'mp')), may hold values from -6 to 6
Outputs:
- layer_out: bfloat16 [27648, 768], P(('dp', 'mp'))
- tokens_grad: float32 [27648, 768], P(('dp', 'mp'))
- gain_one_grad: float32 [768], replicated
- shift_one_grad: float32 [768], replicated
- w_qkv_grad: float32 [3, 768, 768], P(None, None, 'mp')
- w_out_grad: float32 [768, 768], P('mp')
- b_out_grad: float32 [768], replicated
- gain_two_grad: float32 [768], replicated
- shift_two_grad: float32 [768], replicated
- w_up_grad: float32 [768, 1536], P(None, 'mp')
- b_up_grad: float32 [1536], P('mp')
- w_down_grad: float32 [1536, 768], P('mp')
- b_down_grad: float32 [768], replicated
Inputs may be any that keep to these rules, and one draw needn't show every extreme that they name: `scene_ids`: within each packed sequence of 3456 tokens the scene numbers start at 0 and never fall, each scene is one contiguous run of at least 600 and at most 1500 tokens, a sequence holds two to four scenes, and -1 marks padding after its last scene.
All inputs are finite; a program needn't handle non-finite values.
Results may differ from a plain program's by a relative error of at most 0.018.
The roundings to bfloat16 on the way count: a program that leaves them out, or rounds other values in their place, can miss the bound.
Values may be sent and summed in bfloat16 or wider, within the bound.
A program may use at most 192 MiB of HBM per device.

v0:
```python
import jax
import jax.numpy as jnp
from jax import lax
from jax.sharding import PartitionSpec as P

HEAD = 64
SEQ = 3456
BLOCK_ROWS = 576


epsilon = 1e-05
masked_value = -1e30


def layer_norm(values, gain_vec, shift_vec):
    average = jnp.mean(values, axis=-1, keepdims=True)
    centred = values - average
    variance = jnp.mean(centred * centred, axis=-1, keepdims=True)
    return centred * lax.rsqrt(variance + epsilon) * gain_vec + shift_vec


def exact_gelu(values):
    return jax.nn.gelu(values, approximate=False)


def allowed_pairs(query_ids, key_ids, query_place, key_place):
    same_scene = (query_ids[:, None] == key_ids[None, :]) & (query_ids[:, None] >= 0)
    return same_scene | (query_place[:, None] == key_place[None, :])


def add_rows(totals, addend):
    return totals + addend


def shards(
    tokens,
    scene_ids,
    gain_one,
    shift_one,
    w_qkv,
    w_out,
    b_out,
    gain_two,
    shift_two,
    w_up,
    b_up,
    w_down,
    b_down,
    cotangent,
):
    all_rows = scene_ids.shape[0]
    local_heads = w_qkv.shape[2] // HEAD
    local_width = local_heads * HEAD
    block_total = all_rows // BLOCK_ROWS
    scaling = HEAD ** (-0.5)
    residual_in = tokens.astype(jnp.float32)
    normed_one = layer_norm(residual_in, gain_one, shift_one).astype(jnp.bfloat16)
    normed_full = lax.all_gather(normed_one, "mp", axis=0, tiled=True)
    projected = jnp.einsum(
        "td,cde->cte", normed_full, w_qkv, preferred_element_type=jnp.float32
    ).astype(jnp.bfloat16)
    queries = projected[0].reshape(all_rows, local_heads, HEAD)
    key_rows = projected[1].reshape(all_rows, local_heads, HEAD)
    value_rows = projected[2].reshape(all_rows, local_heads, HEAD)
    key_place = jnp.arange(SEQ, dtype=jnp.int32)

    def block_view(block_index):
        first_row = block_index * BLOCK_ROWS
        seq_start = first_row // SEQ * SEQ
        query_blk = lax.dynamic_slice_in_dim(queries, first_row, BLOCK_ROWS, 0)
        query_ids = lax.dynamic_slice_in_dim(scene_ids, first_row, BLOCK_ROWS, 0)
        query_place = first_row - seq_start + jnp.arange(BLOCK_ROWS, dtype=jnp.int32)
        allowed = allowed_pairs(query_ids, scene_ids, query_place, key_place)
        raw_scores = (
            jnp.einsum("qhd,khd->hqk", query_blk, key_rows, preferred_element_type=jnp.float32)
            * scaling
        )
        shifted = jnp.where(allowed[None], raw_scores, masked_value)
        keep_rows = (query_ids >= 0).astype(jnp.float32)
        return (first_row, seq_start, query_blk, key_rows, value_rows, shifted, keep_rows)

    def forward_block(block_index):
        first_row, seq_start, query_blk, key_seq, value_seq, shifted, keep_rows = block_view(
            block_index
        )
        row_top = jnp.max(shifted, axis=-1, keepdims=True)
        weights = jnp.exp(shifted - row_top)
        row_total = jnp.sum(weights, axis=-1, keepdims=True)
        probs_low = (weights / row_total).astype(jnp.bfloat16)
        mixed_rows = jnp.einsum(
            "hqk,khd->qhd", probs_low, value_seq, preferred_element_type=jnp.float32
        )
        mixed_rows = (mixed_rows * keep_rows[:, None, None]).astype(jnp.bfloat16)
        return (mixed_rows, (row_top + jnp.log(row_total))[..., 0])

    mixed_blocks, log_totals = lax.map(forward_block, jnp.arange(block_total, dtype=jnp.int32))
    attended = mixed_blocks.reshape(all_rows, local_width)
    branch_out = lax.psum_scatter(
        jnp.dot(attended, w_out, preferred_element_type=jnp.float32).astype(jnp.bfloat16),
        "mp",
        scatter_dimension=0,
        tiled=True,
    ).astype(jnp.float32)
    middle = residual_in + branch_out + b_out
    normed_two = layer_norm(middle, gain_two, shift_two).astype(jnp.bfloat16)
    mlp_input = lax.all_gather(normed_two, "mp", axis=0, tiled=True)
    hidden = jnp.dot(mlp_input, w_up, preferred_element_type=jnp.float32) + b_up
    active = exact_gelu(hidden).astype(jnp.bfloat16)
    branch_mlp = lax.psum_scatter(
        jnp.dot(active, w_down, preferred_element_type=jnp.float32).astype(jnp.bfloat16),
        "mp",
        scatter_dimension=0,
        tiled=True,
    ).astype(jnp.float32)
    layer_out = (middle + branch_mlp + b_down).astype(jnp.bfloat16)
    grad_output = cotangent.astype(jnp.float32)
    grad_full = lax.all_gather(cotangent, "mp", axis=0, tiled=True)
    grad_down = jnp.einsum("tf,td->fd", active, grad_full, preferred_element_type=jnp.float32)
    grad_active = jnp.einsum("td,fd->tf", grad_full, w_down, preferred_element_type=jnp.float32)
    grad_hidden = jax.vjp(exact_gelu, hidden)[1](grad_active)[0].astype(jnp.bfloat16)
    grad_up = jnp.einsum("td,tf->df", mlp_input, grad_hidden, preferred_element_type=jnp.float32)
    grad_up_bias = jnp.sum(grad_hidden.astype(jnp.float32), axis=0)
    grad_normed_two = lax.psum_scatter(
        jnp.einsum("tf,df->td", grad_hidden, w_up, preferred_element_type=jnp.float32).astype(
            jnp.bfloat16
        ),
        "mp",
        scatter_dimension=0,
        tiled=True,
    ).astype(jnp.float32)
    norm_two_back = jax.vjp(layer_norm, middle, gain_two, shift_two)[1]
    grad_middle_part, grad_gain_two, grad_shift_two = norm_two_back(grad_normed_two)
    grad_middle = grad_output + grad_middle_part
    grad_middle_low = grad_middle.astype(jnp.bfloat16)
    middle_full = lax.all_gather(grad_middle_low, "mp", axis=0, tiled=True)
    grad_out_weight = jnp.einsum(
        "te,td->ed", attended, middle_full, preferred_element_type=jnp.float32
    )
    grad_attended = jnp.einsum(
        "td,ed->te", middle_full, w_out, preferred_element_type=jnp.float32
    ).astype(jnp.bfloat16)
    grad_heads = grad_attended.reshape(all_rows, local_heads, HEAD)

    def backward_block(carried, block_index):
        key_grads, value_grads = carried
        first_row, seq_start, query_blk, key_seq, value_seq, shifted, keep_rows = block_view(
            block_index
        )
        log_total = lax.dynamic_index_in_dim(log_totals, block_index, 0, keepdims=False)
        attn_probs = jnp.exp(shifted - log_total[..., None])
        probs_low = attn_probs.astype(jnp.bfloat16)
        grad_blk = lax.dynamic_slice_in_dim(grad_heads, first_row, BLOCK_ROWS, 0) * keep_rows[
            :, None, None
        ].astype(jnp.bfloat16)
        grad_probs = jnp.einsum(
            "qhd,khd->hqk", grad_blk, value_seq, preferred_element_type=jnp.float32
        )
        value_part = jnp.einsum(
            "hqk,qhd->khd", probs_low, grad_blk, preferred_element_type=jnp.float32
        )
        inner_sum = jnp.sum(attn_probs * grad_probs, axis=-1, keepdims=True)
        grad_scores = (attn_probs * (grad_probs - inner_sum)).astype(jnp.bfloat16)
        query_grad = (
            jnp.einsum("hqk,khd->qhd", grad_scores, key_seq, preferred_element_type=jnp.float32)
            * scaling
        )
        key_part = (
            jnp.einsum("hqk,qhd->khd", grad_scores, query_blk, preferred_element_type=jnp.float32)
            * scaling
        )
        return ((add_rows(key_grads, key_part), add_rows(value_grads, value_part)), query_grad)

    zero_grads = jnp.zeros((all_rows, local_heads, HEAD), jnp.float32)
    (key_grads, value_grads), query_grads = lax.scan(
        backward_block, (zero_grads, zero_grads), jnp.arange(block_total, dtype=jnp.int32)
    )
    grad_proj = jnp.stack(
        [
            query_grads.reshape(all_rows, local_width),
            key_grads.reshape(all_rows, local_width),
            value_grads.reshape(all_rows, local_width),
        ]
    ).astype(jnp.bfloat16)
    grad_qkv_weight = jnp.einsum(
        "td,cte->cde", normed_full, grad_proj, preferred_element_type=jnp.float32
    )
    grad_normed_one = lax.psum_scatter(
        jnp.einsum("cte,cde->td", grad_proj, w_qkv, preferred_element_type=jnp.float32).astype(
            jnp.bfloat16
        ),
        "mp",
        scatter_dimension=0,
        tiled=True,
    ).astype(jnp.float32)
    norm_one_back = jax.vjp(layer_norm, residual_in, gain_one, shift_one)[1]
    grad_input_part, grad_gain_one, grad_shift_one = norm_one_back(grad_normed_one)
    tokens_grad = grad_middle + grad_input_part
    grad_gain_one, grad_shift_one, grad_out_bias, grad_gain_two, grad_shift_two, grad_down_bias = (
        lax.psum(
            (
                grad_gain_one,
                grad_shift_one,
                jnp.sum(grad_middle, axis=0),
                grad_gain_two,
                grad_shift_two,
                jnp.sum(grad_output, axis=0),
            ),
            ("dp", "mp"),
        )
    )
    grad_qkv_weight, grad_out_weight, grad_up, grad_up_bias, grad_down = lax.psum(
        (grad_qkv_weight, grad_out_weight, grad_up, grad_up_bias, grad_down), "dp"
    )
    return (
        layer_out,
        tokens_grad,
        grad_gain_one,
        grad_shift_one,
        grad_qkv_weight,
        grad_out_weight,
        grad_out_bias,
        grad_gain_two,
        grad_shift_two,
        grad_up,
        grad_up_bias,
        grad_down,
        grad_down_bias,
    )


def solution(mesh):
    return jax.shard_map(
        shards,
        mesh=mesh,
        in_specs=(
            P(("dp", "mp"), None),
            P("dp"),
            P(),
            P(),
            P(None, None, "mp"),
            P("mp", None),
            P(),
            P(),
            P(),
            P(None, "mp"),
            P("mp"),
            P("mp", None),
            P(),
            P(("dp", "mp"), None),
        ),
        out_specs=(
            P(("dp", "mp"), None),
            P(("dp", "mp"), None),
            P(),
            P(),
            P(None, None, "mp"),
            P("mp", None),
            P(),
            P(),
            P(),
            P(None, "mp"),
            P("mp"),
            P("mp", None),
            P(),
        ),
        check_vma=False,
    )
```

profile of v0, /device:TPU:1, one launch (start us, length us, event | category | flops | bytes accessed | tf_op | source)
XLA Modules:
  0.0 1757.1 jit_solution(14801854086481193852)
XLA Ops:
  13.8 101.5 %all-gather.5.cloned.1.call-done = bf16[3456,768]{1,0:T(8,128)(2,1)} async-done(((bf16[864,768]{1,0:T(8,128)(2,1)}), bf16[3456,768]{1,0:T(8,128)(2,1)}) %all-gather.5.cloned.1.call-update) | async-done | bytes 5308432 | tf_op jit(solution)/shard_map/all_gather | solution.py:58
  123.0 247.2 %while.32 = (s32[]{:T(128)}, bf16[6,576,3,64]{1,3,2,0:T(8,128)(2,1)}, f32[6,3,576]{2,1,0:T(4,128)}, s32[6]{0:T(128)}, s32[3456]{0:T(1024)S(1)}, /*index=5*/bf16[...) while((s32[]{:T(128)}, ...), condition=%wide.region_5.6_spmd.clone, body=%wide.region_2.5_spmd.clone.sunk | while | flops 1608671232 | bytes 82862000 | solution.py:96
  384.2 93.2 %reduce-scatter.5.cloned.1.call-done = bf16[864,768]{1,0:T(8,128)(2,1)} async-done(((bf16[3456,768]{1,0:T(8,128)(2,1)}), bf16[864,768]{1,0:T(8,128)(2,1)}) %reduce-scatter.5.cloned.1.call-update) | async-done | bytes 1327120 | tf_op jit(solution)/shard_map/reduce_scatter | solution.py:98
  485.1 99.3 %all-gather.7.cloned.1.call-done = bf16[3456,768]{1,0:T(8,128)(2,1)} async-done(((bf16[864,768]{1,0:T(8,128)(2,1)}), bf16[3456,768]{1,0:T(8,128)(2,1)}) %all-gather.7.cloned.1.call-update) | async-done | bytes 5308432 | tf_op jit(solution)/shard_map/all_gather | solution.py:106
  592.4 91.0 %all-gather.9.cloned.1.call-done = bf16[3456,768]{1,0:T(8,128)(2,1)} async-done(((bf16[864,768]{1,0:T(8,128)(2,1)}), bf16[3456,768]{1,0:T(8,128)(2,1)}) %all-gather.9.cloned.1.call-update) | async-done | bytes 5308432 | tf_op jit(solution)/shard_map/all_gather | solution.py:117
  683.4 18.6 %convert_reduce_fusion = (f32[384]{0:T(512)}, bf16[3456,384]{1,0:T(8,128)(2,1)S(1)}, f32[3456,384]{1,0:T(8,128)}) fusion(f32[3456,384]{1,0:T(8,128)} %convolution_add_fusion, bf16[3456,768]{1,0:T(8,128)(2,1)} %all-gather.9.cloned.1.call-done, bf16[384,768]{1,0:T(8,128)(2,1)} %param.29), kind=kOutput, calls=%fused_computation.64 | convolution fusion | flops 2136637056 | bytes 19170816 | tf_op jit(solution)/shard_map/td,fd->tf/dot_general | solution.py:119
  719.4 82.1 %reduce-scatter.9.cloned.1.call-done = bf16[864,768]{1,0:T(8,128)(2,1)} async-done(((bf16[3456,768]{1,0:T(8,128)(2,1)}), bf16[864,768]{1,0:T(8,128)(2,1)}) %reduce-scatter.9.cloned.1.call-update) | async-done | bytes 1327120 | tf_op jit(solution)/shard_map/reduce_scatter | solution.py:123
  807.7 91.3 %reduce-scatter.7.cloned.1.call-done = bf16[864,768]{1,0:T(8,128)(2,1)} async-done(((bf16[3456,768]{1,0:T(8,128)(2,1)}), bf16[864,768]{1,0:T(8,128)(2,1)}) %reduce-scatter.7.cloned.1.call-update) | async-done | bytes 1327120 | tf_op jit(solution)/shard_map/reduce_scatter | solution.py:109
  906.7 99.8 %all-gather.11.cloned.1.call-done = bf16[3456,768]{1,0:T(8,128)(2,1)} async-done(((bf16[864,768]{1,0:T(8,128)(2,1)}), bf16[3456,768]{1,0:T(8,128)(2,1)}) %all-gather.11.cloned.1.call-update) | async-done | bytes 5308432 | tf_op jit(solution)/shard_map/all_gather | solution.py:135
  1012.6 527.3 %while.33 = (s32[]{:T(128)}, f32[3456,3,64]{0,2,1:T(8,128)}, f32[3456,3,64]{0,2,1:T(8,128)}, bf16[6,576,3,64]{1,3,2,0:T(8,128)(2,1)}, s32[6]{0:T(128)}, /*index=...) while((s32[]{:T(128)}, f32[3456,3,64]{0,2,1:T(8,128)}, ...), condition=%wide.region_15.16_spmd.clone, body=%wide.region_13.15_spmd.clone.sunk | while | flops 3923915264 | bytes 235123696 | solution.py:174
  1043.9 18.3 %multiply_reduce_fusion.3 = (f32[3,576]{1,0:T(4,128)S(1)}, f32[3,576,3456]{2,1,0:T(8,128)}) fusion(f32[3,576,3456]{2,1,0:T(8,128)} %fusion.150, f32[3,576]{1,0:T(4,128)S(1)} %dynamic-slice_bitcast_fusion.2, pred[576,3456]{1,0:T(8,128)(4,1)S(1)} %fusion.151, bf16[3456,3,64]{0,2,1:T(8,128)(2,1)} %get-tuple-element.636, ...), kind=kOutput, calls=%fused_computation.23.clone.1 | convolution fusion | flops 794712384 | bytes 51354244 | tf_op jit(solution)/shard_map/while/body/eval_jaxpr/qhd,khd->hqk/dot_general | solution.py:155
  1062.2 20.6 %multiply_convert_fusion.3 = bf16[3,576,3456]{2,1,0:T(8,128)(2,1)} fusion(f32[3,576,3456]{2,1,0:T(8,128)} %get-tuple-element.551, f32[3,576,3456]{2,1,0:T(8,128)} %fusion.150, f32[3,576]{1,0:T(4,128)S(1)} %get-tuple-element.552, f32[3,576]{1,0:T(4,128)S(1)} %dynamic-slice_bitcast_fusion.2, pred[576,3456]{1,0:T(8,128)(4,1)S(1)} %fusion.151), kind=kLoop, calls=%fused_computation.22.clone.1 | loop fusion | flops 35831808 | bytes 61724160 | tf_op jit(solution)/shard_map/while/body/eval_jaxpr/convert_element_type | solution.py:162
  1131.8 18.3 %multiply_reduce_fusion.3 = (f32[3,576]{1,0:T(4,128)S(1)}, f32[3,576,3456]{2,1,0:T(8,128)}) fusion(f32[3,576,3456]{2,1,0:T(8,128)} %fusion.150, f32[3,576]{1,0:T(4,128)S(1)} %dynamic-slice_bitcast_fusion.2, pred[576,3456]{1,0:T(8,128)(4,1)S(1)} %fusion.151, bf16[3456,3,64]{0,2,1:T(8,128)(2,1)} %get-tuple-element.636, ...), kind=kOutput, calls=%fused_computation.23.clone.1 | convolution fusion | flops 794712384 | bytes 51354244 | tf_op jit(solution)/shard_map/while/body/eval_jaxpr/qhd,khd->hqk/dot_general | solution.py:155
  1150.1 20.6 %multiply_convert_fusion.3 = bf16[3,576,3456]{2,1,0:T(8,128)(2,1)} fusion(f32[3,576,3456]{2,1,0:T(8,128)} %get-tuple-element.551, f32[3,576,3456]{2,1,0:T(8,128)} %fusion.150, f32[3,576]{1,0:T(4,128)S(1)} %get-tuple-element.552, f32[3,576]{1,0:T(4,128)S(1)} %dynamic-slice_bitcast_fusion.2, pred[576,3456]{1,0:T(8,128)(4,1)S(1)} %fusion.151), kind=kLoop, calls=%fused_computation.22.clone.1 | loop fusion | flops 35831808 | bytes 61724160 | tf_op jit(solution)/shard_map/while/body/eval_jaxpr/convert_element_type | solution.py:162
  1238.0 20.6 %multiply_convert_fusion.3 = bf16[3,576,3456]{2,1,0:T(8,128)(2,1)} fusion(f32[3,576,3456]{2,1,0:T(8,128)} %get-tuple-element.551, f32[3,576,3456]{2,1,0:T(8,128)} %fusion.150, f32[3,576]{1,0:T(4,128)S(1)} %get-tuple-element.552, f32[3,576]{1,0:T(4,128)S(1)} %dynamic-slice_bitcast_fusion.2, pred[576,3456]{1,0:T(8,128)(4,1)S(1)} %fusion.151), kind=kLoop, calls=%fused_computation.22.clone.1 | loop fusion | flops 35831808 | bytes 61724160 | tf_op jit(solution)/shard_map/while/body/eval_jaxpr/convert_element_type | solution.py:162
  1307.6 18.3 %multiply_reduce_fusion.3 = (f32[3,576]{1,0:T(4,128)S(1)}, f32[3,576,3456]{2,1,0:T(8,128)}) fusion(f32[3,576,3456]{2,1,0:T(8,128)} %fusion.150, f32[3,576]{1,0:T(4,128)S(1)} %dynamic-slice_bitcast_fusion.2, pred[576,3456]{1,0:T(8,128)(4,1)S(1)} %fusion.151, bf16[3456,3,64]{0,2,1:T(8,128)(2,1)} %get-tuple-element.636, ...), kind=kOutput, calls=%fused_computation.23.clone.1 | convolution fusion | flops 794712384 | bytes 51354244 | tf_op jit(solution)/shard_map/while/body/eval_jaxpr/qhd,khd->hqk/dot_general | solution.py:155
  1325.9 20.6 %multiply_convert_fusion.3 = bf16[3,576,3456]{2,1,0:T(8,128)(2,1)} fusion(f32[3,576,3456]{2,1,0:T(8,128)} %get-tuple-element.551, f32[3,576,3456]{2,1,0:T(8,128)} %fusion.150, f32[3,576]{1,0:T(4,128)S(1)} %get-tuple-element.552, f32[3,576]{1,0:T(4,128)S(1)} %dynamic-slice_bitcast_fusion.2, pred[576,3456]{1,0:T(8,128)(4,1)S(1)} %fusion.151), kind=kLoop, calls=%fused_computation.22.clone.1 | loop fusion | flops 35831808 | bytes 61724160 | tf_op jit(solution)/shard_map/while/body/eval_jaxpr/convert_element_type | solution.py:162
  1395.5 18.3 %multiply_reduce_fusion.3 = (f32[3,576]{1,0:T(4,128)S(1)}, f32[3,576,3456]{2,1,0:T(8,128)}) fusion(f32[3,576,3456]{2,1,0:T(8,128)} %fusion.150, f32[3,576]{1,0:T(4,128)S(1)} %dynamic-slice_bitcast_fusion.2, pred[576,3456]{1,0:T(8,128)(4,1)S(1)} %fusion.151, bf16[3456,3,64]{0,2,1:T(8,128)(2,1)} %get-tuple-element.636, ...), kind=kOutput, calls=%fused_computation.23.clone.1 | convolution fusion | flops 794712384 | bytes 51354244 | tf_op jit(solution)/shard_map/while/body/eval_jaxpr/qhd,khd->hqk/dot_general | solution.py:155
  1413.8 20.6 %multiply_convert_fusion.3 = bf16[3,576,3456]{2,1,0:T(8,128)(2,1)} fusion(f32[3,576,3456]{2,1,0:T(8,128)} %get-tuple-element.551, f32[3,576,3456]{2,1,0:T(8,128)} %fusion.150, f32[3,576]{1,0:T(4,128)S(1)} %get-tuple-element.552, f32[3,576]{1,0:T(4,128)S(1)} %dynamic-slice_bitcast_fusion.2, pred[576,3456]{1,0:T(8,128)(4,1)S(1)} %fusion.151), kind=kLoop, calls=%fused_computation.22.clone.1 | loop fusion | flops 35831808 | bytes 61724160 | tf_op jit(solution)/shard_map/while/body/eval_jaxpr/convert_element_type | solution.py:162
  1483.4 18.3 %multiply_reduce_fusion.3 = (f32[3,576]{1,0:T(4,128)S(1)}, f32[3,576,3456]{2,1,0:T(8,128)}) fusion(f32[3,576,3456]{2,1,0:T(8,128)} %fusion.150, f32[3,576]{1,0:T(4,128)S(1)} %dynamic-slice_bitcast_fusion.2, pred[576,3456]{1,0:T(8,128)(4,1)S(1)} %fusion.151, bf16[3456,3,64]{0,2,1:T(8,128)(2,1)} %get-tuple-element.636, ...), kind=kOutput, calls=%fused_computation.23.clone.1 | convolution fusion | flops 794712384 | bytes 51354244 | tf_op jit(solution)/shard_map/while/body/eval_jaxpr/qhd,khd->hqk/dot_general | solution.py:155
  1501.7 20.6 %multiply_convert_fusion.3 = bf16[3,576,3456]{2,1,0:T(8,128)(2,1)} fusion(f32[3,576,3456]{2,1,0:T(8,128)} %get-tuple-element.551, f32[3,576,3456]{2,1,0:T(8,128)} %fusion.150, f32[3,576]{1,0:T(4,128)S(1)} %get-tuple-element.552, f32[3,576]{1,0:T(4,128)S(1)} %dynamic-slice_bitcast_fusion.2, pred[576,3456]{1,0:T(8,128)(4,1)S(1)} %fusion.151), kind=kLoop, calls=%fused_computation.22.clone.1 | loop fusion | flops 35831808 | bytes 61724160 | tf_op jit(solution)/shard_map/while/body/eval_jaxpr/convert_element_type | solution.py:162
  1595.0 55.7 %reduce-scatter.11.cloned.1.call-done = bf16[864,768]{1,0:T(8,128)(2,1)} async-done(((bf16[3456,768]{1,0:T(8,128)(2,1)}), bf16[864,768]{1,0:T(8,128)(2,1)}) %reduce-scatter.11.cloned.1.call-update) | async-done | bytes 1327120 | tf_op jit(solution)/shard_map/reduce_scatter | solution.py:187
  1656.5 42.5 %all-reduce = (f32[768]{0:T(1024)}, f32[768]{0:T(1024)}, f32[768]{0:T(1024)}, f32[768]{0:T(1024)}, f32[768]{0:T(1024)}, /*index=5*/f32[768]{0:T(1024)}) all-reduce(f32[768]{0:T(1024)} %get-tuple-element.343, f32[768]{0:T(1024)} %get-tuple-element.347, f32[768]{0:T(1024)} %get-tuple-element.406, ...), channel_id=1, replica_groups=mesh['dp'=8,'mp'=4] {'dp','mp'}, use_global_device_ids=true, to_apply=%region_20.21 | all-reduce | flops 4608 | bytes 36864 | tf_op jit(solution)/shard_map/psum | solution.py:199
  1703.2 41.1 %all-reduce.4.cloned.1.call-done = (f32[3,768,192]{1,2,0:T(8,128)}, f32[192,768]{1,0:T(8,128)}, f32[768,384]{1,0:T(8,128)}, f32[384,768]{1,0:T(8,128)}) async-done(((f32[3,768,192]{1,2,0:T(8,128)}, f32[192,768]{1,0:T(8,128)}, f32[768,384]{1,0:T(8,128)}, f32[384,768]{1,0:T(8,128)}), (f32[3,768,192]{1,2,0:T(8,128)}, f32[192,768]{1,0:T(8,128)}, f32[768,384]{1,0:T(8,128)}, ...) | async-done | bytes 4718608 | tf_op jit(solution)/shard_map/psum | solution.py:211
  (321 shorter events, 690.3 us)
Async XLA Ops:
  7.2 108.1 %copy-start = (bf16[3,768,192]{1,2,0:T(8,128)(2,1)S(1)}, bf16[3,768,192]{1,2,0:T(8,128)(2,1)}, u32[]{:S(2)}) copy-start(bf16[3,768,192]{1,2,0:T(8,128)(2,1)} %param.22) | copy-start | bytes 2654212
  7.2 108.0 %all-gather.5.cloned.1.call-start = ((), (), s32[]{:S(2)}) async-start(), calls=%async_computation.4 | async-start | bytes 6635520 | tf_op jit(solution)/shard_map/all_gather | solution.py:58
  13.7 463.6 %reduce-scatter.5.cloned.1.call-start = ((), (), s32[]{:S(2)}) async-start(), calls=%async_computation.5 | async-start | bytes 6635520 | tf_op jit(solution)/shard_map/reduce_scatter | solution.py:98
  384.1 93.2 %copy-start.5 = (bf16[864,768]{1,0:T(8,128)(2,1)S(1)}, bf16[864,768]{1,0:T(8,128)(2,1)}, u32[]{:S(2)}) copy-start(bf16[864,768]{1,0:T(8,128)(2,1)} %param.18) | copy-start | bytes 3981316
  384.1 200.3 %all-gather.7.cloned.1.call-start = ((), (), s32[]{:S(2)}) async-start(), calls=%async_computation.6 | async-start | bytes 6635520 | tf_op jit(solution)/shard_map/all_gather | solution.py:106
  484.5 199.0 %all-gather.9.cloned.1.call-start = ((), (), s32[]{:S(2)}) async-start(), calls=%async_computation.8 | async-start | bytes 6635520 | tf_op jit(solution)/shard_map/all_gather | solution.py:117
  485.0 316.4 %reduce-scatter.9.cloned.1.call-start = ((), (), s32[]{:S(2)}) async-start(), calls=%async_computation.9 | async-start | bytes 6635520 | tf_op jit(solution)/shard_map/reduce_scatter | solution.py:123
  683.4 20.1 %copy-start.49 = (bf16[768,384]{1,0:T(8,128)(2,1)S(1)}, bf16[768,384]{1,0:T(8,128)(2,1)}, u32[]{:S(2)}) copy-start(bf16[768,384]{1,0:T(8,128)(2,1)} %param.27) | copy-start | bytes 1769476
  708.3 190.7 %reduce-scatter.7.cloned.1.call-start = ((), (), s32[]{:S(2)}) async-start(), calls=%async_computation.7 | async-start | bytes 6635520 | tf_op jit(solution)/shard_map/reduce_scatter | solution.py:109
  719.3 287.3 %all-gather.11.cloned.1.call-start = ((), (), s32[]{:S(2)}) async-start(), calls=%async_computation.10 | async-start | bytes 6635520 | tf_op jit(solution)/shard_map/all_gather | solution.py:135
  905.4 101.2 %copy-start.30 = (bf16[192,768]{1,0:T(8,128)(2,1)S(1)}, bf16[192,768]{1,0:T(8,128)(2,1)}, u32[]{:S(2)}) copy-start(bf16[192,768]{1,0:T(8,128)(2,1)} %param.23) | copy-start | bytes 884740
  906.7 744.1 %reduce-scatter.11.cloned.1.call-start = ((), (), s32[]{:S(2)}) async-start(), calls=%async_computation.11 | async-start | bytes 6635520 | tf_op jit(solution)/shard_map/reduce_scatter | solution.py:187
  1062.2 20.6 %copy-start.9 = (bf16[3456,3,64]{0,2,1:T(8,128)(2,1)S(1)}, bf16[3456,3,64]{0,2,1:T(8,128)(2,1)}, u32[]{:S(2)}) copy-start(bf16[3456,3,64]{0,2,1:T(8,128)(2,1)} %get-tuple-element.633) | copy-start | bytes 3981316 | tf_op jit(solution)/shard_map/while
  1150.1 20.6 %copy-start.9 = (bf16[3456,3,64]{0,2,1:T(8,128)(2,1)S(1)}, bf16[3456,3,64]{0,2,1:T(8,128)(2,1)}, u32[]{:S(2)}) copy-start(bf16[3456,3,64]{0,2,1:T(8,128)(2,1)} %get-tuple-element.633) | copy-start | bytes 3981316 | tf_op jit(solution)/shard_map/while
  1238.0 20.6 %copy-start.9 = (bf16[3456,3,64]{0,2,1:T(8,128)(2,1)S(1)}, bf16[3456,3,64]{0,2,1:T(8,128)(2,1)}, u32[]{:S(2)}) copy-start(bf16[3456,3,64]{0,2,1:T(8,128)(2,1)} %get-tuple-element.633) | copy-start | bytes 3981316 | tf_op jit(solution)/shard_map/while
  1325.9 20.6 %copy-start.9 = (bf16[3456,3,64]{0,2,1:T(8,128)(2,1)S(1)}, bf16[3456,3,64]{0,2,1:T(8,128)(2,1)}, u32[]{:S(2)}) copy-start(bf16[3456,3,64]{0,2,1:T(8,128)(2,1)} %get-tuple-element.633) | copy-start | bytes 3981316 | tf_op jit(solution)/shard_map/while
  1413.8 20.6 %copy-start.9 = (bf16[3456,3,64]{0,2,1:T(8,128)(2,1)S(1)}, bf16[3456,3,64]{0,2,1:T(8,128)(2,1)}, u32[]{:S(2)}) copy-start(bf16[3456,3,64]{0,2,1:T(8,128)(2,1)} %get-tuple-element.633) | copy-start | bytes 3981316 | tf_op jit(solution)/shard_map/while
  1501.7 20.6 %copy-start.9 = (bf16[3456,3,64]{0,2,1:T(8,128)(2,1)S(1)}, bf16[3456,3,64]{0,2,1:T(8,128)(2,1)}, u32[]{:S(2)}) copy-start(bf16[3456,3,64]{0,2,1:T(8,128)(2,1)} %get-tuple-element.633) | copy-start | bytes 3981316 | tf_op jit(solution)/shard_map/while
  1557.6 186.8 %all-reduce.4.cloned.1.call-start = ((), (), s32[]{:S(2)}) async-start(), calls=%async_computation.12 | async-start | bytes 9437184 | tf_op jit(solution)/shard_map/psum | solution.py:211
  1559.3 17.5 slice-start
  1581.5 69.3 %copy-start.6 = (bf16[864,768]{1,0:T(8,128)(2,1)S(1)}, bf16[864,768]{1,0:T(8,128)(2,1)}, u32[]{:S(2)}) copy-start(bf16[864,768]{1,0:T(8,128)(2,1)} %param.18) | copy-start | bytes 3981316
  1581.5 69.3 %copy-start.33 = (f32[864]{0:T(1024)S(1)}, f32[864]{0:T(1024)}, u32[]{:S(2)}) copy-start(f32[864]{0:T(1024)} %copy-done.32) | copy-start | bytes 10372
  1581.5 69.3 %copy-start.38 = (f32[768]{0:T(1024)S(1)}, f32[768]{0:T(1024)}, u32[]{:S(2)}) copy-start(f32[768]{0:T(1024)} %param.20) | copy-start | bytes 9220
  1581.5 73.0 %copy-start.40 = (f32[864]{0:T(1024)S(1)}, f32[864]{0:T(1024)}, u32[]{:S(2)}) copy-start(f32[864]{0:T(1024)} %copy-done.39) | copy-start | bytes 10372
  (58 other events, 232.5 us)
Sparse Core Ops, SparseCore 0:
  13.8 101.3 all-gather.4
  384.2 93.0 reduce-scatter.4
  484.6 99.7 all-gather.6
  585.9 97.4 all-gather.8
  708.4 93.0 reduce-scatter.8
  803.6 95.3 reduce-scatter.6
  906.8 99.7 all-gather.10
  1557.7 93.0 reduce-scatter.10
  1655.5 88.7 all-reduce.3
where the time goes:
time: 1770 us; the launch traced here: 1760 us
  waiting for transfers between devices  756 us (43%)
  matrix products  570 us (32%)
  other arithmetic  277 us (16%)
  local copies, waits for them, and re-layouts  63.8 us (4%)
  blocking collectives  55.4 us (3%)
  loops' own time  20.8 us (1%)
    dot_general x12, matrix products, block_view(): jnp.einsum('qhd,khd->hqk', query_blk, key_rows, preferred_element_type=jn...  129 us
    convert_element_type x6, other arithmetic, backward_block(): grad_scores = (attn_probs * (grad_probs - inner_sum)).astype(jnp.bfloat16)  124 us
    dot_general x6, matrix products, backward_block(): jnp.einsum('qhd,khd->hqk', grad_blk, value_seq, preferred_element_type=jn...  110 us
    all_gather x1, waiting for transfers between devices, shards(): normed_full = lax.all_gather(normed_one, 'mp', axis=0, tiled=True)  101 us
    all_gather x1, waiting for transfers between devices, shards(): middle_full = lax.all_gather(grad_middle_low, 'mp', axis=0, tiled=True)  99.8 us
    all_gather x1, waiting for transfers between devices, shards(): mlp_input = lax.all_gather(normed_two, 'mp', axis=0, tiled=True)  99.3 us
    reduce_scatter x1, waiting for transfers between devices, shards(): lax.psum_scatter(jnp.dot(attended, w_out, preferred_element_type=jnp.floa...  93.2 us
    reduce_scatter x1, waiting for transfers between devices, shards(): lax.psum_scatter(jnp.dot(active, w_down, preferred_element_type=jnp.float...  91.3 us
  transfers between devices with their start and end apart: 9, of which 9 were waited for; matrix products, arithmetic and copies ran while one was open for 3% of the time, Pallas kernels for 0%

commit v1 on v0

v1 whole, which is shorter than its diff:
```python
import functools

import jax
import jax.numpy as jnp
from jax import lax
from jax.experimental import pallas as pl
from jax.experimental.pallas import tpu as pltpu
from jax.sharding import PartitionSpec as P

HEAD = 64
D = 768
FF = 1536
LANES = 128
PAD = 384
EPS = 1e-05
MASKED = -1e30
MESH = pl.DeviceIdType.MESH
F32 = jnp.float32
BF16 = jnp.bfloat16
VMEM = pl.BlockSpec(memory_space=pltpu.VMEM)
SMEM = pl.BlockSpec(memory_space=pltpu.SMEM)
ANY = pl.BlockSpec(memory_space=pl.ANY)
DMA = pltpu.SemaphoreType.DMA

NN = (((1,), (0,)), ((), ()))
NT = (((1,), (1,)), ((), ()))
TN = (((0,), (0,)), ((), ()))


def dot(a, b, dims=NN):
    return lax.dot_general(a, b, dims, preferred_element_type=F32)


def limit(mib):
    return pltpu.CompilerParams(vmem_limit_bytes=mib << 20)


class Place:
    def __init__(self):
        self.d = lax.axis_index("dp")
        self.m = lax.axis_index("mp")
        self.c = lax.rem(self.d, 2)
        self.r = lax.rem(self.m, 2)
        self.hf = self.m // 2
        self.q = 2 * self.c + self.r
        self.native = self.c == self.hf
        self.sibling = (self.d + 1 - 2 * self.c, self.m)
        self.cross = (self.d, self.m + 1 - 2 * self.r)
        self.partner = (self.d + 1 - 2 * self.c, lax.rem(self.m + 2, 4))

    def member(self, quarter):
        return (self.d - self.c + quarter // 2, 2 * self.hf + quarter % 2)


def greet(others):
    barrier = pltpu.get_barrier_semaphore()
    for other in others:
        pl.semaphore_signal(barrier, inc=1, device_id=other, device_id_type=MESH)
    pl.semaphore_wait(barrier, len(others))


def remote(src, dst, send, recv, device):
    return pltpu.make_async_remote_copy(
        src_ref=src, dst_ref=dst, send_sem=send, recv_sem=recv, device_id=device, device_id_type=MESH
    )


PIECES = 3


def gather_kernel(
    tok, wq, full, wown, swap_s, swap_r, cross_s, cross_r, sib_s, sib_r, fwd_s, fwd_r, w_s, w_r, loc, wloc
):
    me = Place()
    rows = tok.shape[0]
    piece = rows // PIECES
    greet([me.sibling, me.cross, me.partner])

    def part(quarter, p):
        return full.at[pl.ds(pl.multiple_of(quarter * rows + p * piece, 16), piece)]

    def send_cross(src, p):
        return remote(src, part(me.q, p), cross_s.at[p], cross_r.at[p], me.cross)

    def send_sib(src, p):
        return remote(src, part(me.q, p), sib_s.at[p], sib_r.at[p], me.sibling)

    def tok_part(p):
        return tok.at[pl.ds(p * piece, piece)]

    partner_q = 2 * (1 - me.c) + me.r
    cross_q = 2 * me.c + 1 - me.r
    sib_cross_q = 2 * (1 - me.c) + 1 - me.r

    def swap(p):
        return remote(tok_part(p), part(partner_q, p), swap_s.at[p], swap_r.at[p], me.partner)

    def swap_in(p):
        return remote(tok_part(p), part(me.q, p), swap_s.at[p], swap_r.at[p], me.partner)

    weight = remote(wq, wown, w_s, w_r, me.partner)
    own_rows = full.at[pl.ds(pl.multiple_of(me.q * rows, 16), rows)]

    @pl.when(me.native)
    def _():
        for p in range(PIECES):
            send_cross(tok_part(p), p).start()
            send_sib(tok_part(p), p).start()
        pltpu.make_async_copy(tok, own_rows, loc).start()
        pltpu.make_async_copy(wq, wown, wloc).start()

    @pl.when(jnp.logical_not(me.native))
    def _():
        for p in range(PIECES):
            swap(p).start()
        weight.start()
        for p in range(PIECES):
            swap_in(p).wait_recv()
            send_cross(part(me.q, p), p).start()
            send_sib(part(me.q, p), p).start()

    for p in range(PIECES):
        remote(part(cross_q, p), part(cross_q, p), cross_s.at[p], cross_r.at[p], me.cross).wait_recv()
        remote(part(cross_q, p), part(cross_q, p), fwd_s.at[p], fwd_r.at[p], me.sibling).start()
    for p in range(PIECES):
        remote(part(partner_q, p), part(partner_q, p), sib_s.at[p], sib_r.at[p], me.sibling).wait_recv()
        remote(part(sib_cross_q, p), part(sib_cross_q, p), fwd_s.at[p], fwd_r.at[p], me.sibling).wait_recv()
        remote(part(cross_q, p), part(cross_q, p), fwd_s.at[p], fwd_r.at[p], me.sibling).wait_send()

    @pl.when(me.native)
    def _():
        for p in range(PIECES):
            send_cross(tok_part(p), p).wait_send()
            send_sib(tok_part(p), p).wait_send()
        pltpu.make_async_copy(tok, own_rows, loc).wait()
        pltpu.make_async_copy(wq, wown, wloc).wait()

    @pl.when(jnp.logical_not(me.native))
    def _():
        for p in range(PIECES):
            swap(p).wait_send()
            send_cross(part(me.q, p), p).wait_send()
            send_sib(part(me.q, p), p).wait_send()
        weight.wait_send()
        weight.wait_recv()


def gather_sequence(tokens, w_qkv):
    rows = tokens.shape[0]
    sems = [DMA((PIECES,))] * 8 + [DMA] * 4
    return pl.pallas_call(
        gather_kernel,
        name="gather_sequence",
        in_specs=[ANY, ANY],
        out_specs=[ANY, ANY],
        out_shape=[jax.ShapeDtypeStruct((4 * rows, D), BF16), jax.ShapeDtypeStruct(w_qkv.shape, BF16)],
        scratch_shapes=sems,
        compiler_params=pltpu.CompilerParams(collective_id=1, has_side_effects=True),
    )(tokens, w_qkv)


def exchange_kernel(to_rows, src, dst, send, recv, loc):
    me = Place()
    others = []
    for k in range(1, 4):
        quarter = lax.rem(me.q + k, 4)
        others.append(me.member(quarter))
    greet(others)
    rows = (dst.shape[0] if to_rows else src.shape[0]) // 4

    def block(ref, quarter, by_rows):
        if by_rows:
            return ref.at[pl.ds(pl.multiple_of(quarter * rows, 16), rows)]
        return ref.at[quarter]

    def copy(k):
        quarter = lax.rem(me.q + k, 4)
        return remote(
            block(src, quarter, not to_rows), block(dst, me.q, to_rows), send.at[k], recv.at[k], others[k - 1]
        )

    def arrival(k):
        quarter = lax.rem(me.q + 4 - k, 4)
        return remote(
            block(src, quarter, not to_rows), block(dst, quarter, to_rows), send.at[k], recv.at[k], others[3 - k]
        )

    for k in (2, 1, 3):
        copy(k).start()
    own = pltpu.make_async_copy(block(src, me.q, not to_rows), block(dst, me.q, to_rows), loc)
    own.start()
    for k in (1, 2, 3):
        arrival(k).wait_recv()
    for k in (1, 2, 3):
        copy(k).wait_send()
    own.wait()


def exchange(values, to_rows, number):
    if to_rows:
        _, rows, width = values.shape
        shape = (4 * rows, width)
    else:
        rows, width = values.shape
        shape = (4, rows // 4, width)
    return pl.pallas_call(
        functools.partial(exchange_kernel, to_rows),
        name="exchange_rows" if to_rows else "exchange_heads",
        in_specs=[ANY],
        out_specs=ANY,
        out_shape=jax.ShapeDtypeStruct(shape, values.dtype),
        scratch_shapes=[DMA((4,)), DMA((4,)), DMA],
        compiler_params=pltpu.CompilerParams(collective_id=number, has_side_effects=True),
    )(values)


ROWS_QKV = 384


def normalise(x):
    centred = x - jnp.mean(x, axis=-1, keepdims=True)
    scale = lax.rsqrt(jnp.mean(centred * centred, axis=-1, keepdims=True) + EPS)
    return centred * scale, scale


def widen(x, ones, rows):
    lane = lax.broadcasted_iota(jnp.int32, (rows, LANES - HEAD), 1)
    return jnp.concatenate([x, jnp.where(lane < ones, 1.0, 0.0).astype(x.dtype)], axis=1)


def qkv_kernel(heads, steps, x, gain, shift, w, wt, normed, q, k, v, kt, vt):
    rows = x.shape[0]

    @pl.when(pl.program_id(0) < steps)
    def _():
        unit, _ = normalise(x[...].astype(F32))
        low = (unit * gain[...] + shift[...]).astype(BF16)
        normed[...] = low
        qs = (dot(low, w[0]).astype(BF16).astype(F32) * HEAD**-0.5).astype(BF16)
        ks = dot(low, w[1]).astype(BF16)
        vs = dot(low, w[2]).astype(BF16)
        kts = dot(wt[0], low, NT).astype(BF16)
        vts = dot(wt[1], low, NT).astype(BF16)
        line = lax.broadcasted_iota(jnp.int32, (16, rows), 0)
        ones = jnp.where(line < 1, 1.0, 0.0).astype(BF16)
        for h in range(heads):
            cols = slice(h * HEAD, (h + 1) * HEAD)
            q[h] = widen(qs[:, cols], 0, rows)
            k[h] = widen(ks[:, cols], 3, rows)
            v[h] = widen(vs[:, cols], 3, rows)
            kt[h] = kts[cols]
            vt[h, :HEAD] = vts[cols]
            vt[h, HEAD:] = ones

    @pl.when(pl.program_id(0) >= steps)
    def _():
        for out in (q, k, v, kt, vt):
            out[...] = jnp.zeros_like(out)


def project(full, gain, shift, w):
    total = full.shape[0]
    heads = w.shape[2] // HEAD
    steps = total // ROWS_QKV
    wide = total + PAD
    wt = jnp.swapaxes(w[1:], 1, 2)
    whole = lambda shape: pl.BlockSpec(shape, lambda i: (0,) * len(shape))
    by_rows = pl.BlockSpec((heads, ROWS_QKV, LANES), lambda i: (0, i, 0))
    by_cols = lambda n: pl.BlockSpec((heads, n, ROWS_QKV), lambda i: (0, 0, i))
    clamp = pl.BlockSpec((ROWS_QKV, D), lambda i: (jnp.minimum(i, steps - 1), 0))
    rowed = jax.ShapeDtypeStruct((heads, wide, LANES), BF16)
    return pl.pallas_call(
        functools.partial(qkv_kernel, heads, steps),
        name="norm_and_project",
        grid=(steps + PAD // ROWS_QKV,),
        in_specs=[clamp, whole((1, D)), whole((1, D)), whole(w.shape), whole(wt.shape)],
        out_specs=[clamp, by_rows, by_rows, by_rows, by_cols(HEAD), by_cols(HEAD + 16)],
        out_shape=[
            jax.ShapeDtypeStruct((total, D), BF16),
            rowed,
            rowed,
            rowed,
            jax.ShapeDtypeStruct((heads, HEAD, wide), BF16),
            jax.ShapeDtypeStruct((heads, HEAD + 16, wide), BF16),
        ],
        compiler_params=limit(48),
    )(full, gain, shift, w, wt)


FWD_Q, FWD_K = 384, 512
BWD_Q, BWD_K = 384, 384


def attention_kernel(heads, total, lo, hi, idc, idr, q, k, vt, out, lse):
    step = FWD_K // LANES

    def one_block(i, _):
        r0 = pl.multiple_of(i * FWD_Q, LANES)
        qs = [q[h, pl.ds(r0, FWD_Q), :] for h in range(heads)]
        mine = idr[:, pl.ds(r0, FWD_Q)]

        def keys(at, carry):
            c0 = pl.multiple_of(at * LANES, LANES)
            allowed = idc[pl.ds(c0, FWD_K), :] == mine
            new = []
            for h in range(heads):
                top, acc = carry[h]
                s = jnp.where(allowed, dot(k[h, pl.ds(c0, FWD_K), :], qs[h], NT), MASKED)
                above = jnp.maximum(top, jnp.max(s, axis=0, keepdims=True))
                p = jnp.exp(s - above).astype(BF16)
                acc = acc * jnp.exp(top - above) + dot(vt[h, :, pl.ds(c0, FWD_K)], p)
                new.append((above, acc))
            return tuple(new)

        start = tuple(
            (jnp.full((1, FWD_Q), MASKED, F32), jnp.zeros((vt.shape[1], FWD_Q), F32)) for _ in range(heads)
        )
        first = lo[i]
        count = (hi[i] - first + step - 1) // step
        done = lax.fori_loop(0, count, lambda n, c: keys(first + n * step, c), start)
        valid = jnp.where(mine >= 0, 1.0, 0.0)
        mixed = []
        for h in range(heads):
            top, acc = done[h]
            row_total = acc[HEAD : HEAD + 1]
            mixed.append(acc[:HEAD] * (valid / row_total))
            lse[pl.ds(h, 1), pl.ds(r0, FWD_Q)] = top + jnp.log(row_total)
        out[pl.ds(r0, FWD_Q), :] = jnp.concatenate(mixed, axis=0).T.astype(BF16)
        return 0

    lax.fori_loop(0, total // FWD_Q, one_block, 0)


def attention(ids, q, k, vt):
    lo, hi, idc, idr = ids
    heads, wide, _ = q.shape
    total = wide - PAD
    return pl.pallas_call(
        functools.partial(attention_kernel, heads, total),
        name="attention",
        in_specs=[SMEM, SMEM] + [VMEM] * 5,
        out_specs=[VMEM, VMEM],
        out_shape=[
            jax.ShapeDtypeStruct((total, heads * HEAD), BF16),
            jax.ShapeDtypeStruct((heads, total), F32),
        ],
        compiler_params=limit(56),
    )(lo, hi, idc, idr, q, k, vt)


def thirds(x):
    a = x.astype(BF16).astype(F32)
    b = (x - a).astype(BF16).astype(F32)
    return a, b, x - a - b


def attention_back_kernel(
    heads, total, lo, hi, idc, idr, q, k, v, kt, out, grad, lse, dproj, qe, ge, dq
):
    wide = q.shape[1]
    step = BWD_Q // LANES
    lane = lax.broadcasted_iota(jnp.int32, (PAD, LANES), 1)

    def extend(values, tail):
        a, b, c = thirds(tail)
        return jnp.where(
            lane == HEAD, a, jnp.where(lane == HEAD + 1, b, jnp.where(lane == HEAD + 2, c, values))
        ).astype(BF16)

    def prepare(i, _):
        rows = pl.ds(pl.multiple_of(i * PAD, LANES), PAD)
        valid = jnp.where(idc[rows, :] >= 0, 1.0, 0.0)
        grads = grad[rows, :].astype(F32) * valid
        inner = grads * out[rows, :].astype(F32)
        for h in range(heads):
            cols = slice(h * HEAD, (h + 1) * HEAD)
            g = jnp.concatenate([grads[:, cols], jnp.zeros((PAD, LANES - HEAD), F32)], axis=1)
            ge[h, rows, :] = extend(g, -jnp.sum(inner[:, cols], axis=1, keepdims=True))
            qe[h, rows, :] = extend(q[h, rows, :].astype(F32), -lse[rows, h : h + 1])
            dq[h, :, rows] = jnp.zeros((HEAD, PAD), F32)
        return 0

    lax.fori_loop(0, total // PAD, prepare, 0)
    for h in range(heads):
        qe[h, total:, :] = jnp.zeros((wide - total, LANES), BF16)
        ge[h, total:, :] = jnp.zeros((wide - total, LANES), BF16)
        dq[h, :, total:] = jnp.zeros((HEAD, wide - total), F32)

    def one_block(i, _):
        c0 = pl.multiple_of(i * BWD_K, LANES)
        cols = pl.ds(c0, BWD_K)
        mine = idc[cols, :]

        def queries(at, carry):
            r0 = pl.multiple_of(at * LANES, LANES)
            rows = pl.ds(r0, BWD_Q)
            allowed = mine == idr[:, rows]
            new = []
            for h in range(heads):
                dk, dv = carry[h]
                qh = qe[h, rows, :]
                gh = ge[h, rows, :]
                p = jnp.where(allowed, jnp.exp(dot(k[h, cols, :], qh, NT)), 0.0)
                ds = (p * dot(v[h, cols, :], gh, NT)).astype(BF16)
                dv = dv + dot(p.astype(BF16), gh)
                dk = dk + dot(ds, qh)
                dq[h, :, rows] += dot(kt[h, :, cols], ds)
                new.append((dk, dv))
            return tuple(new)

        zero = jnp.zeros((BWD_K, LANES), F32)
        first = lo[i]
        count = (hi[i] - first + step - 1) // step
        done = lax.fori_loop(
            0, count, lambda n, c: queries(first + n * step, c), tuple((zero, zero) for _ in range(heads))
        )
        for part in range(2):
            joined = jnp.concatenate([done[h][part][:, :HEAD] for h in range(heads)], axis=1)
            dproj[part + 1, cols, :] = joined.astype(BF16)
        return 0

    lax.fori_loop(0, total // BWD_K, one_block, 0)

    def finish(i, _):
        rows = pl.ds(pl.multiple_of(i * PAD, LANES), PAD)
        joined = jnp.concatenate([dq[h, :, rows] for h in range(heads)], axis=0)
        dproj[0, rows, :] = (joined * HEAD**-0.5).T.astype(BF16)
        return 0

    lax.fori_loop(0, total // PAD, finish, 0)


def attention_back(ids, q, k, v, kt, out, grad, lse):
    lo, hi, idc, idr = ids
    heads, wide, _ = q.shape
    total = wide - PAD
    return pl.pallas_call(
        functools.partial(attention_back_kernel, heads, total),
        name="attention_back",
        in_specs=[SMEM, SMEM] + [VMEM] * 9,
        out_specs=VMEM,
        out_shape=jax.ShapeDtypeStruct((3, total, heads * HEAD), BF16),
        scratch_shapes=[
            pltpu.VMEM((heads, wide, LANES), BF16),
            pltpu.VMEM((heads, wide, LANES), BF16),
            pltpu.VMEM((heads, HEAD, wide), F32),
        ],
        compiler_params=limit(60),
    )(lo, hi, idc, idr, q, k, v, kt, out, grad, lse.T)


def scene_ranges(scene, block):
    total = scene.shape[0]
    place = jnp.arange(total, dtype=jnp.int32)
    ids = jnp.where(scene >= 0, scene, -1 - place)
    before = jnp.sum(
        ((scene[None, :] >= 0) & (scene[None, :] < jnp.arange(6, dtype=jnp.int32)[:, None])).astype(jnp.int32), axis=1
    )
    first, last = scene[0::block], scene[block - 1 :: block]
    start = jnp.arange(total // block, dtype=jnp.int32) * block
    pick = lambda number: jnp.sum(
        jnp.where(number[:, None] == jnp.arange(6, dtype=jnp.int32)[None, :], before[None, :], 0), axis=1
    )
    lo = jnp.where(first >= 0, pick(first), start) // LANES
    hi = (jnp.where(last >= 0, pick(last + 1), start + block) + LANES - 1) // LANES
    padded = jnp.pad(ids, (0, PAD), constant_values=-(1 << 20))
    return lo, hi, padded[:, None], padded[None, :]


ROWS_MID = 288


def middle_kernel(
    att, tok, cot, w_out, b_out, gain, shift, w_up, b_up, w_down, b_down,
    layer_out, grad_mid, grad_att, d_out, d_up, d_down, d_vec, d_bup, a_out, a_up, a_down, a_vec, a_bup,
):
    step = pl.program_id(0)
    parts = w_up.shape[0]
    width = att.shape[2]

    @pl.when(step == 0)
    def _():
        for ref in (a_out, a_up, a_down, a_vec, a_bup):
            ref[...] = jnp.zeros_like(ref)

    atts = [att[v] for v in range(parts)]
    middle = tok[...].astype(F32) + b_out[...]
    for v in range(parts):
        middle = middle + dot(atts[v], w_out[v * width : (v + 1) * width, :])
    unit, scale = normalise(middle)
    low = (unit * gain[...] + shift[...]).astype(BF16)
    cot_low = cot[...]
    cot_full = cot_low.astype(F32)
    out = middle + b_down[...]
    grad_norm = jnp.zeros_like(middle)
    for v in range(parts):
        hidden = dot(low, w_up[v]) + b_up[v]
        below = 0.5 * (1.0 + lax.erf(hidden * 0.5**0.5))
        density = jnp.exp(-0.5 * hidden * hidden) * 0.3989422804014327
        active = (hidden * below).astype(BF16)
        out = out + dot(active, w_down[v])
        grad_hidden = (dot(cot_low, w_down[v], NT) * (below + hidden * density)).astype(BF16)
        grad_norm = grad_norm + dot(grad_hidden, w_up[v], NT)
        a_down[v] += dot(active, cot_low, TN)
        a_up[v] += dot(low, grad_hidden, TN)
        a_bup[v] += jnp.sum(grad_hidden.astype(F32), axis=0, keepdims=True)
    layer_out[...] = out.astype(BF16)
    scaled = grad_norm * gain[...]
    back = cot_full + scale * (
        scaled
        - jnp.mean(scaled, axis=-1, keepdims=True)
        - unit * jnp.mean(scaled * unit, axis=-1, keepdims=True)
    )
    grad_mid[...] = back
    back_low = back.astype(BF16)
    for v in range(parts):
        rows = slice(v * width, (v + 1) * width)
        a_out[rows, :] += dot(atts[v], back_low, TN)
        grad_att[v] = dot(back_low, w_out[rows, :], NT).astype(BF16)
    a_vec[0:1] += jnp.sum(grad_norm * unit, axis=0, keepdims=True)
    a_vec[1:2] += jnp.sum(grad_norm, axis=0, keepdims=True)
    a_vec[2:3] += jnp.sum(back, axis=0, keepdims=True)
    a_vec[3:4] += jnp.sum(cot_full, axis=0, keepdims=True)

    @pl.when(step == pl.num_programs(0) - 1)
    def _():
        for ref, total in ((d_out, a_out), (d_up, a_up), (d_down, a_down), (d_vec, a_vec), (d_bup, a_bup)):
            ref[...] = total[...].astype(ref.dtype)


def middle_part(att, tok, cot, w_out, b_out, gain, shift, w_up, b_up, w_down, b_down):
    parts, rows, width = att.shape
    whole = lambda a: pl.BlockSpec(a.shape, lambda i: (0,) * len(a.shape))
    shape = lambda s, t: jax.ShapeDtypeStruct(s, t)
    tile = pl.BlockSpec((ROWS_MID, D), lambda i: (i, 0))
    heads_tile = pl.BlockSpec((parts, ROWS_MID, width), lambda i: (0, i, 0))
    sums = [w_out.shape, w_up.shape, w_down.shape, (8, D), b_up.shape]
    kinds = [BF16, BF16, BF16, F32, F32]
    totals = [shape(s, t) for s, t in zip(sums, kinds)]
    return pl.pallas_call(
        middle_kernel,
        name="middle_part",
        grid=(rows // ROWS_MID,),
        in_specs=[heads_tile, tile, tile] + [whole(a) for a in (w_out, b_out, gain, shift, w_up, b_up, w_down, b_down)],
        out_specs=[tile, tile, heads_tile] + [whole(t) for t in totals],
        out_shape=[shape((rows, D), BF16), shape((rows, D), F32), shape((parts, rows, width), BF16)] + totals,
        scratch_shapes=[pltpu.VMEM(s, F32) for s in sums],
        compiler_params=limit(60),
    )(att, tok, cot, w_out, b_out, gain, shift, w_up, b_up, w_down, b_down)


ROWS_FIN = 384


def project_back_kernel(tok, gain, normed, dproj, w, partial, d_w, d_vec, a_w, a_vec):
    step = pl.program_id(0)

    @pl.when(step == 0)
    def _():
        a_w[...] = jnp.zeros_like(a_w)
        a_vec[...] = jnp.zeros_like(a_vec)

    low = normed[...]
    grad = jnp.zeros(tok.shape, F32)
    for c in range(3):
        grad = grad + dot(dproj[c], w[c], NT)
        a_w[c] += dot(low, dproj[c], TN)
    partial[...] = grad.astype(BF16)
    unit, _ = normalise(tok[...].astype(F32))
    a_vec[0:1] += jnp.sum(grad * unit, axis=0, keepdims=True)
    a_vec[1:2] += jnp.sum(grad, axis=0, keepdims=True)

    @pl.when(step == pl.num_programs(0) - 1)
    def _():
        d_w[...] = a_w[...].astype(BF16)
        d_vec[...] = a_vec[...]


def project_back(full, gain, normed, dproj, w):
    total = full.shape[0]
    width = w.shape[2]
    whole = lambda s: pl.BlockSpec(s, lambda i: (0,) * len(s))
    tile = pl.BlockSpec((ROWS_FIN, D), lambda i: (i, 0))
    return pl.pallas_call(
        project_back_kernel,
        name="project_back",
        grid=(total // ROWS_FIN,),
        in_specs=[tile, whole((1, D)), tile, pl.BlockSpec((3, ROWS_FIN, width), lambda i: (0, i, 0)), whole(w.shape)],
        out_specs=[tile, whole(w.shape), whole((8, D))],
        out_shape=[
            jax.ShapeDtypeStruct((total, D), BF16),
            jax.ShapeDtypeStruct(w.shape, BF16),
            jax.ShapeDtypeStruct((8, D), F32),
        ],
        scratch_shapes=[pltpu.VMEM(w.shape, F32), pltpu.VMEM((8, D), F32)],
        compiler_params=limit(48),
    )(full, gain, normed, dproj, w)


def return_kernel(
    partial, own_tok, grad_mid, gain, vec, grad, vec_sum,
    mine, theirs, sent, crossed, tok, mid, low, back, vz, vzsum, vd,
    load_s, sib_s, sib_r, cross_s, cross_r, swap_s, swap_r, vz_s, vz_r, vd_s, vd_r,
):
    me = Place()
    rows = own_tok.shape[0]
    piece = rows // PIECES
    ndp = vd.shape[0]
    around = [(me.d, lax.rem(me.m + k, 4)) for k in range(1, 4)]
    along = [(lax.rem(me.d + k, ndp), me.m) for k in range(1, ndp)]
    greet([me.sibling, me.cross, me.partner] + around + along)
    other = 1 - me.c

    def rows_of(quarter, p):
        return pl.ds(pl.multiple_of(quarter * rows + p * piece, 16), piece)

    quarters = [2 * me.c + 1 - me.r, me.q]
    for_sib = [2 * other + 1 - me.r, 2 * other + me.r]

    def to_sib(slot, p):
        return remote(
            partial.at[rows_of(for_sib[slot], p)],
            theirs.at[slot, p],
            sib_s.at[slot, p],
            sib_r.at[slot, p],
            me.sibling,
        )

    def load(slot, p):
        return pltpu.make_async_copy(partial.at[rows_of(quarters[slot], p)], mine.at[slot, p], load_s.at[slot, p])

    def to_cross(p):
        return remote(sent.at[p], crossed.at[p], cross_s.at[p], cross_r.at[p], me.cross)

    def to_partner(p):
        return remote(low.at[p], back.at[p], swap_s.at[p], swap_r.at[p], me.partner)

    for slot in range(2):
        for p in range(PIECES):
            to_sib(slot, p).start()
            load(slot, p).start()
    load_tok = pltpu.make_async_copy(own_tok, tok, load_s.at[2, 0])
    load_mid = pltpu.make_async_copy(grad_mid, mid, load_s.at[2, 1])
    load_tok.start()
    load_mid.start()

    vz[me.m] = vec[...]

    def around_copy(k):
        return remote(vz.at[me.m], vz.at[me.m], vz_s.at[k], vz_r.at[k], around[k])

    for k in range(3):
        around_copy(k).start()

    for p in range(PIECES):
        load(0, p).wait()
        to_sib(0, p).wait_recv()
        sent[p] = (mine[0, p].astype(F32) + theirs[0, p].astype(F32)).astype(BF16)
        to_cross(p).start()

    for k in range(3):
        source = lax.rem(me.m + 3 - k, 4)
        remote(vz.at[source], vz.at[source], vz_s.at[k], vz_r.at[k], around[k]).wait_recv()
    vd[me.d] = vz[0] + vz[1] + vz[2] + vz[3]

    def along_copy(k):
        return remote(vd.at[me.d], vd.at[me.d], vd_s.at[k], vd_r.at[k], along[k])

    for k in range(ndp - 1):
        along_copy(k).start()

    load_tok.wait()
    load_mid.wait()
    for p in range(PIECES):
        span = pl.ds(p * piece, piece)
        load(1, p).wait()
        to_sib(1, p).wait_recv()
        to_cross(p).wait_recv()
        total = mine[1, p].astype(F32) + theirs[1, p].astype(F32) + crossed[p].astype(F32)
        unit, scale = normalise(tok[span, :].astype(F32))
        scaled = total * gain[...]
        result = mid[span, :] + scale * (
            scaled
            - jnp.mean(scaled, axis=-1, keepdims=True)
            - unit * jnp.mean(scaled * unit, axis=-1, keepdims=True)
        )

        @pl.when(me.native)
        def _():
            grad[span, :] = result

        @pl.when(jnp.logical_not(me.native))
        def _():
            low[p] = result.astype(BF16)
            to_partner(p).start()

    for k in range(ndp - 1):
        source = lax.rem(me.d + ndp - 1 - k, ndp)
        remote(vd.at[source], vd.at[source], vd_s.at[k], vd_r.at[k], along[k]).wait_recv()
    total = vd[0]
    for i in range(1, ndp):
        total = total + vd[i]
    vec_sum[...] = total

    @pl.when(jnp.logical_not(me.native))
    def _():
        for p in range(PIECES):
            to_partner(p).wait_recv()
            grad[pl.ds(p * piece, piece), :] = back[p].astype(F32)
        for p in range(PIECES):
            to_partner(p).wait_send()

    for slot in range(2):
        for p in range(PIECES):
            to_sib(slot, p).wait_send()
    for p in range(PIECES):
        to_cross(p).wait_send()
    for k in range(3):
        around_copy(k).wait_send()
    for k in range(ndp - 1):
        along_copy(k).wait_send()


def return_home(partial, own_tok, grad_mid, gain, vec, ndp):
    rows = own_tok.shape[0]
    piece = rows // PIECES
    pieces = (PIECES, piece, D)
    return pl.pallas_call(
        return_kernel,
        name="return_home",
        in_specs=[ANY, ANY, ANY, VMEM, VMEM],
        out_specs=[VMEM, VMEM],
        out_shape=[jax.ShapeDtypeStruct((rows, D), F32), jax.ShapeDtypeStruct((8, D), F32)],
        scratch_shapes=[
            pltpu.VMEM((2,) + pieces, BF16),
            pltpu.VMEM((2,) + pieces, BF16),
            pltpu.VMEM(pieces, BF16),
            pltpu.VMEM(pieces, BF16),
            pltpu.VMEM((rows, D), BF16),
            pltpu.VMEM((rows, D), F32),
            pltpu.VMEM(pieces, BF16),
            pltpu.VMEM(pieces, BF16),
            pltpu.VMEM((4, 8, D), F32),
            pltpu.VMEM((8, D), F32),
            pltpu.VMEM((ndp, 8, D), F32),
            DMA((3, PIECES)),
            DMA((2, PIECES)),
            DMA((2, PIECES)),
            DMA((PIECES,)),
            DMA((PIECES,)),
            DMA((PIECES,)),
            DMA((PIECES,)),
            DMA((3,)),
            DMA((3,)),
            DMA((ndp - 1,)),
            DMA((ndp - 1,)),
        ],
        compiler_params=pltpu.CompilerParams(
            collective_id=4, has_side_effects=True, vmem_limit_bytes=48 << 20
        ),
    )(partial, own_tok, grad_mid, gain, vec)


def swap_pairs(ndp):
    pairs = []
    for d in range(ndp):
        for m in range(4):
            native = d % 2 == m // 2
            to = (d, m) if native else (d ^ 1, (m + 2) % 4)
            pairs.append((d * 4 + m, to[0] * 4 + to[1]))
    return pairs


def gather_weights(w_out, w_up, w_down, ndp):
    d = lax.axis_index("dp")
    cut = lambda w: lax.dynamic_slice_in_dim(w, d * (w.shape[0] // ndp), w.shape[0] // ndp, 0)
    a, b, c = cut(w_out), cut(w_up), cut(w_down)
    half = b.shape[0] // 2
    mine = jnp.concatenate([a, jnp.concatenate([b[:half], b[half:]], axis=1), c], axis=0)
    parts = lax.all_gather(mine, ("dp", "mp"), axis=0).reshape(ndp, 4, *mine.shape)
    na, nb = a.shape[0], half
    out = parts[:, :, :na].transpose(1, 0, 2, 3).reshape(D, D)
    up = parts[:, :, na : na + nb].transpose(1, 0, 2, 3)
    up = jnp.stack([up[..., : FF // 4], up[..., FF // 4 :]], axis=2).reshape(4, D, FF // 4)
    down = parts[:, :, na + nb :].transpose(1, 0, 2, 3).reshape(4, FF // 4, D)
    return out, up, down


def reduce_weights(d_out, d_up, d_down, vec, bup, ndp):
    out = d_out.reshape(4, ndp, -1, D).transpose(1, 0, 2, 3)
    up = d_up.reshape(4, ndp, 2, -1, FF // 4)
    up = jnp.concatenate([up[:, :, 0], up[:, :, 1]], axis=-1).transpose(1, 0, 2, 3)
    down = d_down.reshape(4, ndp, -1, D).transpose(1, 0, 2, 3)
    flat = jnp.broadcast_to(vec.reshape(ndp, 1, -1), (ndp, 4, vec.size // ndp))
    flat_up = bup.reshape(4, ndp, -1).transpose(1, 0, 2)
    used = flat.shape[2] + flat_up.shape[2]
    tail = jnp.concatenate([flat, flat_up, jnp.zeros((ndp, 4, D - used), F32)], axis=2)[:, :, None].astype(BF16)
    cells = jnp.concatenate([out, up, down, tail], axis=2)
    n_out, n_up, n_down = out.shape[2], up.shape[2], down.shape[2]
    height = cells.shape[2]
    cells = lax.psum_scatter(cells.reshape(-1, D), "dp", scatter_dimension=0, tiled=True)
    cells = lax.psum_scatter(cells, "mp", scatter_dimension=0, tiled=True)
    cells = cells.reshape(height, D)
    cells = lax.all_gather(cells, "dp", axis=0).astype(F32)
    out = cells[:, :n_out].reshape(-1, D)
    up = cells[:, n_out : n_out + n_up]
    up = jnp.stack([up[..., : FF // 4], up[..., FF // 4 :]], axis=1).reshape(D, FF // 4)
    down = cells[:, n_out + n_up : n_out + n_up + n_down].reshape(-1, D)
    tail = cells[:, -1]
    vec_sum = tail[:, : flat.shape[2]].reshape(vec.shape)
    bup_sum = tail[:, flat.shape[2] : used].reshape(-1)
    return out, up, down, vec_sum, bup_sum


def shards(
    tokens,
    scene_ids,
    gain_one,
    shift_one,
    w_qkv,
    w_out,
    b_out,
    gain_two,
    shift_two,
    w_up,
    b_up,
    w_down,
    b_down,
    cotangent,
    ndp,
):
    rows = tokens.shape[0]
    d, m = lax.axis_index("dp"), lax.axis_index("mp")
    quarter = 2 * (d % 2) + m % 2
    line = lambda v: v.reshape(1, D)
    both = ("dp", "mp")
    swap = swap_pairs(ndp)

    all_out, all_up, all_down = gather_weights(w_out, w_up, w_down, ndp)
    all_bup = lax.all_gather(b_up, "mp", axis=0).reshape(4, 1, FF // 4)
    scene = lax.ppermute(scene_ids, both, [(i, (i // 4 ^ 1) * 4 + i % 4) for i in range(4 * ndp)])
    scene = jnp.where(d % 2 == m // 2, scene_ids, scene)
    lo_f, hi_f, idc, idr = scene_ranges(scene, FWD_Q)
    lo_b, hi_b, _, _ = scene_ranges(scene, BWD_K)

    full, w_mine = gather_sequence(tokens, w_qkv)
    own_cot = lax.ppermute(cotangent, both, swap)
    own_tok = lax.dynamic_slice_in_dim(full, quarter * rows, rows, 0)
    normed, q, k, v, kt, vt = project(full, line(gain_one), line(shift_one), w_mine)
    attended, lse = attention((lo_f, hi_f, idc, idr), q, k, vt)
    att = exchange(attended, False, 2)
    layer_out, grad_mid, grad_att, d_out, d_up, d_down, d_vec, d_bup = middle_part(
        att, own_tok, own_cot, all_out, line(b_out), line(gain_two), line(shift_two), all_up, all_bup, all_down, line(b_down)
    )
    layer_out = lax.ppermute(layer_out, both, swap)
    grad_heads = exchange(grad_att, True, 3)
    g_out, g_up, g_down, g_vec, g_bup = reduce_weights(d_out, d_up, d_down, d_vec[:4], d_bup, ndp)
    dproj = attention_back((lo_b, hi_b, idc, idr), q, k, v, kt, attended, grad_heads, lse)
    partial, d_qkv, d_one = project_back(full, line(gain_one), normed, dproj, w_mine)
    tokens_grad, one_sum = return_home(partial, own_tok, grad_mid, line(gain_one), d_one, ndp)
    g_qkv = lax.psum(lax.ppermute(d_qkv, both, swap), "dp").astype(F32)
    return (
        layer_out,
        tokens_grad,
        one_sum[0],
        one_sum[1],
        g_qkv,
        g_out,
        g_vec[2],
        g_vec[0],
        g_vec[1],
        g_up,
        g_bup,
        g_down,
        g_vec[3],
    )


def solution(mesh):
    ndp = mesh.shape["dp"]
    return jax.shard_map(
        functools.partial(shards, ndp=ndp),
        mesh=mesh,
        in_specs=(
            P(("dp", "mp"), None),
            P("dp"),
            P(),
            P(),
            P(None, None, "mp"),
            P("mp", None),
            P(),
            P(),
            P(),
            P(None, "mp"),
            P("mp"),
            P("mp", None),
            P(),
            P(("dp", "mp"), None),
        ),
        out_specs=(
            P(("dp", "mp"), None),
            P(("dp", "mp"), None),
            P(),
            P(),
            P(None, None, "mp"),
            P("mp", None),
            P(),
            P(),
            P(),
            P(None, "mp"),
            P("mp"),
            P("mp", None),
            P(),
        ),
        check_vma=False,
    )
```

time: 1770 us -> 612 us (0.35)
  waiting for transfers between devices: 756 us -> 6.14 us
  matrix products: 570 us -> 0 us
  Pallas kernels: 0 us -> 387 us
  other arithmetic: 277 us -> 15.7 us
  blocking collectives: 55.4 us -> 111 us
  loops' own time: 20.8 us -> 0 us
    dot_general x53 -> x0, matrix products: 564 us -> none  [the longest x12 129 us: block_view(): jnp.einsum('qhd,khd->hqk', query_blk, key_rows, preferred_element_type=jn...]
    all_gather x4 -> x2, waiting for transfers between devices: 392 us -> 0.01 us  [the longest x1 0.01 us: gather_weights(): lax.all_gather(mine, ('dp', 'mp'), axis=0).reshape(ndp, 4, *mine.shape)]
    pallas_call x0 -> x9, Pallas kernels: none -> 387 us  [the longest x1 109 us: gather_sequence(): pl.pallas_call(gather_kernel, name='gather_sequence', in_specs=[ANY, ANY]...]
    reduce_scatter x4 -> x0, waiting for transfers between devices: 322 us -> none  [the longest x1 93.2 us: shards(): lax.psum_scatter(jnp.dot(attended, w_out, preferred_element_type=jnp.floa...]
    convert_element_type x23 -> x2, other arithmetic: 135 us -> 4.2 us  [the longest x1 2.52 us: shards(): g_qkv = lax.psum(lax.ppermute(d_qkv, both, swap), 'dp').astype(F32)]
    unnamed x0 -> x2, blocking collectives: none -> 101 us
    reduce_sum x15 -> x2, other arithmetic: 92.4 us -> 0.23 us  [the longest x1 0.14 us: scene_ranges(): jnp.sum(((scene[None, :] >= 0) & (scene[None, :] < jnp.arange(6, dtype=jn...]
    psum x2 -> x0, blocking collectives: 55.4 us -> none  [the longest x1 42.5 us: shards(): lax.psum((grad_gain_one, grad_shift_one, jnp.sum(grad_middle, axis=0), gr...]
  transfers between devices with their start and end apart: 9 -> 9, of which waited for: 9 -> 1; matrix products, arithmetic and copies ran while one was open for 3% -> 22% of each run, Pallas kernels for 0% -> 42%
where the time goes in v1:
time: 612 us; the launch traced here: 609 us
  Pallas kernels  387 us (63%)
  blocking collectives  111 us (18%)
  local copies, waits for them, and re-layouts  56.1 us (9%)
  starting transfers between devices  17.3 us (3%)
  other arithmetic  15.7 us (3%)
  between operations  15.6 us (3%)
  waiting for transfers between devices  6.14 us (1%)
    pallas_call x1, Pallas kernels, gather_sequence(): pl.pallas_call(gather_kernel, name='gather_sequence', in_specs=[ANY, ANY]...  109 us
    unnamed x2, blocking collectives  101 us
    pallas_call x1, Pallas kernels, return_home(): pl.pallas_call(return_kernel, name='return_home', in_specs=[ANY, ANY, ANY...  69.9 us
    pallas_call x1, Pallas kernels, attention_back(): pl.pallas_call(functools.partial(attention_back_kernel, heads, total), na...  56.9 us
    pallas_call x2, Pallas kernels, exchange(): pl.pallas_call(functools.partial(exchange_kernel, to_rows), name='exchang...  46.9 us
    pallas_call x1, Pallas kernels, middle_part(): pl.pallas_call(middle_kernel, name='middle_part', grid=(rows // ROWS_MID,...  36.8 us
    pallas_call x1, Pallas kernels, attention(): pl.pallas_call(functools.partial(attention_kernel, heads, total), name='a...  36.8 us
    unnamed x70, local copies, waits for them, and re-layouts  19 us
  transfers between devices with their start and end apart: 9, of which 1 were waited for; matrix products, arithmetic and copies ran while one was open for 22% of the time, Pallas kernels for 42%

profile of v1, /device:TPU:1, one launch (start us, length us, event | category | flops | bytes accessed | tf_op | source)
XLA Modules:
  0.0 608.9 jit_solution(11439403198462699788)
XLA Ops:
  9.9 5.6 collective-permute-start.1
  15.5 2.3 copy.86.wq
  17.9 109.3 %gather_sequence.1 = (bf16[3456,768]{1,0:T(8,128)(2,1)}, bf16[3,768,192]{2,1,0:T(8,128)(2,1)}) custom-call(bf16[864,768]{1,0:T(8,128)(2,1)} %tok.1, bf16[3,768,192]{2,1,0:T(8,128)(2,1)} %copy.86.wq), custom_call_target="tpu_custom_call" | custom-call | tf_op jit(solution)/shard_map/gather_sequence/pallas_call | solution.py:151
  129.0 2.6 constant_dynamic-slice_fusion.5.tok.own_tok
  134.0 15.2 %norm_and_project.1 = (bf16[3456,768]{1,0:T(8,128)(2,1)}, bf16[3,3840,128]{2,1,0:T(8,128)(2,1)}, bf16[3,3840,128]{2,1,0:T(8,128)(2,1)}, bf16[3,3840,128]{2,1,0:T...) custom-call(bf16[3456,768]{1,0:T(8,128)(2,1)} %get-tuple-element.36.x.tok, ...), custom_call_target="tpu_custom_call" | custom-call | tf_op jit(solution)/shard_map/norm_and_project/pallas_call | solution.py:272
  151.6 9.8 %all-gather.3.b_up = f32[4,1,384]{2,1,0:T(1,128)} all-gather(f32[1,1,384]{2,1,0:T(1,128)S(1)} %reshape.165), channel_id=3, replica_groups=mesh['dp'=8,'mp'=4] {'mp'}, dimensions={0}, use_global_device_ids=true | all-gather | bytes 7680 | tf_op jit(solution)/shard_map/all_gather | solution.py:840
  161.4 2.9 broadcast_in_dim.66.idc
  165.8 36.8 %attention.1 = (bf16[3456,192]{1,0:T(8,128)(2,1)}, f32[3,3456]{1,0:T(4,128)}) custom-call(s32[9]{0:T(128)} %get-tuple-element.119.lo, s32[9]{0:T(128)} %get-tuple-element.118.hi, s32[3840,1]{1,0:T(8,128)} %broadcast_in_dim.66.idc, s32[1,3840]{1,0:T(1,128)} %broadcast_in_dim.62.idr, bf16[3,3840,128]{2,1,0:T(8,128)(2,1)} %get-tuple-element.38.q, ...), custom_call_target="tpu_custom_call" | custom-call | tf_op jit(solution)/shard_map/attention/pallas_call | solution.py:338
  202.6 24.8 %exchange_heads.1.att = bf16[4,864,192]{2,1,0:T(8,128)(2,1)} custom-call(bf16[3456,192]{1,0:T(8,128)(2,1)} %get-tuple-element.41.src.out), custom_call_target="tpu_custom_call" | custom-call | tf_op jit(solution)/shard_map/exchange_heads/pallas_call | solution.py:206
  230.5 2.8 fusion.4
  238.2 36.8 %middle_part.1 = (bf16[864,768]{1,0:T(8,128)(2,1)}, f32[864,768]{1,0:T(8,128)}, bf16[4,864,192]{2,1,0:T(8,128)(2,1)}, bf16[768,768]{1,0:T(8,128)(2,1)}, bf16[4,7...) custom-call(bf16[4,864,192]{2,1,0:T(8,128)(2,1)} %exchange_heads.1.att, ...), custom_call_target="tpu_custom_call" | custom-call | tf_op jit(solution)/shard_map/middle_part/pallas_call | solution.py:540
  281.9 2.0 maximum_bitcast_fusion
  284.3 5.1 maximum_maximum_fusion
  289.4 6.4 %reshape.153 = bf16[3872,768]{1,0:T(8,128)(2,1)} reshape(bf16[8,4,121,768]{3,2,1,0:T(8,128)(2,1)} %maximum_maximum_fusion) | data formatting | bytes 11894784 | tf_op jit(solution)/shard_map/reshape | solution.py:801
  295.9 22.1 %exchange_rows.1.grad = bf16[3456,192]{1,0:T(8,128)(2,1)} custom-call(bf16[4,864,192]{2,1,0:T(8,128)(2,1)} %get-tuple-element.46.src), custom_call_target="tpu_custom_call" | custom-call | tf_op jit(solution)/shard_map/exchange_rows/pallas_call | solution.py:206
  318.0 56.9 %attention_back.1.dproj = bf16[3,3456,192]{2,1,0:T(8,128)(2,1)} custom-call(s32[9]{0:T(128)} %get-tuple-element.119.lo, s32[9]{0:T(128)} %get-tuple-element.118.hi, s32[3840,1]{1,0:T(8,128)} %broadcast_in_dim.66.idc, s32[1,3840]{1,0:T(1,128)} %broadcast_in_dim.62.idr, bf16[3,3840,128]{2,1,0:T(8,128)(2,1)} %get-tuple-element.38.q, ...), custom_call_target="tpu_custom_call" | custom-call | tf_op jit(solution)/shard_map/attention_back/pallas_call | solution.py:437
  374.9 15.8 %project_back.1 = (bf16[3456,768]{1,0:T(8,128)(2,1)}, bf16[3,768,192]{2,1,0:T(8,128)(2,1)S(1)}, f32[8,768]{1,0:T(8,128)S(1)}) custom-call(bf16[3456,768]{1,0:T(8,128)(2,1)} %get-tuple-element.36.x.tok, f32[1,768]{1,0:T(1,128)S(1)} %reshape.138.gain, bf16[3456,768]{1,0:T(8,128)(2,1)} %get-tuple-element.43.normed, bf16[3,3456,192]{2,1,0:T(8,128)(2,1)} %attention_back.1.dproj, ...), custom_call_target="tpu_custom_call" | custom-call | tf_op jit(solution)/shard_map/project_back/pallas_call | solution.py:584
  392.0 2.0 collective-permute-start.3
  394.0 81.8 %fusion = bf16[488,768]{1,0:T(8,128)(2,1)S(1)} fusion(bf16[3872,768]{1,0:T(8,128)(2,1)} %reshape.153), kind=kCustom, calls=%all-reduce-scatter | all-reduce-scatter fusion | flops 2998273 | bytes 6697472
  479.1 6.1 collective-permute-done.4
  486.9 19.0 %fusion.1 = bf16[128,768]{1,0:T(8,128)(2,1)S(1)} fusion(bf16[484,768]{1,0:T(8,128)(2,1)S(1)} %constant_dynamic-slice_fusion), kind=kCustom, calls=%all-reduce-scatter.1 | all-reduce-scatter fusion | flops 393217 | bytes 940544
  509.6 6.3 %collective-permute-start.2 = (bf16[864,768]{1,0:T(8,128)(2,1)}, bf16[864,768]{1,0:T(8,128)(2,1)S(1)}, u32[]{:S(2)}, u32[]{:S(2)}) collective-permute-start(bf16[864,768]{1,0:T(8,128)(2,1)} %get-tuple-element.42), channel_id=1, source_target_pairs={{0,0},{1,1},{2,4},{3,5},{4,2},{5,3},{6,6},{7,7},{8,8},{9,9},{10,12... | collective-permute-start | bytes 3981320 | tf_op jit(solution)/shard_map/ppermute | solution.py:855
  515.9 69.9 %return_home.1 = (f32[864,768]{1,0:T(8,128)S(1)}, f32[8,768]{1,0:T(8,128)S(1)}) custom-call(bf16[3456,768]{1,0:T(8,128)(2,1)} %get-tuple-element.48.partial, bf16[864,768]{1,0:T(8,128)(2,1)S(1)} %copy-done.2, f32[864,768]{1,0:T(8,128)} %get-tuple-element.49.grad_mid, f32[1,768]{1,0:T(1,128)S(1)} %reshape.138.gain, f32[8,768]{1,0:T(8,128)S(1)} %get-tuple-element.50.vec), custom_call_target="tpu_custom_call" | custom-call | tf_op jit(solution)/shard_map/return_home/pallas_call | solution.py:728
  587.9 2.5 convert_element_type.20
  (138 shorter events, 48.7 us)
Async XLA Ops:
  7.2 222.0 %all-gather.8.cloned.1.call-start = ((), (), s32[]{:S(2)}) async-start(), calls=%async_computation.1 | async-start | bytes 6082560 | tf_op jit(solution)/shard_map/all_gather | solution.py:780
  9.8 578.1 %all-reduce.7.cloned.1.call-start = ((), (), s32[]{:S(2)}) async-start(), calls=%async_computation | async-start | bytes 1769472 | tf_op jit(solution)/shard_map/psum | solution.py:861
  9.8 151.6 %collective-permute-start = (s32[3456]{0:T(1024)}, s32[3456]{0:T(1024)S(1)}, u32[]{:S(2)}, u32[]{:S(2)}) collective-permute-start(s32[3456]{0:T(1024)} %param.15), channel_id=1, source_target_pairs={{0,4},{1,5},{2,6},{3,7},{4,0},{5,1},{6,2},{7,3},{8,12},{9,13},{10,... | collective-permute-start | bytes 41480 | tf_op jit(solution)/shard_map/ppermute | solution.py:841
  9.9 228.3 %collective-permute-start.1 = (bf16[864,768]{1,0:T(8,128)(2,1)}, bf16[864,768]{1,0:T(8,128)(2,1)}, u32[]{:S(2)}, u32[]{:S(2)}) collective-permute-start(bf16[864,768]{1,0:T(8,128)(2,1)} %param.27), channel_id=1, source_target_pairs={{0,0},{1,1},{2,4},{3,5},{4,2},{5,3},{6,6},{7,7},{8,8},{9,9},{10,12... | collective-permute-start | bytes 3981320 | tf_op jit(solution)/shard_map/ppermute | solution.py:847
  128.8 2.7 copy-start.17
  128.8 2.7 copy-start.18
  128.8 2.7 copy-start.23
  128.8 2.7 copy-start.19
  128.9 3.3 copy-start.20
  128.9 3.9 copy-start.21
  128.9 4.5 copy-start.22
  128.9 5.1 copy-start.3
  134.0 27.4 %copy-start.15 = (s32[3456]{0:T(1024)S(1)}, s32[3456]{0:T(1024)}, u32[]{:S(2)}) copy-start(s32[3456]{0:T(1024)} %param.15) | copy-start | bytes 41476
  202.6 24.8 %copy-start.14 = (f32[3,3456]{1,0:T(4,128)S(1)}, f32[3,3456]{1,0:T(4,128)}, u32[]{:S(2)}) copy-start(f32[3,3456]{1,0:T(4,128)} %get-tuple-element.47) | copy-start | bytes 124420
  392.0 85.8 %copy-start.25 = (u32[32]{0:T(128)S(1)}, u32[32]{0:T(128)}, u32[]{:S(2)}) copy-start(u32[32]{0:T(128)} %constant.98) | copy-start | bytes 388
  392.0 94.8 %collective-permute-start.3 = (bf16[3,768,192]{1,2,0:T(8,128)(2,1)}, bf16[3,768,192]{1,2,0:T(8,128)(2,1)}, u32[]{:S(2)}, u32[]{:S(2)}) collective-permute-start(bf16[3,768,192]{1,2,0:T(8,128)(2,1)} %copy.95), channel_id=1, source_target_pairs={{0,0},{1,1},{2,4},{3,5},{4,2},{5,3},{6,6},{7,7},{8,8},{9,9},{10,12... | collective-permute-start | bytes 2654216 | tf_op jit(solution)/shard_map/ppermute | solution.py:861
  475.9 9.3 %collective-permute-start.4 = (bf16[28,768]{1,0:T(8,128)(2,1)S(1)}, bf16[28,768]{1,0:T(8,128)(2,1)S(1)}, u32[]{:S(2)}, u32[]{:S(2)}) collective-permute-start(bf16[28,768]{1,0:T(8,128)(2,1)S(1)} %slice.132), channel_id=1, source_target_pairs={{0,4},{4,8},{8,12},{12,16},{16,20},{20,24},{24,28},{1,5},{5,9},{9,... | collective-permute-start | bytes 129032
  479.1 28.1 %copy-start.24 = (u32[32]{0:T(128)S(1)}, u32[32]{0:T(128)}, u32[]{:S(2)}) copy-start(u32[32]{0:T(128)} %constant.102) | copy-start | bytes 388
  486.6 29.3 %copy-start.2 = (bf16[864,768]{1,0:T(8,128)(2,1)S(1)}, bf16[864,768]{1,0:T(8,128)(2,1)}, u32[]{:S(2)}) copy-start(bf16[864,768]{1,0:T(8,128)(2,1)} %constant_dynamic-slice_fusion.5.tok.own_tok) | copy-start | bytes 3981316
  486.8 103.6 %all-gather.10.cloned.1.call-start = ((), (), s32[]{:S(2)}) async-start(), calls=%async_computation.2 | async-start | bytes 1769472 | tf_op jit(solution)/shard_map/all_gather | solution.py:804
  505.9 2.6 collective-permute-start.5
  509.6 80.8 %collective-permute-start.2 = (bf16[864,768]{1,0:T(8,128)(2,1)}, bf16[864,768]{1,0:T(8,128)(2,1)S(1)}, u32[]{:S(2)}, u32[]{:S(2)}) collective-permute-start(bf16[864,768]{1,0:T(8,128)(2,1)} %get-tuple-element.42), channel_id=1, source_target_pairs={{0,0},{1,1},{2,4},{3,5},{4,2},{5,3},{6,6},{7,7},{8,8},{9,9},{10,12... | collective-permute-start | bytes 3981320 | tf_op jit(solution)/shard_map/ppermute | solution.py:855
  593.1 4.3 copy-start.9
  599.4 3.0 copy-start.1
  (11 other events, 17.6 us)
Sparse Core Ops, SparseCore 0:
  11.4 96.3 all-gather.7
  487.0 55.9 all-reduce.6
  545.4 26.2 all-gather.9

commit v2 on v1

v2 whole, which is shorter than its diff:
```python
import functools

import jax
import jax.numpy as jnp
from jax import lax
from jax.experimental import pallas as pl
from jax.experimental.pallas import tpu as pltpu
from jax.sharding import PartitionSpec as P

HEAD = 64
D = 768
FF = 1536
LANES = 128
PAD = 384
OUT_ROWS = D // 4
UP_ROWS = FF // 4
VEC_AT = OUT_ROWS + 2 * UP_ROWS
UNITS = 1024
EPS = 1e-05
MASKED = -1e30
MESH = pl.DeviceIdType.MESH
F32 = jnp.float32
BF16 = jnp.bfloat16
VMEM = pl.BlockSpec(memory_space=pltpu.VMEM)
SMEM = pl.BlockSpec(memory_space=pltpu.SMEM)
ANY = pl.BlockSpec(memory_space=pl.ANY)
DMA = pltpu.SemaphoreType.DMA

NN = (((1,), (0,)), ((), ()))
NT = (((1,), (1,)), ((), ()))
TN = (((0,), (0,)), ((), ()))


def dot(a, b, dims=NN):
    return lax.dot_general(a, b, dims, preferred_element_type=F32)


def work(us):
    return pl.CostEstimate(flops=us * 10**9, bytes_accessed=us * 3 * 10**6, transcendentals=0)


def limit(mib):
    return pltpu.CompilerParams(vmem_limit_bytes=mib << 20)


class Place:
    def __init__(self):
        self.d = lax.axis_index("dp")
        self.m = lax.axis_index("mp")
        self.c = lax.rem(self.d, 2)
        self.r = lax.rem(self.m, 2)
        self.hf = self.m // 2
        self.q = 2 * self.c + self.r
        self.native = self.c == self.hf
        self.sibling = (self.d + 1 - 2 * self.c, self.m)
        self.cross = (self.d, self.m + 1 - 2 * self.r)
        self.partner = (self.d + 1 - 2 * self.c, lax.rem(self.m + 2, 4))

    def member(self, quarter):
        return (self.d - self.c + quarter // 2, 2 * self.hf + quarter % 2)


def greet(others):
    barrier = pltpu.get_barrier_semaphore()
    for other in others:
        pl.semaphore_signal(barrier, inc=1, device_id=other, device_id_type=MESH)
    pl.semaphore_wait(barrier, len(others))


def remote(src, dst, send, recv, device):
    return pltpu.make_async_remote_copy(
        src_ref=src, dst_ref=dst, send_sem=send, recv_sem=recv, device_id=device, device_id_type=MESH
    )


PIECES = 3
TILE = 384


def normalise(x):
    centred = x - jnp.mean(x, axis=-1, keepdims=True)
    scale = lax.rsqrt(jnp.mean(centred * centred, axis=-1, keepdims=True) + EPS)
    return centred * scale, scale


def widen(x, ones, rows):
    lane = lax.broadcasted_iota(jnp.int32, (rows, LANES - HEAD), 1)
    return jnp.concatenate([x, jnp.where(lane < ones, 1.0, 0.0).astype(x.dtype)], axis=1)


def start_kernel(
    heads, tok, wq, ids, bup, gain, shift, mine,
    full, own, w_out, ids_own, bups, normed, q, k, v, kt, vt, units,
    buf, w, low_s, q_s, k_s, v_s, kt_s, vt_s,
    swap_s, swap_r, cross_s, cross_r, sib_s, sib_r, fwd_s, fwd_r, w_s, w_r, ids_s, ids_r, b_s, b_r, out_s, late_s,
    uz_s, uz_r,
):
    me = Place()
    foreign = jnp.logical_not(me.native)
    rows = tok.shape[0]
    piece = rows // PIECES
    total = buf.shape[0]
    tiles = total // TILE
    groups = w.shape[1]
    group = me.d // 2
    around = [(me.d, lax.rem(me.m + j, 4)) for j in range(1, 4)]
    lines = [(2 * lax.rem(group + j, groups) + me.c, me.m) for j in range(1, groups)]
    greet([me.sibling, me.partner] + around + lines)

    def rows_of(quarter, n):
        p = jnp.where(me.hf == 0, n, PIECES - 1 - n)
        return pl.ds(pl.multiple_of(quarter * rows + p * piece, 16), piece)

    def part(quarter, n):
        return buf.at[rows_of(quarter, n)]

    sib_q = 2 * (1 - me.c) + me.r
    cross_q = 2 * me.c + 1 - me.r
    sib_cross_q = 2 * (1 - me.c) + 1 - me.r

    def swap(n):
        p = jnp.where(me.hf == 1, n, PIECES - 1 - n)
        src = tok.at[pl.ds(pl.multiple_of(p * piece, 16), piece)]
        dst = buf.at[pl.ds(pl.multiple_of(sib_q * rows + p * piece, 16), piece)]
        return remote(src, dst, swap_s.at[n], swap_r.at[n], me.partner)

    def swap_in(n):
        return remote(part(me.q, n), part(me.q, n), swap_s.at[n], swap_r.at[n], me.partner)

    def cross(quarter, n):
        return remote(part(quarter, n), part(quarter, n), cross_s.at[n], cross_r.at[n], me.cross)

    def sib(quarter, n):
        return remote(part(quarter, n), part(quarter, n), sib_s.at[n], sib_r.at[n], me.sibling)

    def forward(quarter, n):
        return remote(part(quarter, n), part(quarter, n), fwd_s.at[n], fwd_r.at[n], me.sibling)

    weight = remote(wq.at[:, group], w.at[:, group], w_s.at[0], w_r.at[0], me.partner)

    def weight_share(j):
        return remote(w.at[:, group], w.at[:, group], w_s.at[j], w_r.at[j], lines[j - 1])

    def weight_in(j):
        source = lax.rem(group + groups - j, groups)
        return remote(w.at[:, source], w.at[:, source], w_s.at[j], w_r.at[j], lines[j - 1])

    unit_own = pltpu.make_async_copy(mine, units.at[me.m], late_s.at[7])

    def unit_z(j, source):
        return remote(mine, units.at[source], uz_s.at[j], uz_r.at[j], around[j])

    scenes = remote(ids, ids_own, ids_s, ids_r, me.sibling)
    unit_own.start()
    for j in range(3):
        remote(bup, bups.at[me.m], b_s.at[j], b_r.at[j], around[j]).start()
    bups[me.m] = bup[...]

    @pl.when(me.native)
    def _():
        scenes.start()
        buf[pl.ds(pl.multiple_of(me.q * rows, 16), rows), :] = tok[...]
        for n in range(PIECES):
            cross(me.q, n).start()
            sib(me.q, n).start()
        w[...] = wq[...]
        ids_own[...] = ids[...]

    @pl.when(foreign)
    def _():
        weight.start()
        for n in range(PIECES):
            swap(n).start()

    def share(n):
        swap_in(n).wait_recv()
        cross(me.q, n).start()
        sib(me.q, n).start()

    def pass_on(n):
        cross(cross_q, n).wait_recv()
        forward(cross_q, n).start()

    def from_sibling(n):
        sib(sib_q, n).wait_recv()
        forward(sib_cross_q, n).wait_recv()

    def outputs(t):
        span = pl.ds(pl.multiple_of(t * TILE, LANES), TILE)
        pairs = [
            (low_s.at[span], normed.at[span]),
            (buf.at[span], full.at[span]),
            (q_s.at[:, span], q.at[:, span]),
            (k_s.at[:, span], k.at[:, span]),
            (v_s.at[:, span], v.at[:, span]),
            (kt_s.at[:, :, span], kt.at[:, :, span]),
            (vt_s.at[:, :, span], vt.at[:, :, span]),
        ]
        return [pltpu.make_async_copy(src, dst, out_s.at[t, j]) for j, (src, dst) in enumerate(pairs)]

    line = lax.broadcasted_iota(jnp.int32, (16, TILE), 0)
    ones = jnp.where(line < 1, 1.0, 0.0).astype(BF16)

    def compute(first, stride, count):
        def one(n, _):
            at = first + stride * n
            t = jnp.where(me.hf == 0, at, tiles - 1 - at)
            span = pl.ds(pl.multiple_of(t * TILE, LANES), TILE)
            unit, _ = normalise(buf[span, :].astype(F32))
            low = (unit * gain[...] + shift[...]).astype(BF16)
            low_s[span, :] = low
            qs = (dot(low, w[0].reshape(D, -1)).astype(BF16).astype(F32) * HEAD**-0.5).astype(BF16)
            ks = dot(low, w[1].reshape(D, -1))
            vs = dot(low, w[2].reshape(D, -1))
            kts = ks.T.astype(BF16)
            vts = vs.T.astype(BF16)
            ks = ks.astype(BF16)
            vs = vs.astype(BF16)
            for h in range(heads):
                cols = slice(h * HEAD, (h + 1) * HEAD)
                q_s[h, span, :] = widen(qs[:, cols], 0, TILE)
                k_s[h, span, :] = widen(ks[:, cols], 3, TILE)
                v_s[h, span, :] = widen(vs[:, cols], 3, TILE)
                kt_s[h, :, span] = kts[cols]
                vt_s[h, :HEAD, span] = vts[cols]
                vt_s[h, HEAD:, span] = ones
            for copy in outputs(t):
                copy.start()
            return 0

        lax.fori_loop(0, count, one, 0)

    pad = pl.ds(total, PAD)
    zeros = jnp.zeros((heads, PAD, LANES), BF16)
    for ref in (q_s, k_s, v_s):
        ref[:, pad, :] = zeros
    for ref in (kt_s, vt_s):
        ref[:, :, pad] = jnp.zeros((heads, ref.shape[1], PAD), BF16)
    padding = [
        pltpu.make_async_copy(src, dst, late_s.at[j])
        for j, (src, dst) in enumerate(
            [(a.at[:, pad], b.at[:, pad]) for a, b in ((q_s, q), (k_s, k), (v_s, v))]
            + [(a.at[:, :, pad], b.at[:, :, pad]) for a, b in ((kt_s, kt), (vt_s, vt))]
        )
    ]
    for copy in padding:
        copy.start()

    @pl.when(me.native)
    def _():
        for n in range(PIECES):
            pass_on(n)

    @pl.when(foreign)
    def _():
        weight.wait_recv()
        for j in range(1, groups):
            weight_share(j).start()
        for n in range(PIECES):
            share(n)
        for j in range(1, groups):
            weight_in(j).wait_recv()
        for n in range(PIECES):
            from_sibling(n)

    for j in range(3):
        unit_z(j, me.m).start()
    compute(0, 1, 2)

    @pl.when(foreign)
    def _():
        pass_on(0)

    compute(2, 1, 2)

    @pl.when(foreign)
    def _():
        pass_on(1)

    @pl.when(me.native)
    def _():
        from_sibling(0)

    compute(4, 1, 1)

    @pl.when(me.native)
    def _():
        from_sibling(1)

    compute(5, 2, 2)

    @pl.when(foreign)
    def _():
        pass_on(2)

    @pl.when(me.native)
    def _():
        from_sibling(2)

    own_copy = pltpu.make_async_copy(buf.at[pl.ds(pl.multiple_of(me.q * rows, 16), rows)], own, late_s.at[5])
    w_copy = pltpu.make_async_copy(w, w_out, late_s.at[6])
    own_copy.start()
    w_copy.start()
    compute(6, 2, 2)
    unit_own.wait()
    for j in range(3):
        unit_z(j, lax.rem(me.m + 3 - j, 4)).wait_recv()
        unit_z(j, me.m).wait_send()

    for j in range(3):
        source = lax.rem(me.m + 3 - j, 4)
        remote(bup, bups.at[source], b_s.at[j], b_r.at[j], around[j]).wait_recv()
        remote(bup, bups.at[me.m], b_s.at[j], b_r.at[j], around[j]).wait_send()

    @pl.when(me.native)
    def _():
        scenes.wait_send()

    @pl.when(foreign)
    def _():
        scenes.wait_recv()
        weight.wait_send()
        for j in range(1, groups):
            weight_share(j).wait_send()
        for n in range(PIECES):
            swap(n).wait_send()

    for n in range(PIECES):
        cross(me.q, n).wait_send()
        sib(me.q, n).wait_send()
        forward(cross_q, n).wait_send()
    for copy in padding + [own_copy, w_copy]:
        copy.wait()

    def finish_tile(t, _):
        for copy in outputs(t):
            copy.wait()
        return 0

    lax.fori_loop(0, tiles, finish_tile, 0)


def start(tokens, w_qkv, scene_ids, b_up, gain, shift, mine, ndp):
    rows = tokens.shape[0]
    total = 4 * rows
    heads = w_qkv.shape[2] // HEAD
    groups = ndp // 2
    w_qkv = w_qkv.reshape(3, groups, D // groups, -1)
    units = (4,) + mine.shape
    wide = total + PAD
    shape = jax.ShapeDtypeStruct
    rowed = (heads, wide, LANES)
    k_cols, v_cols = (heads, HEAD, wide), (heads, HEAD + 16, wide)
    three = DMA((PIECES,))
    return pl.pallas_call(
        functools.partial(start_kernel, heads),
        name="start",
        cost_estimate=work(50),
        in_specs=[VMEM] * 6 + [ANY],
        out_specs=[ANY, ANY, ANY, VMEM, VMEM] + [ANY] * 7,
        out_shape=[
            shape((total, D), BF16),
            shape((rows, D), BF16),
            shape(w_qkv.shape, BF16),
            shape(scene_ids.shape, jnp.int32),
            shape((4,) + b_up.shape, F32),
            shape((total, D), BF16),
            shape(rowed, BF16),
            shape(rowed, BF16),
            shape(rowed, BF16),
            shape(k_cols, BF16),
            shape(v_cols, BF16),
            shape(units, BF16),
        ],
        scratch_shapes=[
            pltpu.VMEM((total, D), BF16),
            pltpu.VMEM(w_qkv.shape, BF16),
            pltpu.VMEM((total, D), BF16),
            pltpu.VMEM(rowed, BF16),
            pltpu.VMEM(rowed, BF16),
            pltpu.VMEM(rowed, BF16),
            pltpu.VMEM(k_cols, BF16),
            pltpu.VMEM(v_cols, BF16),
        ]
        + [three] * 8
        + [DMA((groups,))] * 2
        + [DMA] * 2
        + [DMA((3,))] * 2
        + [DMA((total // TILE, 7)), DMA((8,))]
        + [DMA((3,))] * 2,
        compiler_params=pltpu.CompilerParams(
            collective_id=1, has_side_effects=True, vmem_limit_bytes=60 << 20
        ),
    )(tokens, w_qkv, scene_ids, b_up, gain, shift, mine)


def exchange_kernel(to_rows, src, dst, send, recv, loc):
    me = Place()
    others = []
    for k in range(1, 4):
        quarter = lax.rem(me.q + k, 4)
        others.append(me.member(quarter))
    greet(others)
    rows = (dst.shape[0] if to_rows else src.shape[0]) // 4

    def block(ref, quarter, by_rows):
        if by_rows:
            return ref.at[pl.ds(pl.multiple_of(quarter * rows, 16), rows)]
        return ref.at[quarter]

    def copy(k):
        quarter = lax.rem(me.q + k, 4)
        return remote(
            block(src, quarter, not to_rows), block(dst, me.q, to_rows), send.at[k], recv.at[k], others[k - 1]
        )

    def arrival(k):
        quarter = lax.rem(me.q + 4 - k, 4)
        return remote(
            block(src, quarter, not to_rows), block(dst, quarter, to_rows), send.at[k], recv.at[k], others[3 - k]
        )

    for k in (2, 1, 3):
        copy(k).start()
    own = pltpu.make_async_copy(block(src, me.q, not to_rows), block(dst, me.q, to_rows), loc)
    own.start()
    for k in (1, 2, 3):
        arrival(k).wait_recv()
    for k in (1, 2, 3):
        copy(k).wait_send()
    own.wait()


def exchange(values, to_rows, number):
    if to_rows:
        _, rows, width = values.shape
        shape = (4 * rows, width)
    else:
        rows, width = values.shape
        shape = (4, rows // 4, width)
    return pl.pallas_call(
        functools.partial(exchange_kernel, to_rows),
        name="exchange_rows" if to_rows else "exchange_heads",
        in_specs=[ANY],
        out_specs=ANY,
        out_shape=jax.ShapeDtypeStruct(shape, values.dtype),
        scratch_shapes=[DMA((4,)), DMA((4,)), DMA],
        cost_estimate=work(20),
        compiler_params=pltpu.CompilerParams(collective_id=number, has_side_effects=True),
    )(values)


FWD_Q, FWD_K = 384, 512
BWD_Q, BWD_K = 384, 384


def attention_kernel(heads, total, lo, hi, idc, idr, q, k, vt, out, lse):
    step = FWD_K // LANES

    def one_block(i, _):
        r0 = pl.multiple_of(i * FWD_Q, LANES)
        qs = [q[h, pl.ds(r0, FWD_Q), :] for h in range(heads)]
        mine = idr[:, pl.ds(r0, FWD_Q)]

        def keys(at, carry):
            c0 = pl.multiple_of(at * LANES, LANES)
            allowed = idc[pl.ds(c0, FWD_K), :] == mine
            new = []
            for h in range(heads):
                top, acc = carry[h]
                s = jnp.where(allowed, dot(k[h, pl.ds(c0, FWD_K), :], qs[h], NT), MASKED)
                above = jnp.maximum(top, jnp.max(s, axis=0, keepdims=True))
                p = jnp.exp(s - above).astype(BF16)
                acc = acc * jnp.exp(top - above) + dot(vt[h, :, pl.ds(c0, FWD_K)], p)
                new.append((above, acc))
            return tuple(new)

        start = tuple(
            (jnp.full((1, FWD_Q), MASKED, F32), jnp.zeros((vt.shape[1], FWD_Q), F32)) for _ in range(heads)
        )
        first = lo[i]
        count = (hi[i] - first + step - 1) // step
        done = lax.fori_loop(0, count, lambda n, c: keys(first + n * step, c), start)
        valid = jnp.where(mine >= 0, 1.0, 0.0)
        mixed = []
        for h in range(heads):
            top, acc = done[h]
            row_total = acc[HEAD : HEAD + 1]
            mixed.append(acc[:HEAD] * (valid / row_total))
            lse[pl.ds(h, 1), pl.ds(r0, FWD_Q)] = top + jnp.log(row_total)
        out[pl.ds(r0, FWD_Q), :] = jnp.concatenate(mixed, axis=0).T.astype(BF16)
        return 0

    lax.fori_loop(0, total // FWD_Q, one_block, 0)


def attention(ids, q, k, vt):
    lo, hi, idc, idr = ids
    heads, wide, _ = q.shape
    total = wide - PAD
    return pl.pallas_call(
        functools.partial(attention_kernel, heads, total),
        name="attention",
        cost_estimate=work(31),
        in_specs=[SMEM, SMEM] + [VMEM] * 5,
        out_specs=[VMEM, VMEM],
        out_shape=[
            jax.ShapeDtypeStruct((total, heads * HEAD), BF16),
            jax.ShapeDtypeStruct((heads, total), F32),
        ],
        compiler_params=limit(56),
    )(lo, hi, idc, idr, q, k, vt)


def thirds(x):
    a = x.astype(BF16).astype(F32)
    b = (x - a).astype(BF16).astype(F32)
    return a, b, x - a - b


def attention_back_kernel(
    heads, total, lo, hi, idc, idr, q, k, v, kt, out, grad, lse, dproj, qe, ge, dq
):
    wide = q.shape[1]
    step = BWD_Q // LANES
    lane = lax.broadcasted_iota(jnp.int32, (PAD, LANES), 1)

    def extend(values, tail):
        a, b, c = thirds(tail)
        return jnp.where(
            lane == HEAD, a, jnp.where(lane == HEAD + 1, b, jnp.where(lane == HEAD + 2, c, values))
        ).astype(BF16)

    def prepare(i, _):
        rows = pl.ds(pl.multiple_of(i * PAD, LANES), PAD)
        valid = jnp.where(idc[rows, :] >= 0, 1.0, 0.0)
        grads = grad[rows, :].astype(F32) * valid
        inner = grads * out[rows, :].astype(F32)
        for h in range(heads):
            cols = slice(h * HEAD, (h + 1) * HEAD)
            g = jnp.concatenate([grads[:, cols], jnp.zeros((PAD, LANES - HEAD), F32)], axis=1)
            ge[h, rows, :] = extend(g, -jnp.sum(inner[:, cols], axis=1, keepdims=True))
            qe[h, rows, :] = extend(q[h, rows, :].astype(F32), -lse[rows, h : h + 1])
            dq[h, :, rows] = jnp.zeros((HEAD, PAD), F32)
        return 0

    lax.fori_loop(0, total // PAD, prepare, 0)
    for h in range(heads):
        qe[h, total:, :] = jnp.zeros((wide - total, LANES), BF16)
        ge[h, total:, :] = jnp.zeros((wide - total, LANES), BF16)
        dq[h, :, total:] = jnp.zeros((HEAD, wide - total), F32)

    def one_block(i, _):
        c0 = pl.multiple_of(i * BWD_K, LANES)
        cols = pl.ds(c0, BWD_K)
        mine = idc[cols, :]

        def queries(at, carry):
            r0 = pl.multiple_of(at * LANES, LANES)
            rows = pl.ds(r0, BWD_Q)
            allowed = mine == idr[:, rows]
            new = []
            for h in range(heads):
                dk, dv = carry[h]
                qh = qe[h, rows, :]
                gh = ge[h, rows, :]
                p = jnp.where(allowed, jnp.exp(dot(k[h, cols, :], qh, NT)), 0.0)
                ds = (p * dot(v[h, cols, :], gh, NT)).astype(BF16)
                dv = dv + dot(p.astype(BF16), gh)
                dk = dk + dot(ds, qh)
                dq[h, :, rows] += dot(kt[h, :, cols], ds)
                new.append((dk, dv))
            return tuple(new)

        zero = jnp.zeros((BWD_K, LANES), F32)
        first = lo[i]
        count = (hi[i] - first + step - 1) // step
        done = lax.fori_loop(
            0, count, lambda n, c: queries(first + n * step, c), tuple((zero, zero) for _ in range(heads))
        )
        for part in range(2):
            joined = jnp.concatenate([done[h][part][:, :HEAD] for h in range(heads)], axis=1)
            dproj[part + 1, cols, :] = joined.astype(BF16)
        return 0

    lax.fori_loop(0, total // BWD_K, one_block, 0)

    def finish(i, _):
        rows = pl.ds(pl.multiple_of(i * PAD, LANES), PAD)
        joined = jnp.concatenate([dq[h, :, rows] for h in range(heads)], axis=0)
        dproj[0, rows, :] = (joined * HEAD**-0.5).T.astype(BF16)
        return 0

    lax.fori_loop(0, total // PAD, finish, 0)


def attention_back(ids, q, k, v, kt, out, grad, lse):
    lo, hi, idc, idr = ids
    heads, wide, _ = q.shape
    total = wide - PAD
    return pl.pallas_call(
        functools.partial(attention_back_kernel, heads, total),
        name="attention_back",
        cost_estimate=work(51),
        in_specs=[SMEM, SMEM] + [VMEM] * 9,
        out_specs=VMEM,
        out_shape=jax.ShapeDtypeStruct((3, total, heads * HEAD), BF16),
        scratch_shapes=[
            pltpu.VMEM((heads, wide, LANES), BF16),
            pltpu.VMEM((heads, wide, LANES), BF16),
            pltpu.VMEM((heads, HEAD, wide), F32),
        ],
        compiler_params=limit(60),
    )(lo, hi, idc, idr, q, k, v, kt, out, grad, lse.T)


def scene_ranges(scene, block):
    total = scene.shape[0]
    place = jnp.arange(total, dtype=jnp.int32)
    ids = jnp.where(scene >= 0, scene, -1 - place)
    before = jnp.sum(
        ((scene[None, :] >= 0) & (scene[None, :] < jnp.arange(6, dtype=jnp.int32)[:, None])).astype(jnp.int32), axis=1
    )
    first, last = scene[0::block], scene[block - 1 :: block]
    start = jnp.arange(total // block, dtype=jnp.int32) * block
    pick = lambda number: jnp.sum(
        jnp.where(number[:, None] == jnp.arange(6, dtype=jnp.int32)[None, :], before[None, :], 0), axis=1
    )
    lo = jnp.where(first >= 0, pick(first), start) // LANES
    hi = (jnp.where(last >= 0, pick(last + 1), start + block) + LANES - 1) // LANES
    padded = jnp.pad(ids, (0, PAD), constant_values=-(1 << 20))
    return lo, hi, padded[:, None], padded[None, :]


ROWS_MID = 288


def middle_kernel(
    weights, att, tok, cot, b_out, gain, shift, b_up, b_down,
    layer_out, grad_mid, grad_att, cells, w, acc, vec, bup, sems,
):
    step = pl.program_id(0)
    ndp, parts, piece, _ = cells.shape
    width = att.shape[2]

    @pl.when(step == 0)
    def _():
        def load(i):
            rows = pl.ds(i // parts * piece, piece)
            return pltpu.make_async_copy(weights.at[i // parts, i % parts], w.at[i % parts, rows], sems.at[i])

        for i in range(ndp * parts):
            load(i).start()
        for ref in (acc, vec, bup):
            ref[...] = jnp.zeros_like(ref)
        for i in range(ndp * parts):
            load(i).wait()

    out_rows = slice(0, OUT_ROWS)
    down_rows = slice(OUT_ROWS, OUT_ROWS + UP_ROWS)
    up_rows = slice(OUT_ROWS + UP_ROWS, VEC_AT)
    atts = [att[v] for v in range(parts)]
    middle = tok[...].astype(F32) + b_out[...]
    for v in range(parts):
        middle = middle + dot(atts[v], w[v, out_rows])
    unit, scale = normalise(middle)
    low = (unit * gain[...] + shift[...]).astype(BF16)
    cot_low = cot[...]
    cot_full = cot_low.astype(F32)
    out = middle + b_down[...]
    grad_norm = jnp.zeros_like(middle)
    for v in range(parts):
        hidden = dot(low, w[v, up_rows], NT) + b_up[v]
        below = 0.5 * (1.0 + lax.erf(hidden * 0.5**0.5))
        density = jnp.exp(-0.5 * hidden * hidden) * 0.3989422804014327
        active = (hidden * below).astype(BF16)
        out = out + dot(active, w[v, down_rows])
        grad_hidden = (dot(cot_low, w[v, down_rows], NT) * (below + hidden * density)).astype(BF16)
        grad_norm = grad_norm + dot(grad_hidden, w[v, up_rows])
        acc[v, down_rows] += dot(active, cot_low, TN)
        acc[v, up_rows] += dot(grad_hidden, low, TN)
        bup[v] += jnp.sum(grad_hidden.astype(F32), axis=0, keepdims=True)
    layer_out[...] = out.astype(BF16)
    scaled = grad_norm * gain[...]
    back = cot_full + scale * (
        scaled
        - jnp.mean(scaled, axis=-1, keepdims=True)
        - unit * jnp.mean(scaled * unit, axis=-1, keepdims=True)
    )
    grad_mid[...] = back
    back_low = back.astype(BF16)
    for v in range(parts):
        acc[v, out_rows] += dot(atts[v], back_low, TN)
        grad_att[v] = dot(back_low, w[v, out_rows], NT).astype(BF16)
    vec[0:1] += jnp.sum(grad_norm * unit, axis=0, keepdims=True)
    vec[1:2] += jnp.sum(grad_norm, axis=0, keepdims=True)
    vec[2:3] += jnp.sum(back, axis=0, keepdims=True)
    vec[3:4] += jnp.sum(cot_full, axis=0, keepdims=True)

    @pl.when(step == pl.num_programs(0) - 1)
    def _():
        for v in range(parts):
            acc[v, VEC_AT : VEC_AT + 8] = vec[...]
            acc[v, VEC_AT + 4 : VEC_AT + 5, :UP_ROWS] = bup[v]
            for d in range(ndp):
                cells[d, v] = acc[v, d * piece : (d + 1) * piece].astype(BF16)


def middle_part(weights, att, tok, cot, b_out, gain, shift, b_up, b_down):
    parts, rows, width = att.shape
    ndp = weights.shape[0]
    whole = lambda a: pl.BlockSpec(a.shape, lambda i: (0,) * len(a.shape))
    shape = lambda s, t: jax.ShapeDtypeStruct(s, t)
    tile = pl.BlockSpec((ROWS_MID, D), lambda i: (i, 0))
    heads_tile = pl.BlockSpec((parts, ROWS_MID, width), lambda i: (0, i, 0))
    cells = shape((ndp, parts, UNITS // ndp, D), BF16)
    return pl.pallas_call(
        middle_kernel,
        name="middle_part",
        cost_estimate=work(37),
        grid=(rows // ROWS_MID,),
        in_specs=[ANY, heads_tile, tile, tile] + [whole(a) for a in (b_out, gain, shift, b_up, b_down)],
        out_specs=[tile, tile, heads_tile, whole(cells)],
        out_shape=[shape((rows, D), BF16), shape((rows, D), F32), shape((parts, rows, width), BF16), cells],
        scratch_shapes=[
            pltpu.VMEM((parts, UNITS, D), BF16),
            pltpu.VMEM((parts, UNITS, D), F32),
            pltpu.VMEM((8, D), F32),
            pltpu.VMEM(b_up.shape, F32),
            DMA((ndp * parts,)),
        ],
        compiler_params=limit(60),
    )(weights, att, tok, cot, b_out, gain, shift, b_up, b_down)


def finish_kernel(
    dproj, normed, full, w, grad_mid, gain, cells, grad, vec_sum, d_w, sums,
    part, theirs, sent, crossed, low, back, acc, w_part, w_in, w_z, w_all, vec, vz, vd,
    sib_s, sib_r, cross_s, cross_r, swap_s, swap_r, vz_s, vz_r, vd_s, vd_r,
    ws_s, ws_r, wz_s, wz_r, wg_s, wg_r, wf_s, wf_r,
    u_in, u_all, uz_s, uz_r, ug_s, ug_r, uf_s, uf_r,
):
    me = Place()
    foreign = jnp.logical_not(me.native)
    rows = grad_mid.shape[0]
    piece = rows // PIECES
    width = w.shape[2]
    ndp = vd.shape[0]
    groups, w_rows, _ = w_part.shape
    group = me.d // 2
    around = [(me.d, lax.rem(me.m + k, 4)) for k in range(1, 4)]
    along = [(lax.rem(me.d + k, ndp), me.m) for k in range(1, ndp)]
    greet([me.partner] + around + along)

    order = [2 * (1 - me.hf) + 1 - me.r, 2 * (1 - me.hf) + me.r, 2 * me.hf + 1 - me.r, 2 * me.hf + me.r]

    def to_sib(k, p):
        slot = k % 2
        return remote(part.at[k, p], theirs.at[slot, p], sib_s.at[slot, p], sib_r.at[slot, p], me.sibling)

    def to_cross(p):
        return remote(sent.at[p], crossed.at[p], cross_s.at[p], cross_r.at[p], me.cross)

    def to_partner(p):
        return remote(low.at[p], back.at[p], swap_s.at[p], swap_r.at[p], me.partner)

    def unit_z(j):
        to = lax.rem(me.m + 1 + j, 4)
        return remote(cells.at[to], u_in.at[j], uz_s.at[j], uz_r.at[j], around[j])

    def unit_give(j):
        return remote(
            u_all.at[me.d], u_all.at[me.d], ug_s.at[j], ug_r.at[j], (2 * lax.rem(group + j, groups) + me.c, me.m)
        )

    def unit_forward(j):
        source = 2 * lax.rem(group + groups - j, groups) + me.c
        return remote(u_all.at[source], u_all.at[source], uf_s.at[j], uf_r.at[j], me.sibling)

    def unit_give_in(j):
        source = 2 * lax.rem(group + groups - j, groups) + me.c
        return remote(u_all.at[source], u_all.at[source], ug_s.at[j], ug_r.at[j], (source, me.m))

    def unit_forward_in(j):
        source = 2 * lax.rem(group + groups - j, groups) + 1 - me.c
        return remote(u_all.at[source], u_all.at[source], uf_s.at[j], uf_r.at[j], me.sibling)

    for j in range(3):
        unit_z(j).start()
    acc[...] = jnp.zeros_like(acc)
    vec[...] = jnp.zeros_like(vec)

    def compute(k):
        def one(p, _):
            span = pl.ds(pl.multiple_of(order[k] * rows + p * piece, 16), piece)
            rounded = normed[span, :]
            total = jnp.zeros((piece, D), F32)
            for c in range(3):
                given = dproj[c, span, :]
                total = total + dot(given, w[c], NT)
                acc[c * width : (c + 1) * width, :] += dot(given, rounded, TN)
            part[k, p] = total.astype(BF16)
            unit, _ = normalise(full[span, :].astype(F32))
            vec[0:1] += jnp.sum(total * unit, axis=0, keepdims=True)
            vec[1:2] += jnp.sum(total, axis=0, keepdims=True)

            @pl.when(me.native if k < 2 else foreign)
            def _():
                to_sib(k, p).start()

            return 0

        lax.fori_loop(0, PIECES, one, 0)

    def pass_across(k):
        for p in range(PIECES):
            to_sib(k, p).wait_recv()
            sent[p] = (part[k, p].astype(F32) + theirs[0, p].astype(F32)).astype(BF16)
            to_cross(p).start()

    def conclude(k, p):
        to_sib(k, p).wait_recv()
        to_cross(p).wait_recv()
        total = part[k, p].astype(F32) + theirs[1, p].astype(F32) + crossed[p].astype(F32)
        span = pl.ds(pl.multiple_of(me.q * rows + p * piece, 16), piece)
        unit, scale = normalise(full[span, :].astype(F32))
        scaled = total * gain[...]
        return grad_mid[p * piece : (p + 1) * piece, :] + scale * (
            scaled
            - jnp.mean(scaled, axis=-1, keepdims=True)
            - unit * jnp.mean(scaled * unit, axis=-1, keepdims=True)
        )

    def conclude_foreign(p):
        low[p] = conclude(1, p).astype(BF16)
        to_partner(p).start()

    compute(0)

    @pl.when(foreign)
    def _():
        pass_across(0)

    compute(1)
    compute(2)
    unit_sum = cells[me.m].astype(F32)
    for j in range(3):
        unit_z(j).wait_recv()
        unit_sum = unit_sum + u_in[j].astype(F32)
    u_all[me.d] = unit_sum.astype(BF16)
    for j in range(1, groups):
        unit_give(j).start()
    unit_forward(0).start()

    @pl.when(me.native)
    def _():
        pass_across(2)

    @pl.when(foreign)
    def _():
        conclude_foreign(0)

    compute(3)

    for i in range(groups):
        w_part[i] = acc[i * w_rows : (i + 1) * w_rows, :].astype(BF16)

    def other_group(k):
        return lax.rem(group + k, groups)

    def w_send(k):
        to = other_group(k)
        return remote(w_part.at[to], w_in.at[k], ws_s.at[k], ws_r.at[k], (2 * to + me.c, me.m))

    for k in range(1, groups):
        w_send(k).start()

    vz[me.m] = vec[...]

    def around_copy(k):
        return remote(vz.at[me.m], vz.at[me.m], vz_s.at[k], vz_r.at[k], around[k])

    for k in range(3):
        around_copy(k).start()

    @pl.when(foreign)
    def _():
        for p in range(1, PIECES):
            conclude_foreign(p)

    for k in range(3):
        source = lax.rem(me.m + 3 - k, 4)
        remote(vz.at[source], vz.at[source], vz_s.at[k], vz_r.at[k], around[k]).wait_recv()
    vd[me.d] = vz[0] + vz[1] + vz[2] + vz[3]

    def along_copy(k):
        return remote(vd.at[me.d], vd.at[me.d], vd_s.at[k], vd_r.at[k], along[k])

    for k in range(ndp - 1):
        along_copy(k).start()

    w_sum = w_part[group].astype(F32)
    for k in range(1, groups):
        w_send(k).wait_recv()
        w_sum = w_sum + w_in[k].astype(F32)

    to_z = remote(w_z.at[0], w_z.at[1], wz_s, wz_r, (me.d, lax.rem(me.m + 2, 4)))

    def w_give(k):
        return remote(
            w_all.at[group], w_all.at[group], wg_s.at[k], wg_r.at[k], (2 * other_group(k) + me.c, me.m)
        )

    def w_forward(k):
        source = lax.rem(group + groups - k, groups)
        return remote(w_all.at[source], w_all.at[source], wf_s.at[k], wf_r.at[k], me.sibling)

    @pl.when(foreign)
    def _():
        w_z[0] = w_sum.astype(BF16)
        to_z.start()

    @pl.when(me.native)
    def _():
        to_z.wait_recv()
        w_all[group] = (w_sum + w_z[1].astype(F32)).astype(BF16)
        for k in range(1, groups):
            w_give(k).start()
        w_forward(0).start()
        for p in range(PIECES):
            grad[p * piece : (p + 1) * piece, :] = conclude(3, p)
        for k in range(1, groups):
            source = lax.rem(group + groups - k, groups)
            remote(
                w_all.at[source], w_all.at[source], wg_s.at[k], wg_r.at[k], (2 * source + me.c, me.m)
            ).wait_recv()
            w_forward(k).start()

    for k in range(ndp - 1):
        source = lax.rem(me.d + ndp - 1 - k, ndp)
        remote(vd.at[source], vd.at[source], vd_s.at[k], vd_r.at[k], along[k]).wait_recv()
    total = vd[0]
    for i in range(1, ndp):
        total = total + vd[i]
    vec_sum[...] = total

    @pl.when(foreign)
    def _():
        for k in range(groups):
            source = lax.rem(group + groups - k, groups)
            remote(w_all.at[source], w_all.at[source], wf_s.at[k], wf_r.at[k], me.sibling).wait_recv()

    for i in range(groups):
        d_w[i * w_rows : (i + 1) * w_rows, :] = w_all[i].astype(F32)
    for j in range(1, groups):
        unit_give_in(j).wait_recv()
        unit_forward(j).start()
    for j in range(groups):
        unit_forward_in(j).wait_recv()
    height = sums.shape[0] // ndp
    for i in range(ndp):
        sums[i * height : (i + 1) * height, :] = u_all[i].astype(F32)
    for j in range(groups):
        unit_forward(j).wait_send()
    for j in range(1, groups):
        unit_give(j).wait_send()
    for j in range(3):
        unit_z(j).wait_send()

    @pl.when(foreign)
    def _():
        for p in range(PIECES):
            to_partner(p).wait_recv()
            grad[p * piece : (p + 1) * piece, :] = back[p].astype(F32)
        for p in range(PIECES):
            to_partner(p).wait_send()
            to_sib(2, p).wait_send()
            to_sib(3, p).wait_send()
        to_z.wait_send()

    @pl.when(me.native)
    def _():
        for p in range(PIECES):
            to_sib(0, p).wait_send()
            to_sib(1, p).wait_send()
        for k in range(1, groups):
            w_give(k).wait_send()
        for k in range(groups):
            w_forward(k).wait_send()

    for p in range(PIECES):
        to_cross(p).wait_send()
    for k in range(1, groups):
        w_send(k).wait_send()
    for k in range(3):
        around_copy(k).wait_send()
    for k in range(ndp - 1):
        along_copy(k).wait_send()


def finish(dproj, normed, full, w, grad_mid, gain, cells, ndp):
    rows = grad_mid.shape[0]
    piece = rows // PIECES
    pieces = (PIECES, piece, D)
    groups = ndp // 2
    columns = 3 * w.shape[2]
    cut = (groups, columns // groups, D)
    return pl.pallas_call(
        finish_kernel,
        name="finish",
        cost_estimate=work(60),
        in_specs=[VMEM] * 7,
        out_specs=[VMEM] * 4,
        out_shape=[
            jax.ShapeDtypeStruct((rows, D), F32),
            jax.ShapeDtypeStruct((8, D), F32),
            jax.ShapeDtypeStruct((columns, D), F32),
            jax.ShapeDtypeStruct((UNITS, D), F32),
        ],
        scratch_shapes=[
            pltpu.VMEM((4,) + pieces, BF16),
            pltpu.VMEM((2,) + pieces, BF16),
            pltpu.VMEM(pieces, BF16),
            pltpu.VMEM(pieces, BF16),
            pltpu.VMEM(pieces, BF16),
            pltpu.VMEM(pieces, BF16),
            pltpu.VMEM((columns, D), F32),
            pltpu.VMEM(cut, BF16),
            pltpu.VMEM(cut, BF16),
            pltpu.VMEM((2,) + cut[1:], BF16),
            pltpu.VMEM(cut, BF16),
            pltpu.VMEM((8, D), F32),
            pltpu.VMEM((4, 8, D), F32),
            pltpu.VMEM((ndp, 8, D), F32),
            DMA((2, PIECES)),
            DMA((2, PIECES)),
            DMA((PIECES,)),
            DMA((PIECES,)),
            DMA((PIECES,)),
            DMA((PIECES,)),
            DMA((3,)),
            DMA((3,)),
            DMA((ndp - 1,)),
            DMA((ndp - 1,)),
            DMA((groups,)),
            DMA((groups,)),
            DMA,
            DMA,
            DMA((groups,)),
            DMA((groups,)),
            DMA((groups,)),
            DMA((groups,)),
            pltpu.VMEM((3, UNITS // ndp, D), BF16),
            pltpu.VMEM((ndp, UNITS // ndp, D), BF16),
            DMA((3,)),
            DMA((3,)),
            DMA((groups,)),
            DMA((groups,)),
            DMA((groups,)),
            DMA((groups,)),
        ],
        compiler_params=pltpu.CompilerParams(
            collective_id=4, has_side_effects=True, vmem_limit_bytes=60 << 20
        ),
    )(dproj, normed, full, w, grad_mid, gain, cells)


def swap_pairs(ndp):
    return [
        (d * 4 + m, (d ^ 1) * 4 + (m + 2) % 4) for d in range(ndp) for m in range(4) if d % 2 != m // 2
    ]


def weight_piece(w_out, w_up, w_down, ndp):
    block = jnp.concatenate([w_out, w_down, w_up.T, jnp.zeros((UNITS - w_out.shape[0] - 2 * w_down.shape[0], D), BF16)])
    piece = UNITS // ndp
    return lax.dynamic_slice_in_dim(block, lax.axis_index("dp") * piece, piece, 0)


def sum_over_dp(cells):
    return lax.psum_scatter(cells.reshape(-1, D), "dp", scatter_dimension=0, tiled=True)


def shards(
    tokens,
    scene_ids,
    gain_one,
    shift_one,
    w_qkv,
    w_out,
    b_out,
    gain_two,
    shift_two,
    w_up,
    b_up,
    w_down,
    b_down,
    cotangent,
    ndp,
):
    d, m = lax.axis_index("dp"), lax.axis_index("mp")
    native = d % 2 == m // 2
    line = lambda v: v.reshape(1, D)
    both = ("dp", "mp")
    swap = swap_pairs(ndp)

    full, own_tok, w_mine, scene, all_bup, normed, q, k, v, kt, vt, weights = start(
        tokens,
        w_qkv,
        scene_ids.reshape(-1, LANES),
        b_up.reshape(1, FF // 4),
        line(gain_one),
        line(shift_one),
        weight_piece(w_out, w_up, w_down, ndp),
        ndp,
    )
    w_mine = w_mine.reshape(w_qkv.shape)
    weights = lax.all_gather(weights, "dp", axis=0)
    scene = scene.reshape(-1)
    lo_f, hi_f, idc, idr = scene_ranges(scene, FWD_Q)
    lo_b, hi_b = (lo_f, hi_f) if BWD_K == FWD_Q else scene_ranges(scene, BWD_K)[:2]
    sent_cot, q = lax.optimization_barrier((cotangent, q))
    own_cot = jnp.where(native, cotangent, lax.ppermute(sent_cot, both, swap))
    attended, lse = attention((lo_f, hi_f, idc, idr), q, k, vt)
    att = exchange(attended, False, 2)
    layer_out, grad_mid, grad_att, cells = middle_part(
        weights, att, own_tok, own_cot, line(b_out), line(gain_two), line(shift_two), all_bup, line(b_down)
    )
    grad_heads = exchange(grad_att, True, 3)
    sent_out, grad_heads = lax.optimization_barrier((layer_out, grad_heads))
    layer_out = jnp.where(native, layer_out, lax.ppermute(sent_out, both, swap))
    cells = sum_over_dp(cells)
    dproj = attention_back((lo_b, hi_b, idc, idr), q, k, v, kt, attended, grad_heads, lse)
    cells, dproj = lax.optimization_barrier((cells, dproj))
    tokens_grad, one_sum, d_qkv, sums = finish(
        dproj, normed, full, w_mine, grad_mid, line(gain_one), cells.reshape(4, -1, D), ndp
    )
    g_qkv = jnp.swapaxes(d_qkv.reshape(3, -1, D), 1, 2)
    g_vec = sums[VEC_AT : VEC_AT + 4]
    return (
        layer_out,
        tokens_grad,
        one_sum[0],
        one_sum[1],
        g_qkv,
        sums[:OUT_ROWS],
        g_vec[2],
        g_vec[0],
        g_vec[1],
        sums[OUT_ROWS + UP_ROWS : VEC_AT].T,
        sums[VEC_AT + 4, :UP_ROWS],
        sums[OUT_ROWS : OUT_ROWS + UP_ROWS],
        g_vec[3],
    )


def solution(mesh):
    ndp = mesh.shape["dp"]
    return jax.shard_map(
        functools.partial(shards, ndp=ndp),
        mesh=mesh,
        in_specs=(
            P(("dp", "mp"), None),
            P("dp"),
            P(),
            P(),
            P(None, None, "mp"),
            P("mp", None),
            P(),
            P(),
            P(),
            P(None, "mp"),
            P("mp"),
            P("mp", None),
            P(),
            P(("dp", "mp"), None),
        ),
        out_specs=(
            P(("dp", "mp"), None),
            P(("dp", "mp"), None),
            P(),
            P(),
            P(None, None, "mp"),
            P("mp", None),
            P(),
            P(),
            P(),
            P(None, "mp"),
            P("mp"),
            P("mp", None),
            P(),
        ),
        check_vma=False,
    )
```

time: 612 us -> 409 us (0.67)
  blocking collectives: 111 us -> 0 us
  Pallas kernels: 387 us -> 351 us
  local copies, waits for them, and re-layouts: 56.1 us -> 30.5 us
  starting transfers between devices: 17.3 us -> 5.84 us
  other arithmetic: 15.7 us -> 4.77 us
    unnamed x2 -> x0, blocking collectives: 101 us -> none
    pallas_call x5 -> x3, Pallas kernels: 247 us -> 197 us  [the longest x1 89.5 us: finish(): pl.pallas_call(finish_kernel, name='finish', cost_estimate=work(60), in_s...]
    pallas_call x1, Pallas kernels: 56.9 us -> 67.2 us  [attention_back(): pl.pallas_call(functools.partial(attention_back_kernel, heads, total), na...]
    all_gather x1 -> x0, blocking collectives: 9.8 us -> none  [shards(): all_bup = lax.all_gather(b_up, 'mp', axis=0).reshape(4, 1, FF // 4)]
    unnamed x70 -> x33, local copies, waits for them, and re-layouts: 19 us -> 9.81 us
    reshape x5 -> x1, local copies, waits for them, and re-layouts: 8.9 us -> 0.56 us  [shards(): b_up.reshape(1, FF // 4)]
    ppermute x4 -> x2, starting transfers between devices: 14 us -> 5.76 us  [the longest x1 3.33 us: shards(): layer_out = jnp.where(native, layer_out, lax.ppermute(sent_out, both, swap))]
  transfers between devices with their start and end apart: 9 -> 4, of which waited for: 1 -> 0; matrix products, arithmetic and copies ran while one was open for 22% -> 3% of each run, Pallas kernels for 42% -> 38%
where the time goes in v2:
time: 409 us; the launch traced here: 406 us
  Pallas kernels  351 us (86%)
  local copies, waits for them, and re-layouts  30.5 us (7%)
  between operations  14.3 us (3%)
  starting transfers between devices  5.84 us (1%)
  other arithmetic  4.77 us (1%)
    pallas_call x1, Pallas kernels, finish(): pl.pallas_call(finish_kernel, name='finish', cost_estimate=work(60), in_s...  89.5 us
    pallas_call x1, Pallas kernels, start(): pl.pallas_call(functools.partial(start_kernel, heads), name='start', cost...  70.2 us
    pallas_call x1, Pallas kernels, attention_back(): pl.pallas_call(functools.partial(attention_back_kernel, heads, total), na...  67.2 us
    pallas_call x2, Pallas kernels, exchange(): pl.pallas_call(functools.partial(exchange_kernel, to_rows), name='exchang...  44.2 us
    pallas_call x1, Pallas kernels, attention(): pl.pallas_call(functools.partial(attention_kernel, heads, total), name='a...  42.7 us
    pallas_call x1, Pallas kernels, middle_part(): pl.pallas_call(middle_kernel, name='middle_part', cost_estimate=work(37),...  37 us
    unnamed x33, local copies, waits for them, and re-layouts  9.81 us
  transfers between devices with their start and end apart: 4, of which 0 were waited for; matrix products, arithmetic and copies ran while one was open for 3% of the time, Pallas kernels for 38%

profile of v2, /device:TPU:1, one launch (start us, length us, event | category | flops | bytes accessed | tf_op | source)
XLA Modules:
  0.0 406.2 jit_solution(1061733097275980918)
XLA Ops:
  7.3 1.4 copy.44
  8.7 1.3 reshape.83.gain
  10.0 1.4 copy.43
  13.5 70.2 %start.1 = (bf16[3456,768]{1,0:T(8,128)(2,1)}, bf16[864,768]{1,0:T(8,128)(2,1)}, bf16[3,4,192,192]{3,2,1,0:T(8,128)(2,1)}, s32[27,128]{1,0:T(8,128)}, f32[4,1,38...) custom-call(bf16[864,768]{1,0:T(8,128)(2,1)} %tok.1, ...), custom_call_target="tpu_custom_call" | custom-call | flops 49999998976 | bytes 150000000 | tf_op jit(solution)/shard_map/start/pallas_call | solution.py:355
  83.8 2.4 collective-permute-start
  88.6 2.9 broadcast_in_dim.37.idc
  95.2 42.7 %attention.1 = (bf16[3456,192]{1,0:T(8,128)(2,1)}, f32[3,3456]{1,0:T(4,128)}) custom-call(s32[9]{0:T(128)} %get-tuple-element.132.lo, s32[9]{0:T(128)} %get-tuple-element.131.hi, s32[3840,1]{1,0:T(8,128)} %broadcast_in_dim.37.idc, s32[1,3840]{1,0:T(1,128)} %broadcast_in_dim.36.idr, bf16[3,3840,128]{2,1,0:T(8,128)(2,1)} %get-tuple-element.44.q, ...), custom_call_target="tpu_custom_call" | custom-call | flops 31000000512 | bytes 93000000 | tf_op jit(solution)/shard_map/attention/pallas_call | solution.py:501
  137.9 21.8 %exchange_heads.1.att = bf16[4,864,192]{2,1,0:T(8,128)(2,1)} custom-call(bf16[3456,192]{1,0:T(8,128)(2,1)} %get-tuple-element.47.src.out), custom_call_target="tpu_custom_call" | custom-call | flops 20000000000 | bytes 60000000 | tf_op jit(solution)/shard_map/exchange_heads/pallas_call | solution.py:441
  159.7 1.2 broadcast_select_fusion.1.cot
  160.9 37.0 %middle_part.1 = (bf16[864,768]{1,0:T(8,128)(2,1)}, f32[864,768]{1,0:T(8,128)}, bf16[4,864,192]{2,1,0:T(8,128)(2,1)}, bf16[8,4,128,768]{3,2,1,0:T(8,128)(2,1)}) custom-call(bf16[8,4,128,768]{3,2,1,0:T(8,128)(2,1)} %bitcast.24, bf16[4,864,192]{2,1,0:T(8,128)(2,1)} %exchange_heads.1.att, bf16[864,768]{1,0:T(8,128)(2,1)} %get-tuple-element.48.tok, ...), custom_call_target="tpu_custom_call" | custom-call | flops 36999999488 | bytes 111000000 | tf_op jit(solution)/shard_map/middle_part/pallas_call | solution.py:717
  198.8 1.8 copy.46
  200.5 22.4 %exchange_rows.1.grad = bf16[3456,192]{1,0:T(8,128)(2,1)} custom-call(bf16[4,864,192]{2,1,0:T(8,128)(2,1)} %get-tuple-element.52.src), custom_call_target="tpu_custom_call" | custom-call | flops 20000000000 | bytes 60000000 | tf_op jit(solution)/shard_map/exchange_rows/pallas_call | solution.py:441
  222.9 3.3 collective-permute-start.1
  226.3 67.2 %attention_back.1.dproj = bf16[3,3456,192]{2,1,0:T(8,128)(2,1)} custom-call(s32[9]{0:T(128)} %get-tuple-element.132.lo, s32[9]{0:T(128)} %get-tuple-element.131.hi, s32[3840,1]{1,0:T(8,128)} %broadcast_in_dim.37.idc, s32[1,3840]{1,0:T(1,128)} %broadcast_in_dim.36.idr, bf16[3,3840,128]{2,1,0:T(8,128)(2,1)} %get-tuple-element.44.q, ...), custom_call_target="tpu_custom_call" | custom-call | flops 51000000512 | bytes 153000000 | tf_op jit(solution)/shard_map/attention_back/pallas_call | solution.py:601
  293.5 1.2 broadcast_select_fusion
  294.7 89.5 %finish.1 = (f32[864,768]{1,0:T(8,128)}, f32[8,768]{1,0:T(8,128)}, f32[576,768]{1,0:T(8,128)}, f32[1024,768]{1,0:T(8,128)}) custom-call(bf16[3,3456,192]{2,1,0:T(8,128)(2,1)} %attention_back.1.dproj, bf16[3456,768]{1,0:T(8,128)(2,1)} %get-tuple-element.60.normed, bf16[3456,768]{1,0:T(8,128)(2,1)} %get-tuple-element.61.full, bf16[3,768,192]{2,1,0:T(8,128)(2,1)} %bitcast.27, ...), custom_call_target="tpu_custom_call" | custom-call | flops 60000002048 | bytes 180000000 | tf_op jit(solution)/shard_map/finish/pallas_call | solution.py:1008
  384.2 2.8 fusion.5
  387.0 1.9 slice.45
  388.9 1.5 slice_reduce_fusion
  390.5 1.3 slice_reduce_fusion.6
  391.8 1.4 copy.48
  393.1 1.4 slice_reduce_fusion.4
  394.6 3.6 copy.51
  398.1 1.2 copy.52
  (55 shorter events, 9.1 us)
Async XLA Ops:
  7.2 2.8 copy-start.3
  7.2 153.7 %all-gather.3.cloned.1.call-start = ((), (), s32[]{:S(2)}) async-start(), calls=%async_computation.2 | async-start | bytes 7077888 | tf_op jit(solution)/shard_map/all_gather | solution.py:1118
  7.2 4.1 %copy-start.8 = (f32[768]{0:T(1024)S(1)}, f32[768]{0:T(1024)}, u32[]{:S(2)}) copy-start(f32[768]{0:T(1024)} %param.17) | copy-start | bytes 9220
  7.3 4.7 %copy-start.13 = (f32[384]{0:T(512)S(1)}, f32[384]{0:T(512)}, u32[]{:S(2)}) copy-start(f32[384]{0:T(512)} %param.24) | copy-start | bytes 4612
  7.3 5.4 %copy-start.4 = (bf16[384,768]{1,0:T(8,128)(2,1)S(1)}, bf16[384,768]{1,0:T(8,128)(2,1)}, u32[]{:S(2)}) copy-start(bf16[384,768]{1,0:T(8,128)(2,1)} %param.25) | copy-start | bytes 1769476
  7.3 5.3 %copy-start.5 = (bf16[192,768]{1,0:T(8,128)(2,1)S(1)}, bf16[192,768]{1,0:T(8,128)(2,1)}, u32[]{:S(2)}) copy-start(bf16[192,768]{1,0:T(8,128)(2,1)} %param.19) | copy-start | bytes 884740
  13.5 70.3 %copy-start.1 = (bf16[864,768]{1,0:T(8,128)(2,1)S(1)}, bf16[864,768]{1,0:T(8,128)(2,1)}, u32[]{:S(2)}) copy-start(bf16[864,768]{1,0:T(8,128)(2,1)} %param.27) | copy-start | bytes 3981316
  83.7 8.4 %copy-start.9 = (f32[768]{0:T(1024)S(1)}, f32[768]{0:T(1024)}, u32[]{:S(2)}) copy-start(f32[768]{0:T(1024)} %param.20) | copy-start | bytes 9220
  83.7 9.0 %copy-start.10 = (f32[768]{0:T(1024)S(1)}, f32[768]{0:T(1024)}, u32[]{:S(2)}) copy-start(f32[768]{0:T(1024)} %param.21) | copy-start | bytes 9220
  83.7 9.6 %copy-start.11 = (f32[768]{0:T(1024)S(1)}, f32[768]{0:T(1024)}, u32[]{:S(2)}) copy-start(f32[768]{0:T(1024)} %param.22) | copy-start | bytes 9220
  83.7 10.1 %copy-start.12 = (f32[768]{0:T(1024)S(1)}, f32[768]{0:T(1024)}, u32[]{:S(2)}) copy-start(f32[768]{0:T(1024)} %param.26) | copy-start | bytes 9220
  83.7 10.7 %copy-start.6 = (s32[27,128]{1,0:T(8,128)S(1)}, s32[27,128]{1,0:T(8,128)}, u32[]{:S(2)}) copy-start(s32[27,128]{1,0:T(8,128)} %get-tuple-element.42) | copy-start | bytes 41476
  83.8 211.0 %reduce-scatter.2.cloned.1.call-start = ((), (), s32[]{:S(2)}) async-start(), calls=%async_computation.1 | async-start | bytes 7077888 | tf_op jit(solution)/shard_map/reduce_scatter | solution.py:1081
  83.8 75.9 %collective-permute-start = (bf16[864,768]{1,0:T(8,128)(2,1)S(1)}, bf16[864,768]{1,0:T(8,128)(2,1)S(1)}, u32[]{:S(2)}, u32[]{:S(2)}) collective-permute-start(bf16[864,768]{1,0:T(8,128)(2,1)S(1)} %copy-done.1), channel_id=1, source_target_pairs={{2,4},{3,5},{4,2},{5,3},{10,12},{11,13},{12,10},{13,11},{18,20},{1... | collective-permute-start | bytes 3981320 | tf_op jit(solution)/shard_map/ppermute | solution.py:1123
  197.9 0.8 copy-start.7
  200.5 22.4 %copy-start.2 = (bf16[864,768]{1,0:T(8,128)(2,1)S(1)}, bf16[864,768]{1,0:T(8,128)(2,1)}, u32[]{:S(2)}) copy-start(bf16[864,768]{1,0:T(8,128)(2,1)} %get-tuple-element.53) | copy-start | bytes 3981316
  222.9 70.6 %collective-permute-start.1 = (bf16[864,768]{1,0:T(8,128)(2,1)S(1)}, bf16[864,768]{1,0:T(8,128)(2,1)S(1)}, u32[]{:S(2)}, u32[]{:S(2)}) collective-permute-start(bf16[864,768]{1,0:T(8,128)(2,1)S(1)} %copy-done.2), channel_id=1, source_target_pairs={{2,4},{3,5},{4,2},{5,3},{10,12},{11,13},{12,10},{13,11},{18,20},{1... | collective-permute-start | bytes 3981320 | tf_op jit(solution)/shard_map/ppermute | solution.py:1131
  394.6 3.6 copy-start
Sparse Core Ops, SparseCore 0:
  83.9 47.1 all-gather.2
  198.1 65.0 reduce-scatter.1

commit v3 on v2

--- a/solution.py
+++ b/solution.py
@@ -394,110 +394,60 @@
     )(tokens, w_qkv, scene_ids, b_up, gain, shift, mine)
 
 
-def exchange_kernel(to_rows, src, dst, send, recv, loc):
-    me = Place()
-    others = []
-    for k in range(1, 4):
-        quarter = lax.rem(me.q + k, 4)
-        others.append(me.member(quarter))
-    greet(others)
-    rows = (dst.shape[0] if to_rows else src.shape[0]) // 4
-
-    def block(ref, quarter, by_rows):
-        if by_rows:
-            return ref.at[pl.ds(pl.multiple_of(quarter * rows, 16), rows)]
-        return ref.at[quarter]
-
-    def copy(k):
-        quarter = lax.rem(me.q + k, 4)
-        return remote(
-            block(src, quarter, not to_rows), block(dst, me.q, to_rows), send.at[k], recv.at[k], others[k - 1]
-        )
-
-    def arrival(k):
-        quarter = lax.rem(me.q + 4 - k, 4)
-        return remote(
-            block(src, quarter, not to_rows), block(dst, quarter, to_rows), send.at[k], recv.at[k], others[3 - k]
-        )
-
-    for k in (2, 1, 3):
-        copy(k).start()
-    own = pltpu.make_async_copy(block(src, me.q, not to_rows), block(dst, me.q, to_rows), loc)
-    own.start()
-    for k in (1, 2, 3):
-        arrival(k).wait_recv()
-    for k in (1, 2, 3):
-        copy(k).wait_send()
-    own.wait()
-
-
-def exchange(values, to_rows, number):
-    if to_rows:
-        _, rows, width = values.shape
-        shape = (4 * rows, width)
-    else:
-        rows, width = values.shape
-        shape = (4, rows // 4, width)
-    return pl.pallas_call(
-        functools.partial(exchange_kernel, to_rows),
-        name="exchange_rows" if to_rows else "exchange_heads",
-        in_specs=[ANY],
-        out_specs=ANY,
-        out_shape=jax.ShapeDtypeStruct(shape, values.dtype),
-        scratch_shapes=[DMA((4,)), DMA((4,)), DMA],
-        cost_estimate=work(20),
-        compiler_params=pltpu.CompilerParams(collective_id=number, has_side_effects=True),
-    )(values)
-
-
-FWD_Q, FWD_K = 384, 512
-BWD_Q, BWD_K = 384, 384
+BLOCK = 256
+
+
+def blocks(total):
+    return -(-total // BLOCK)
 
 
 def attention_kernel(heads, total, lo, hi, idc, idr, q, k, vt, out, lse):
-    step = FWD_K // LANES
-
     def one_block(i, _):
-        r0 = pl.multiple_of(i * FWD_Q, LANES)
-        qs = [q[h, pl.ds(r0, FWD_Q), :] for h in range(heads)]
-        mine = idr[:, pl.ds(r0, FWD_Q)]
-
-        def keys(at, carry):
-            c0 = pl.multiple_of(at * LANES, LANES)
-            allowed = idc[pl.ds(c0, FWD_K), :] == mine
+        r0 = pl.multiple_of(i * BLOCK, LANES)
+        qs = [q[h, pl.ds(r0, BLOCK), :] for h in range(heads)]
+        mine = idr[:, pl.ds(r0, BLOCK)]
+
+        def keys(size, at, carry):
+            cols = pl.ds(pl.multiple_of(at * LANES, LANES), size)
+            allowed = idc[cols, :] == mine
+            scores = [jnp.where(allowed, dot(k[h, cols, :], qs[h], NT), MASKED) for h in range(heads)]
             new = []
             for h in range(heads):
                 top, acc = carry[h]
-                s = jnp.where(allowed, dot(k[h, pl.ds(c0, FWD_K), :], qs[h], NT), MASKED)
-                above = jnp.maximum(top, jnp.max(s, axis=0, keepdims=True))
-                p = jnp.exp(s - above).astype(BF16)
-                acc = acc * jnp.exp(top - above) + dot(vt[h, :, pl.ds(c0, FWD_K)], p)
+                above = jnp.maximum(top, jnp.max(scores[h], axis=0, keepdims=True))
+                p = jnp.exp(scores[h] - above).astype(BF16)
+                acc = acc * jnp.exp(top - above) + dot(vt[h, :, cols], p)
                 new.append((above, acc))
             return tuple(new)
 
-        start = tuple(
-            (jnp.full((1, FWD_Q), MASKED, F32), jnp.zeros((vt.shape[1], FWD_Q), F32)) for _ in range(heads)
-        )
+        done = tuple((jnp.full((1, BLOCK), MASKED, F32), jnp.zeros((vt.shape[1], BLOCK), F32)) for _ in range(heads))
         first = lo[i]
-        count = (hi[i] - first + step - 1) // step
-        done = lax.fori_loop(0, count, lambda n, c: keys(first + n * step, c), start)
+        done = in_steps(first, hi[i], keys, done)
         valid = jnp.where(mine >= 0, 1.0, 0.0)
         mixed = []
         for h in range(heads):
             top, acc = done[h]
             row_total = acc[HEAD : HEAD + 1]
             mixed.append(acc[:HEAD] * (valid / row_total))
-            lse[pl.ds(h, 1), pl.ds(r0, FWD_Q)] = top + jnp.log(row_total)
-        out[pl.ds(r0, FWD_Q), :] = jnp.concatenate(mixed, axis=0).T.astype(BF16)
+            lse[pl.ds(h, 1), pl.ds(r0, BLOCK)] = top + jnp.log(row_total)
+        out[pl.ds(r0, BLOCK), :] = jnp.concatenate(mixed, axis=0).T.astype(BF16)
         return 0
 
-    lax.fori_loop(0, total // FWD_Q, one_block, 0)
+    lax.fori_loop(0, blocks(total), one_block, 0)
+
+
+def in_steps(first, last, body, carry):
+    wide, narrow = 2 * BLOCK // LANES, BLOCK // LANES
+    count = (last - first + narrow - 1) // narrow
+    carry = lax.fori_loop(0, count // 2, lambda n, c: body(2 * BLOCK, first + n * wide, c), carry)
+    return lax.fori_loop(0, count % 2, lambda n, c: body(BLOCK, first + (count - 1) * narrow, c), carry)
 
 
 def attention(ids, q, k, vt):
     lo, hi, idc, idr = ids
     heads, wide, _ = q.shape
     total = wide - PAD
+    rows = blocks(total) * BLOCK
     return pl.pallas_call(
         functools.partial(attention_kernel, heads, total),
         name="attention",
@@ -505,85 +455,71 @@
         in_specs=[SMEM, SMEM] + [VMEM] * 5,
         out_specs=[VMEM, VMEM],
         out_shape=[
-            jax.ShapeDtypeStruct((total, heads * HEAD), BF16),
-            jax.ShapeDtypeStruct((heads, total), F32),
+            jax.ShapeDtypeStruct((rows, heads * HEAD), BF16),
+            jax.ShapeDtypeStruct((heads, rows), F32),
         ],
         compiler_params=limit(56),
     )(lo, hi, idc, idr, q, k, vt)
 
 
-def thirds(x):
-    a = x.astype(BF16).astype(F32)
-    b = (x - a).astype(BF16).astype(F32)
-    return a, b, x - a - b
-
-
-def attention_back_kernel(
-    heads, total, lo, hi, idc, idr, q, k, v, kt, out, grad, lse, dproj, qe, ge, dq
-):
+def attention_back_kernel(heads, total, lo, hi, idc, idr, q, k, v, kt, out, grad, lse, dproj, g, delta, dq):
     wide = q.shape[1]
-    step = BWD_Q // LANES
-    lane = lax.broadcasted_iota(jnp.int32, (PAD, LANES), 1)
-
-    def extend(values, tail):
-        a, b, c = thirds(tail)
-        return jnp.where(
-            lane == HEAD, a, jnp.where(lane == HEAD + 1, b, jnp.where(lane == HEAD + 2, c, values))
-        ).astype(BF16)
+    width = heads * HEAD
+    head_of = lax.broadcasted_iota(jnp.int32, (8, width), 1) // HEAD
+    pick = jnp.where(head_of == lax.broadcasted_iota(jnp.int32, (8, width), 0), 1.0, 0.0).astype(BF16)
+    none = jnp.zeros((PAD, LANES - HEAD), BF16)
 
     def prepare(i, _):
         rows = pl.ds(pl.multiple_of(i * PAD, LANES), PAD)
-        valid = jnp.where(idc[rows, :] >= 0, 1.0, 0.0)
-        grads = grad[rows, :].astype(F32) * valid
+        grads = jnp.where(idc[rows, :] >= 0, grad[rows, :].astype(F32), 0.0)
         inner = grads * out[rows, :].astype(F32)
+        high = inner.astype(BF16)
+        rest = (inner - high.astype(F32)).astype(BF16)
+        delta[:, rows] = dot(pick, high, NT) + dot(pick, rest, NT)
+        grads = grads.astype(BF16)
         for h in range(heads):
-            cols = slice(h * HEAD, (h + 1) * HEAD)
-            g = jnp.concatenate([grads[:, cols], jnp.zeros((PAD, LANES - HEAD), F32)], axis=1)
-            ge[h, rows, :] = extend(g, -jnp.sum(inner[:, cols], axis=1, keepdims=True))
-            qe[h, rows, :] = extend(q[h, rows, :].astype(F32), -lse[rows, h : h + 1])
+            g[h, rows, :] = jnp.concatenate([grads[:, h * HEAD : (h + 1) * HEAD], none], axis=1)
             dq[h, :, rows] = jnp.zeros((HEAD, PAD), F32)
         return 0
 
     lax.fori_loop(0, total // PAD, prepare, 0)
+    tail = wide - total
+    delta[:, total:] = jnp.zeros((8, tail), F32)
     for h in range(heads):
-        qe[h, total:, :] = jnp.zeros((wide - total, LANES), BF16)
-        ge[h, total:, :] = jnp.zeros((wide - total, LANES), BF16)
-        dq[h, :, total:] = jnp.zeros((HEAD, wide - total), F32)
+        g[h, total:, :] = jnp.zeros((tail, LANES), BF16)
+        dq[h, :, total:] = jnp.zeros((HEAD, tail), F32)
 
     def one_block(i, _):
-        c0 = pl.multiple_of(i * BWD_K, LANES)
-        cols = pl.ds(c0, BWD_K)
+        c0 = pl.multiple_of(i * BLOCK, LANES)
+        cols = pl.ds(c0, BLOCK)
         mine = idc[cols, :]
 
-        def queries(at, carry):
-            r0 = pl.multiple_of(at * LANES, LANES)
-            rows = pl.ds(r0, BWD_Q)
+        def queries(size, at, carry):
+            rows = pl.ds(pl.multiple_of(at * LANES, LANES), size)
             allowed = mine == idr[:, rows]
+            both = [
+                (dot(k[h, cols, :], q[h, rows, :], NT), dot(v[h, cols, :], g[h, rows, :], NT)) for h in range(heads)
+            ]
             new = []
             for h in range(heads):
                 dk, dv = carry[h]
-                qh = qe[h, rows, :]
-                gh = ge[h, rows, :]
-                p = jnp.where(allowed, jnp.exp(dot(k[h, cols, :], qh, NT)), 0.0)
-                ds = (p * dot(v[h, cols, :], gh, NT)).astype(BF16)
-                dv = dv + dot(p.astype(BF16), gh)
-                dk = dk + dot(ds, qh)
+                s, dp = both[h]
+                p = jnp.where(allowed, jnp.exp(s - lse[h : h + 1, rows]), 0.0)
+                ds = (p * (dp - delta[h : h + 1, rows])).astype(BF16)
+                dv = dv + dot(p.astype(BF16), g[h, rows, :])
+                dk = dk + dot(ds, q[h, rows, :])
                 dq[h, :, rows] += dot(kt[h, :, cols], ds)
                 new.append((dk, dv))
             return tuple(new)
 
-        zero = jnp.zeros((BWD_K, LANES), F32)
-        first = lo[i]
-        count = (hi[i] - first + step - 1) // step
-        done = lax.fori_loop(
-            0, count, lambda n, c: queries(first + n * step, c), tuple((zero, zero) for _ in range(heads))
-        )
+        zero = jnp.zeros((BLOCK, LANES), F32)
+        done = in_steps(lo[i], hi[i], queries, tuple((zero, zero) for _ in range(heads)))
         for part in range(2):
             joined = jnp.concatenate([done[h][part][:, :HEAD] for h in range(heads)], axis=1)
             dproj[part + 1, cols, :] = joined.astype(BF16)
         return 0
 
-    lax.fori_loop(0, total // BWD_K, one_block, 0)
+    lax.fori_loop(0, blocks(total), one_block, 0)
 
     def finish(i, _):
         rows = pl.ds(pl.multiple_of(i * PAD, LANES), PAD)
@@ -598,36 +534,38 @@
     lo, hi, idc, idr = ids
     heads, wide, _ = q.shape
     total = wide - PAD
+    lse = jnp.pad(lse, ((0, 0), (0, wide - lse.shape[1])))
     return pl.pallas_call(
         functools.partial(attention_back_kernel, heads, total),
         name="attention_back",
         cost_estimate=work(51),
         in_specs=[SMEM, SMEM] + [VMEM] * 9,
         out_specs=VMEM,
-        out_shape=jax.ShapeDtypeStruct((3, total, heads * HEAD), BF16),
+        out_shape=jax.ShapeDtypeStruct((3, blocks(total) * BLOCK, heads * HEAD), BF16),
         scratch_shapes=[
             pltpu.VMEM((heads, wide, LANES), BF16),
-            pltpu.VMEM((heads, wide, LANES), BF16),
+            pltpu.VMEM((8, wide), F32),
             pltpu.VMEM((heads, HEAD, wide), F32),
         ],
         compiler_params=limit(60),
-    )(lo, hi, idc, idr, q, k, v, kt, out, grad, lse.T)
-
-
-def scene_ranges(scene, block):
+    )(lo, hi, idc, idr, q, k, v, kt, out, grad, lse)
+
+
+def scene_ranges(scene):
     total = scene.shape[0]
     place = jnp.arange(total, dtype=jnp.int32)
     ids = jnp.where(scene >= 0, scene, -1 - place)
     before = jnp.sum(
         ((scene[None, :] >= 0) & (scene[None, :] < jnp.arange(6, dtype=jnp.int32)[:, None])).astype(jnp.int32), axis=1
     )
-    first, last = scene[0::block], scene[block - 1 :: block]
-    start = jnp.arange(total // block, dtype=jnp.int32) * block
+    whole = jnp.pad(scene, (0, blocks(total) * BLOCK - total), constant_values=-1)
+    first, last = whole[0::BLOCK], whole[BLOCK - 1 :: BLOCK]
+    start = jnp.arange(blocks(total), dtype=jnp.int32) * BLOCK
     pick = lambda number: jnp.sum(
         jnp.where(number[:, None] == jnp.arange(6, dtype=jnp.int32)[None, :], before[None, :], 0), axis=1
     )
     lo = jnp.where(first >= 0, pick(first), start) // LANES
-    hi = (jnp.where(last >= 0, pick(last + 1), start + block) + LANES - 1) // LANES
+    hi = (jnp.where(last >= 0, pick(last + 1), start + BLOCK) + LANES - 1) // LANES
     padded = jnp.pad(ids, (0, PAD), constant_values=-(1 << 20))
     return lo, hi, padded[:, None], padded[None, :]
 
@@ -636,101 +574,178 @@
 
 
 def middle_kernel(
-    weights, att, tok, cot, b_out, gain, shift, b_up, b_down,
-    layer_out, grad_mid, grad_att, cells, w, acc, vec, bup, sems,
+    attended, tok, cot, weights, b_out, gain, shift, b_up, b_down,
+    layer_out, grad_mid, grad_heads, cells,
+    att, grad_att, w, acc, vec, bup, units, att_s, att_r, own_s, grad_s, grad_r, back_s, unit_s, cell_s,
 ):
-    step = pl.program_id(0)
-    ndp, parts, piece, _ = cells.shape
+    me = Place()
+    ndp, parts, piece, _ = weights.shape
+    rows = tok.shape[0]
+    tiles = rows // ROWS_MID
     width = att.shape[2]
-
-    @pl.when(step == 0)
-    def _():
-        def load(i):
-            rows = pl.ds(i // parts * piece, piece)
-            return pltpu.make_async_copy(weights.at[i // parts, i % parts], w.at[i % parts, rows], sems.at[i])
-
-        for i in range(ndp * parts):
-            load(i).start()
-        for ref in (acc, vec, bup):
-            ref[...] = jnp.zeros_like(ref)
-        for i in range(ndp * parts):
-            load(i).wait()
+    others = [lax.rem(me.q + k, 4) for k in range(1, 4)]
+    greet([me.member(quarter) for quarter in others])
+
+    def tile(t, quarter=0):
+        return pl.ds(pl.multiple_of(quarter * rows + t * ROWS_MID, 16), ROWS_MID)
+
+    def att_to(k, t):
+        return remote(
+            attended.at[tile(t, others[k])], att.at[me.q, tile(t)], att_s.at[k, t], att_r.at[k, t], me.member(others[k])
+        )
+
+    def att_from(k, t):
+        source = others[2 - k]
+        return remote(
+            attended.at[tile(t)], att.at[source, tile(t)], att_s.at[k, t], att_r.at[k, t], me.member(source)
+        )
+
+    def att_own(t):
+        return pltpu.make_async_copy(attended.at[tile(t, me.q)], att.at[me.q, tile(t)], own_s.at[t])
+
+    def grad_to(k, t):
+        return remote(
+            grad_att.at[others[k], tile(t)], grad_heads.at[tile(t, me.q)], grad_s.at[k, t], grad_r.at[k, t], me.member(others[k])
+        )
+
+    def grad_from(k, t):
+        source = others[2 - k]
+        return remote(
+            grad_att.at[source, tile(t)], grad_heads.at[tile(t, source)], grad_s.at[k, t], grad_r.at[k, t], me.member(source)
+        )
+
+    def grad_own(t):
+        return pltpu.make_async_copy(grad_att.at[me.q, tile(t)], grad_heads.at[tile(t, me.q)], back_s.at[t])
+
+    for t in range(tiles):
+        for k in (1, 0, 2):
+            att_to(k, t).start()
+        att_own(t).start()
+
+    def load(i):
+        at = pl.ds(i // parts * piece, piece)
+        return pltpu.make_async_copy(weights.at[i // parts, i % parts], w.at[i % parts, at], unit_s.at[i])
+
+    for i in range(ndp * parts):
+        load(i).start()
+    for ref in (acc, vec, bup):
+        ref[...] = jnp.zeros_like(ref)
+    for i in range(ndp * parts):
+        load(i).wait()
 
     out_rows = slice(0, OUT_ROWS)
     down_rows = slice(OUT_ROWS, OUT_ROWS + UP_ROWS)
     up_rows = slice(OUT_ROWS + UP_ROWS, VEC_AT)
-    atts = [att[v] for v in range(parts)]
-    middle = tok[...].astype(F32) + b_out[...]
+
+    def one_tile(t, _):
+        here = tile(t)
+        att_own(t).wait()
+        for k in range(3):
+            att_from(k, t).wait_recv()
+        atts = [att[v, here, :] for v in range(parts)]
+        middle = tok[here, :].astype(F32) + b_out[...]
+        for v in range(parts):
+            middle = middle + dot(atts[v], w[v, out_rows])
+        unit, scale = normalise(middle)
+        low = (unit * gain[...] + shift[...]).astype(BF16)
+        cot_low = cot[here, :]
+        cot_full = cot_low.astype(F32)
+        out = middle + b_down[...]
+        grad_norm = jnp.zeros_like(middle)
+        for v in range(parts):
+            hidden = dot(low, w[v, up_rows], NT) + b_up[v]
+            below = 0.5 * (1.0 + lax.erf(hidden * 0.5**0.5))
+            density = jnp.exp(-0.5 * hidden * hidden) * 0.3989422804014327
+            active = (hidden * below).astype(BF16)
+            out = out + dot(active, w[v, down_rows])
+            grad_hidden = (dot(cot_low, w[v, down_rows], NT) * (below + hidden * density)).astype(BF16)
+            grad_norm = grad_norm + dot(grad_hidden, w[v, up_rows])
+            acc[v, down_rows] += dot(active, cot_low, TN)
+            acc[v, up_rows] += dot(grad_hidden, low, TN)
+            bup[v] += jnp.sum(grad_hidden.astype(F32), axis=0, keepdims=True)
+        layer_out[here, :] = out.astype(BF16)
+        scaled = grad_norm * gain[...]
+        back = cot_full + scale * (
+            scaled
+            - jnp.mean(scaled, axis=-1, keepdims=True)
+            - unit * jnp.mean(scaled * unit, axis=-1, keepdims=True)
+        )
+        grad_mid[here, :] = back
+        back_low = back.astype(BF16)
+        for v in range(parts):
+            grad_att[v, here, :] = dot(back_low, w[v, out_rows], NT).astype(BF16)
+        for k in (1, 0, 2):
+            grad_to(k, t).start()
+        grad_own(t).start()
+        for v in range(parts):
+            acc[v, out_rows] += dot(atts[v], back_low, TN)
+        vec[0:1] += jnp.sum(grad_norm * unit, axis=0, keepdims=True)
+        vec[1:2] += jnp.sum(grad_norm, axis=0, keepdims=True)
+        vec[2:3] += jnp.sum(back, axis=0, keepdims=True)
+        vec[3:4] += jnp.sum(cot_full, axis=0, keepdims=True)
+        return 0
+
+    lax.fori_loop(0, tiles, one_tile, 0)
+
+    def give(d):
+        return pltpu.make_async_copy(units.at[d], cells.at[d], cell_s.at[d])
+
     for v in range(parts):
-        middle = middle + dot(atts[v], w[v, out_rows])
-    unit, scale = normalise(middle)
-    low = (unit * gain[...] + shift[...]).astype(BF16)
-    cot_low = cot[...]
-    cot_full = cot_low.astype(F32)
-    out = middle + b_down[...]
-    grad_norm = jnp.zeros_like(middle)
-    for v in range(parts):
-        hidden = dot(low, w[v, up_rows], NT) + b_up[v]
-        below = 0.5 * (1.0 + lax.erf(hidden * 0.5**0.5))
-        density = jnp.exp(-0.5 * hidden * hidden) * 0.3989422804014327
-        active = (hidden * below).astype(BF16)
-        out = out + dot(active, w[v, down_rows])
-        grad_hidden = (dot(cot_low, w[v, down_rows], NT) * (below + hidden * density)).astype(BF16)
-        grad_norm = grad_norm + dot(grad_hidden, w[v, up_rows])
-        acc[v, down_rows] += dot(active, cot_low, TN)
-        acc[v, up_rows] += dot(grad_hidden, low, TN)
-        bup[v] += jnp.sum(grad_hidden.astype(F32), axis=0, keepdims=True)
-    layer_out[...] = out.astype(BF16)
-    scaled = grad_norm * gain[...]
-    back = cot_full + scale * (
-        scaled
-        - jnp.mean(scaled, axis=-1, keepdims=True)
-        - unit * jnp.mean(scaled * unit, axis=-1, keepdims=True)
-    )
-    grad_mid[...] = back
-    back_low = back.astype(BF16)
-    for v in range(parts):
-        acc[v, out_rows] += dot(atts[v], back_low, TN)
-        grad_att[v] = dot(back_low, w[v, out_rows], NT).astype(BF16)
-    vec[0:1] += jnp.sum(grad_norm * unit, axis=0, keepdims=True)
-    vec[1:2] += jnp.sum(grad_norm, axis=0, keepdims=True)
-    vec[2:3] += jnp.sum(back, axis=0, keepdims=True)
-    vec[3:4] += jnp.sum(cot_full, axis=0, keepdims=True)
-
-    @pl.when(step == pl.num_programs(0) - 1)
-    def _():
+        acc[v, VEC_AT : VEC_AT + 8] = vec[...]
+        acc[v, VEC_AT + 4 : VEC_AT + 5, :UP_ROWS] = bup[v]
+    for d in range(ndp):
         for v in range(parts):
-            acc[v, VEC_AT : VEC_AT + 8] = vec[...]
-            acc[v, VEC_AT + 4 : VEC_AT + 5, :UP_ROWS] = bup[v]
-            for d in range(ndp):
-                cells[d, v] = acc[v, d * piece : (d + 1) * piece].astype(BF16)
-
-
-def middle_part(weights, att, tok, cot, b_out, gain, shift, b_up, b_down):
-    parts, rows, width = att.shape
-    ndp = weights.shape[0]
-    whole = lambda a: pl.BlockSpec(a.shape, lambda i: (0,) * len(a.shape))
-    shape = lambda s, t: jax.ShapeDtypeStruct(s, t)
-    tile = pl.BlockSpec((ROWS_MID, D), lambda i: (i, 0))
-    heads_tile = pl.BlockSpec((parts, ROWS_MID, width), lambda i: (0, i, 0))
-    cells = shape((ndp, parts, UNITS // ndp, D), BF16)
+            units[d, v] = acc[v, d * piece : (d + 1) * piece].astype(BF16)
+        give(d).start()
+    for t in range(tiles):
+        for k in range(3):
+            grad_from(k, t).wait_recv()
+            grad_to(k, t).wait_send()
+            att_to(k, t).wait_send()
+        grad_own(t).wait()
+    for d in range(ndp):
+        give(d).wait()
+
+
+def middle_part(attended, tok, cot, weights, b_out, gain, shift, b_up, b_down):
+    rows = tok.shape[0]
+    width = attended.shape[1]
+    ndp, parts, piece, _ = weights.shape
+    tiles = rows // ROWS_MID
+    shape = jax.ShapeDtypeStruct
     return pl.pallas_call(
         middle_kernel,
         name="middle_part",
-        cost_estimate=work(37),
-        grid=(rows // ROWS_MID,),
-        in_specs=[ANY, heads_tile, tile, tile] + [whole(a) for a in (b_out, gain, shift, b_up, b_down)],
-        out_specs=[tile, tile, heads_tile, whole(cells)],
-        out_shape=[shape((rows, D), BF16), shape((rows, D), F32), shape((parts, rows, width), BF16), cells],
+        cost_estimate=work(50),
+        in_specs=[ANY, VMEM, VMEM, ANY] + [VMEM] * 5,
+        out_specs=[VMEM, VMEM, ANY, ANY],
+        out_shape=[
+            shape((rows, D), BF16),
+            shape((rows, D), F32),
+            shape((4 * rows, width), BF16),
+            shape((ndp, parts, piece, D), BF16),
+        ],
         scratch_shapes=[
+            pltpu.VMEM((parts, rows, width), BF16),
+            pltpu.VMEM((parts, rows, width), BF16),
             pltpu.VMEM((parts, UNITS, D), BF16),
             pltpu.VMEM((parts, UNITS, D), F32),
             pltpu.VMEM((8, D), F32),
             pltpu.VMEM(b_up.shape, F32),
+            pltpu.VMEM((ndp, parts, piece, D), BF16),
+            DMA((3, tiles)),
+            DMA((3, tiles)),
+            DMA((tiles,)),
+            DMA((3, tiles)),
+            DMA((3, tiles)),
+            DMA((tiles,)),
             DMA((ndp * parts,)),
+            DMA((ndp,)),
         ],
-        compiler_params=limit(60),
-    )(weights, att, tok, cot, b_out, gain, shift, b_up, b_down)
+        compiler_params=pltpu.CompilerParams(
+            collective_id=2, has_side_effects=True, vmem_limit_bytes=60 << 20
+        ),
+    )(attended, tok, cot, weights, b_out, gain, shift, b_up, b_down)
 
 
 def finish_kernel(
@@ -1117,20 +1132,17 @@
     w_mine = w_mine.reshape(w_qkv.shape)
     weights = lax.all_gather(weights, "dp", axis=0)
     scene = scene.reshape(-1)
-    lo_f, hi_f, idc, idr = scene_ranges(scene, FWD_Q)
-    lo_b, hi_b = (lo_f, hi_f) if BWD_K == FWD_Q else scene_ranges(scene, BWD_K)[:2]
+    ids = scene_ranges(scene)
     sent_cot, q = lax.optimization_barrier((cotangent, q))
     own_cot = jnp.where(native, cotangent, lax.ppermute(sent_cot, both, swap))
-    attended, lse = attention((lo_f, hi_f, idc, idr), q, k, vt)
-    att = exchange(attended, False, 2)
-    layer_out, grad_mid, grad_att, cells = middle_part(
-        weights, att, own_tok, own_cot, line(b_out), line(gain_two), line(shift_two), all_bup, line(b_down)
+    attended, lse = attention(ids, q, k, vt)
+    layer_out, grad_mid, grad_heads, cells = middle_part(
+        attended, own_tok, own_cot, weights, line(b_out), line(gain_two), line(shift_two), all_bup, line(b_down)
     )
-    grad_heads = exchange(grad_att, True, 3)
     sent_out, grad_heads = lax.optimization_barrier((layer_out, grad_heads))
     layer_out = jnp.where(native, layer_out, lax.ppermute(sent_out, both, swap))
     cells = sum_over_dp(cells)
-    dproj = attention_back((lo_b, hi_b, idc, idr), q, k, v, kt, attended, grad_heads, lse)
+    dproj = attention_back(ids, q, k, v, kt, attended, grad_heads, lse)
     cells, dproj = lax.optimization_barrier((cells, dproj))
     tokens_grad, one_sum, d_qkv, sums = finish(
         dproj, normed, full, w_mine, grad_mid, line(gain_one), cells.reshape(4, -1, D), ndp

time: 409 us -> 360 us (0.88)
  Pallas kernels: 351 us -> 302 us
    pallas_call x3 -> x1, Pallas kernels: 81.2 us -> 50.1 us  [middle_part(): pl.pallas_call(middle_kernel, name='middle_part', cost_estimate=work(50),...]
    pallas_call x1, Pallas kernels: 42.7 us -> 33.4 us  [attention(): pl.pallas_call(functools.partial(attention_kernel, heads, total), name='a...]
    pallas_call x1, Pallas kernels: 67.2 us -> 59.1 us  [attention_back(): pl.pallas_call(functools.partial(attention_back_kernel, heads, total), na...]
  transfers between devices with their start and end apart: 4 -> 4, of which waited for: 0 -> 1; matrix products, arithmetic and copies ran while one was open for 3% -> 3% of each run, Pallas kernels for 38% -> 26%
where the time goes in v3:
time: 360 us; the launch traced here: 358 us
  Pallas kernels  302 us (84%)
  local copies, waits for them, and re-layouts  28.6 us (8%)
  between operations  14.2 us (4%)
  starting transfers between devices  6.81 us (2%)
  other arithmetic  4.77 us (1%)
    pallas_call x1, Pallas kernels, finish(): pl.pallas_call(finish_kernel, name='finish', cost_estimate=work(60), in_s...  88.8 us
    pallas_call x1, Pallas kernels, start(): pl.pallas_call(functools.partial(start_kernel, heads), name='start', cost...  70.2 us
    pallas_call x1, Pallas kernels, attention_back(): pl.pallas_call(functools.partial(attention_back_kernel, heads, total), na...  59.1 us
    pallas_call x1, Pallas kernels, middle_part(): pl.pallas_call(middle_kernel, name='middle_part', cost_estimate=work(50),...  50.1 us
    pallas_call x1, Pallas kernels, attention(): pl.pallas_call(functools.partial(attention_kernel, heads, total), name='a...  33.4 us
    unnamed x33, local copies, waits for them, and re-layouts  9.8 us
  transfers between devices with their start and end apart: 4, of which 1 were waited for; matrix products, arithmetic and copies ran while one was open for 3% of the time, Pallas kernels for 26%

profile of v3, /device:TPU:1, one launch (start us, length us, event | category | flops | bytes accessed | tf_op | source)
XLA Modules:
  0.0 358.1 jit_solution(8428829908829365980)
XLA Ops:
  7.3 1.4 copy.41
  8.7 1.3 reshape.83.gain
  10.0 1.4 copy.40
  12.6 0.9 fusion.2.mine
  13.5 70.2 %start.1 = (bf16[3456,768]{1,0:T(8,128)(2,1)}, bf16[864,768]{1,0:T(8,128)(2,1)}, bf16[3,4,192,192]{3,2,1,0:T(8,128)(2,1)}, s32[27,128]{1,0:T(8,128)}, f32[4,1,38...) custom-call(bf16[864,768]{1,0:T(8,128)(2,1)} %tok.1, ...), custom_call_target="tpu_custom_call" | custom-call | flops 49999998976 | bytes 150000000 | tf_op jit(solution)/shard_map/start/pallas_call | solution.py:355
  83.8 2.4 collective-permute-start
  87.9 2.8 broadcast_in_dim.37.idc
  92.1 33.4 %attention.1 = (bf16[3584,192]{1,0:T(8,128)(2,1)}, f32[3,3584]{1,0:T(4,128)}) custom-call(s32[14]{0:T(128)} %get-tuple-element.132.lo, s32[14]{0:T(128)} %get-tuple-element.131.hi, s32[3840,1]{1,0:T(8,128)} %broadcast_in_dim.37.idc, s32[1,3840]{1,0:T(1,128)} %broadcast_in_dim.36.idr, bf16[3,3840,128]{2,1,0:T(8,128)(2,1)} %get-tuple-element.43.q, ...), custom_call_target="tpu_custom_call" | custom-call | flops 31000000512 | bytes 93000000 | tf_op jit(solution)/shard_map/attention/pallas_call | solution.py:451
  127.8 1.2 broadcast_select_fusion.1.cot
  129.0 2.1 all-gather.3.cloned.1.call-done
  131.1 50.1 %middle_part.1 = (bf16[864,768]{1,0:T(8,128)(2,1)}, f32[864,768]{1,0:T(8,128)}, bf16[3456,192]{1,0:T(8,128)(2,1)}, bf16[8,4,128,768]{3,2,1,0:T(8,128)(2,1)}) custom-call(bf16[3584,192]{1,0:T(8,128)(2,1)} %get-tuple-element.46.attended.out, bf16[864,768]{1,0:T(8,128)(2,1)} %get-tuple-element.47.tok, bf16[864,768]{1,0:T(8,128)(2,1)} %broadcast_select_fusion.1.cot, ...), custom_call_target="tpu_custom_call" | custom-call | flops 49999998976 | bytes 150000000 | tf_op jit(solution)/shard_map/middle_part/pallas_call | solution.py:716
  181.3 0.8 copy-done.7
  182.7 4.3 %collective-permute-start.1 = (bf16[864,768]{1,0:T(8,128)(2,1)S(1)}, bf16[864,768]{1,0:T(8,128)(2,1)S(1)}, u32[]{:S(2)}, u32[]{:S(2)}) collective-permute-start(bf16[864,768]{1,0:T(8,128)(2,1)S(1)} %copy-done.2), channel_id=1, source_target_pairs={{2,4},{3,5},{4,2},{5,3},{10,12},{11,13},{12,10},{13,11},{18,20},{1... | collective-permute-start | bytes 3981320 | tf_op jit(solution)/shard_map/ppermute | solution.py:1143
  187.0 59.1 %attention_back.1.dproj = bf16[3,3584,192]{2,1,0:T(8,128)(2,1)} custom-call(s32[14]{0:T(128)} %get-tuple-element.132.lo, s32[14]{0:T(128)} %get-tuple-element.131.hi, s32[3840,1]{1,0:T(8,128)} %broadcast_in_dim.37.idc, s32[1,3840]{1,0:T(1,128)} %broadcast_in_dim.36.idr, bf16[3,3840,128]{2,1,0:T(8,128)(2,1)} %get-tuple-element.43.q, ...), custom_call_target="tpu_custom_call" | custom-call | flops 51000000512 | bytes 153000000 | tf_op jit(solution)/shard_map/attention_back/pallas_call | solution.py:538
  246.1 1.2 broadcast_select_fusion
  247.3 88.8 %finish.1 = (f32[864,768]{1,0:T(8,128)}, f32[8,768]{1,0:T(8,128)}, f32[576,768]{1,0:T(8,128)}, f32[1024,768]{1,0:T(8,128)}) custom-call(bf16[3,3584,192]{2,1,0:T(8,128)(2,1)} %attention_back.1.dproj, bf16[3456,768]{1,0:T(8,128)(2,1)} %get-tuple-element.60.normed, bf16[3456,768]{1,0:T(8,128)(2,1)} %get-tuple-element.61.full, bf16[3,768,192]{2,1,0:T(8,128)(2,1)} %bitcast.24, ...), custom_call_target="tpu_custom_call" | custom-call | flops 60000002048 | bytes 180000000 | tf_op jit(solution)/shard_map/finish/pallas_call | solution.py:1023
  336.2 2.8 fusion.5
  338.9 1.9 slice.45
  340.9 1.5 slice_reduce_fusion
  342.4 1.3 slice_reduce_fusion.6
  343.7 1.4 copy.44
  345.1 1.4 slice_reduce_fusion.4
  346.5 3.6 copy.47
  350.0 1.2 copy.48
  (54 shorter events, 7.4 us)
Async XLA Ops:
  7.2 2.8 copy-start.3
  7.2 123.9 %all-gather.3.cloned.1.call-start = ((), (), s32[]{:S(2)}) async-start(), calls=%async_computation.2 | async-start | bytes 7077888 | tf_op jit(solution)/shard_map/all_gather | solution.py:1133
  7.2 4.1 %copy-start.8 = (f32[768]{0:T(1024)S(1)}, f32[768]{0:T(1024)}, u32[]{:S(2)}) copy-start(f32[768]{0:T(1024)} %param.17) | copy-start | bytes 9220
  7.3 4.7 %copy-start.13 = (f32[384]{0:T(512)S(1)}, f32[384]{0:T(512)}, u32[]{:S(2)}) copy-start(f32[384]{0:T(512)} %param.24) | copy-start | bytes 4612
  7.3 5.4 %copy-start.4 = (bf16[384,768]{1,0:T(8,128)(2,1)S(1)}, bf16[384,768]{1,0:T(8,128)(2,1)}, u32[]{:S(2)}) copy-start(bf16[384,768]{1,0:T(8,128)(2,1)} %param.25) | copy-start | bytes 1769476
  7.3 5.3 %copy-start.5 = (bf16[192,768]{1,0:T(8,128)(2,1)S(1)}, bf16[192,768]{1,0:T(8,128)(2,1)}, u32[]{:S(2)}) copy-start(bf16[192,768]{1,0:T(8,128)(2,1)} %param.19) | copy-start | bytes 884740
  13.5 70.3 %copy-start.1 = (bf16[864,768]{1,0:T(8,128)(2,1)S(1)}, bf16[864,768]{1,0:T(8,128)(2,1)}, u32[]{:S(2)}) copy-start(bf16[864,768]{1,0:T(8,128)(2,1)} %param.27) | copy-start | bytes 3981316
  83.7 7.6 %copy-start.6 = (s32[27,128]{1,0:T(8,128)S(1)}, s32[27,128]{1,0:T(8,128)}, u32[]{:S(2)}) copy-start(s32[27,128]{1,0:T(8,128)} %get-tuple-element.41) | copy-start | bytes 41476
  83.7 163.6 %reduce-scatter.2.cloned.1.call-start = ((), (), s32[]{:S(2)}) async-start(), calls=%async_computation.1 | async-start | bytes 7077888 | tf_op jit(solution)/shard_map/reduce_scatter | solution.py:1096
  83.8 44.0 %collective-permute-start = (bf16[864,768]{1,0:T(8,128)(2,1)S(1)}, bf16[864,768]{1,0:T(8,128)(2,1)S(1)}, u32[]{:S(2)}, u32[]{:S(2)}) collective-permute-start(bf16[864,768]{1,0:T(8,128)(2,1)S(1)} %copy-done.1), channel_id=1, source_target_pairs={{2,4},{3,5},{4,2},{5,3},{10,12},{11,13},{12,10},{13,11},{18,20},{1... | collective-permute-start | bytes 3981320 | tf_op jit(solution)/shard_map/ppermute | solution.py:1137
  92.1 33.4 %copy-start.9 = (f32[768]{0:T(1024)S(1)}, f32[768]{0:T(1024)}, u32[]{:S(2)}) copy-start(f32[768]{0:T(1024)} %param.20) | copy-start | bytes 9220
  92.1 34.0 %copy-start.10 = (f32[768]{0:T(1024)S(1)}, f32[768]{0:T(1024)}, u32[]{:S(2)}) copy-start(f32[768]{0:T(1024)} %param.21) | copy-start | bytes 9220
  92.1 34.5 %copy-start.11 = (f32[768]{0:T(1024)S(1)}, f32[768]{0:T(1024)}, u32[]{:S(2)}) copy-start(f32[768]{0:T(1024)} %param.22) | copy-start | bytes 9220
  92.1 35.1 %copy-start.12 = (f32[768]{0:T(1024)S(1)}, f32[768]{0:T(1024)}, u32[]{:S(2)}) copy-start(f32[768]{0:T(1024)} %param.26) | copy-start | bytes 9220
  181.2 0.8 copy-start.7
  181.2 1.4 copy-start.2
  182.7 63.4 %collective-permute-start.1 = (bf16[864,768]{1,0:T(8,128)(2,1)S(1)}, bf16[864,768]{1,0:T(8,128)(2,1)S(1)}, u32[]{:S(2)}, u32[]{:S(2)}) collective-permute-start(bf16[864,768]{1,0:T(8,128)(2,1)S(1)} %copy-done.2), channel_id=1, source_target_pairs={{2,4},{3,5},{4,2},{5,3},{10,12},{11,13},{12,10},{13,11},{18,20},{1... | collective-permute-start | bytes 3981320 | tf_op jit(solution)/shard_map/ppermute | solution.py:1143
  346.5 3.6 copy-start
Sparse Core Ops, SparseCore 0:
  83.8 47.1 all-gather.2
  181.4 60.7 reduce-scatter.1

commit v4 on v3

v4 whole, which is shorter than its diff:
```python
import functools

import jax
import jax.numpy as jnp
from jax import lax
from jax.experimental import pallas as pl
from jax.experimental.pallas import tpu as pltpu
from jax.sharding import PartitionSpec as P

HEAD = 64
D = 768
FF = 1536
LANES = 128
PAD = 512
OUT_ROWS = D // 4
UP_ROWS = FF // 4
VEC_AT = OUT_ROWS + 2 * UP_ROWS
UNITS = 1024
EPS = 1e-05
MASKED = -1e30
MESH = pl.DeviceIdType.MESH
F32 = jnp.float32
BF16 = jnp.bfloat16
VMEM = pl.BlockSpec(memory_space=pltpu.VMEM)
SMEM = pl.BlockSpec(memory_space=pltpu.SMEM)
ANY = pl.BlockSpec(memory_space=pl.ANY)
DMA = pltpu.SemaphoreType.DMA

NN = (((1,), (0,)), ((), ()))
NT = (((1,), (1,)), ((), ()))
TN = (((0,), (0,)), ((), ()))


def dot(a, b, dims=NN):
    return lax.dot_general(a, b, dims, preferred_element_type=F32)


def work(us):
    return pl.CostEstimate(flops=us * 10**9, bytes_accessed=us * 3 * 10**6, transcendentals=0)


def limit(mib):
    return pltpu.CompilerParams(vmem_limit_bytes=mib << 20)


def line(ref):
    return ref[...].reshape(1, -1)


class Place:
    def __init__(self):
        self.d = lax.axis_index("dp")
        self.m = lax.axis_index("mp")
        self.c = lax.rem(self.d, 2)
        self.r = lax.rem(self.m, 2)
        self.hf = self.m // 2
        self.q = 2 * self.c + self.r
        self.native = self.c == self.hf
        self.sibling = (self.d + 1 - 2 * self.c, self.m)
        self.cross = (self.d, self.m + 1 - 2 * self.r)
        self.partner = (self.d + 1 - 2 * self.c, lax.rem(self.m + 2, 4))

    def member(self, quarter):
        return (self.d - self.c + quarter // 2, 2 * self.hf + quarter % 2)


def greet(others):
    barrier = pltpu.get_barrier_semaphore()
    for other in others:
        pl.semaphore_signal(barrier, inc=1, device_id=other, device_id_type=MESH)
    pl.semaphore_wait(barrier, len(others))


def remote(src, dst, send, recv, device):
    return pltpu.make_async_remote_copy(
        src_ref=src, dst_ref=dst, send_sem=send, recv_sem=recv, device_id=device, device_id_type=MESH
    )


PIECES = 3
TILE = 384
SCENES = 4


def normalise(x):
    centred = x - jnp.mean(x, axis=-1, keepdims=True)
    scale = lax.rsqrt(jnp.mean(centred * centred, axis=-1, keepdims=True) + EPS)
    return centred * scale, scale


def widen(x, ones, rows):
    lane = lax.broadcasted_iota(jnp.int32, (rows, LANES - HEAD), 1)
    return jnp.concatenate([x, jnp.where(lane < ones, 1.0, 0.0).astype(x.dtype)], axis=1)


def describe_scenes(ids, row, column, before):
    lines = ids.shape[0]
    for j in range(lines):
        place = j * LANES + lax.broadcasted_iota(jnp.int32, (1, LANES), 1)
        number = ids[j : j + 1, :]
        number = jnp.where(number >= 0, number, -1 - place)
        span = slice(j * LANES, (j + 1) * LANES)
        row[:, span] = number
        column[span, :] = jnp.broadcast_to(number.astype(F32), (LANES, LANES)).T[:, :1].astype(jnp.int32)
    rest = row.shape[1] - lines * LANES
    row[:, lines * LANES :] = jnp.full((1, rest), -(1 << 21), jnp.int32)
    column[lines * LANES :, :] = jnp.full((rest, 1), -(1 << 20), jnp.int32)
    lane = lax.broadcasted_iota(jnp.int32, (1, LANES), 1)
    counts = jnp.zeros((1, LANES), F32)
    for number in range(1, SCENES + 1):
        mine = jnp.where((ids[...] >= 0) & (ids[...] < number), 1.0, 0.0)
        total = jnp.sum(jnp.sum(mine, axis=0, keepdims=True), axis=1, keepdims=True)
        counts = jnp.where(lane == number, total, counts)
    before[...] = counts.astype(jnp.int32)


def start_kernel(
    heads, tok, wq, ids, b_up, gain, shift, mine,
    full, own, w_out, ids_own, id_row, id_column, before, b_ups, normed, q, k, v, kt, vt, units,
    buf, w, low_s, q_s, k_s, v_s, kt_s, vt_s,
    swap_s, swap_r, cross_s, cross_r, sib_s, sib_r, fwd_s, fwd_r, w_s, w_r, ids_s, ids_r, b_s, b_r, out_s, late_s,
    uz_s, uz_r,
):
    me = Place()
    foreign = jnp.logical_not(me.native)
    rows = tok.shape[0]
    piece = rows // PIECES
    total = buf.shape[0]
    tiles = total // TILE
    groups = w.shape[1]
    group = me.d // 2
    around = [(me.d, lax.rem(me.m + j, 4)) for j in range(1, 4)]
    lines = [(2 * lax.rem(group + j, groups) + me.c, me.m) for j in range(1, groups)]
    greet([me.sibling, me.partner] + around + lines)

    def rows_of(quarter, n):
        p = jnp.where(me.hf == 0, n, PIECES - 1 - n)
        return pl.ds(pl.multiple_of(quarter * rows + p * piece, 16), piece)

    def part(quarter, n):
        return buf.at[rows_of(quarter, n)]

    sib_q = 2 * (1 - me.c) + me.r
    cross_q = 2 * me.c + 1 - me.r
    sib_cross_q = 2 * (1 - me.c) + 1 - me.r

    def swap(n):
        p = jnp.where(me.hf == 1, n, PIECES - 1 - n)
        src = tok.at[pl.ds(pl.multiple_of(p * piece, 16), piece)]
        dst = buf.at[pl.ds(pl.multiple_of(sib_q * rows + p * piece, 16), piece)]
        return remote(src, dst, swap_s.at[n], swap_r.at[n], me.partner)

    def swap_in(n):
        return remote(part(me.q, n), part(me.q, n), swap_s.at[n], swap_r.at[n], me.partner)

    def cross(quarter, n):
        return remote(part(quarter, n), part(quarter, n), cross_s.at[n], cross_r.at[n], me.cross)

    def sib(quarter, n):
        return remote(part(quarter, n), part(quarter, n), sib_s.at[n], sib_r.at[n], me.sibling)

    def forward(quarter, n):
        return remote(part(quarter, n), part(quarter, n), fwd_s.at[n], fwd_r.at[n], me.sibling)

    weight = remote(wq.at[:, group], w.at[:, group], w_s.at[0], w_r.at[0], me.partner)

    def weight_share(j):
        return remote(w.at[:, group], w.at[:, group], w_s.at[j], w_r.at[j], lines[j - 1])

    def weight_in(j):
        source = lax.rem(group + groups - j, groups)
        return remote(w.at[:, source], w.at[:, source], w_s.at[j], w_r.at[j], lines[j - 1])

    unit_own = pltpu.make_async_copy(mine, units.at[me.m], late_s.at[7])

    def unit_z(j, source):
        return remote(mine, units.at[source], uz_s.at[j], uz_r.at[j], around[j])

    def give_b_up(j):
        return remote(b_ups.at[me.m], b_ups.at[me.m], b_s.at[j], b_r.at[j], around[j])

    scenes = remote(ids, ids_own, ids_s, ids_r, me.sibling)
    unit_own.start()
    b_ups[me.m] = line(b_up)
    for j in range(3):
        give_b_up(j).start()

    @pl.when(me.native)
    def _():
        scenes.start()
        buf[pl.ds(pl.multiple_of(me.q * rows, 16), rows), :] = tok[...]
        for n in range(PIECES):
            cross(me.q, n).start()
            sib(me.q, n).start()
        w[...] = wq[...]
        ids_own[...] = ids[...]

    @pl.when(foreign)
    def _():
        weight.start()
        for n in range(PIECES):
            swap(n).start()

    def share(n):
        swap_in(n).wait_recv()
        cross(me.q, n).start()
        sib(me.q, n).start()

    def pass_on(n):
        cross(cross_q, n).wait_recv()
        forward(cross_q, n).start()

    def from_sibling(n):
        sib(sib_q, n).wait_recv()
        forward(sib_cross_q, n).wait_recv()

    def outputs(t):
        span = pl.ds(pl.multiple_of(t * TILE, LANES), TILE)
        pairs = [
            (low_s.at[span], normed.at[span]),
            (buf.at[span], full.at[span]),
            (q_s.at[:, span], q.at[:, span]),
            (k_s.at[:, span], k.at[:, span]),
            (v_s.at[:, span], v.at[:, span]),
            (kt_s.at[:, :, span], kt.at[:, :, span]),
            (vt_s.at[:, :, span], vt.at[:, :, span]),
        ]
        return [pltpu.make_async_copy(src, dst, out_s.at[t, j]) for j, (src, dst) in enumerate(pairs)]

    ones = jnp.where(lax.broadcasted_iota(jnp.int32, (16, TILE), 0) < 1, 1.0, 0.0).astype(BF16)

    def compute(first, stride, count):
        def one(n, _):
            at = first + stride * n
            t = jnp.where(me.hf == 0, at, tiles - 1 - at)
            span = pl.ds(pl.multiple_of(t * TILE, LANES), TILE)
            unit, _ = normalise(buf[span, :].astype(F32))
            low = (unit * line(gain) + line(shift)).astype(BF16)
            low_s[span, :] = low
            qs = (dot(low, w[0].reshape(-1, D), NT).astype(BF16).astype(F32) * HEAD**-0.5).astype(BF16)
            ks = dot(low, w[1].reshape(-1, D), NT)
            vs = dot(low, w[2].reshape(-1, D), NT)
            kts = ks.T.astype(BF16)
            vts = vs.T.astype(BF16)
            ks = ks.astype(BF16)
            vs = vs.astype(BF16)
            for h in range(heads):
                cols = slice(h * HEAD, (h + 1) * HEAD)
                q_s[h, span, :] = widen(qs[:, cols], 0, TILE)
                k_s[h, span, :] = widen(ks[:, cols], 3, TILE)
                v_s[h, span, :] = widen(vs[:, cols], 3, TILE)
                kt_s[h, :, span] = kts[cols]
                vt_s[h, :HEAD, span] = vts[cols]
                vt_s[h, HEAD:, span] = ones
            for copy in outputs(t):
                copy.start()
            return 0

        lax.fori_loop(0, count, one, 0)

    pad = pl.ds(total, PAD)
    zeros = jnp.zeros((heads, PAD, LANES), BF16)
    for ref in (q_s, k_s, v_s):
        ref[:, pad, :] = zeros
    for ref in (kt_s, vt_s):
        ref[:, :, pad] = jnp.zeros((heads, ref.shape[1], PAD), BF16)
    padding = [
        pltpu.make_async_copy(src, dst, late_s.at[j])
        for j, (src, dst) in enumerate(
            [(a.at[:, pad], b.at[:, pad]) for a, b in ((q_s, q), (k_s, k), (v_s, v))]
            + [(a.at[:, :, pad], b.at[:, :, pad]) for a, b in ((kt_s, kt), (vt_s, vt))]
        )
    ]
    for copy in padding:
        copy.start()

    @pl.when(me.native)
    def _():
        for n in range(PIECES):
            pass_on(n)

    @pl.when(foreign)
    def _():
        weight.wait_recv()
        for j in range(1, groups):
            weight_share(j).start()
        for n in range(PIECES):
            share(n)
        for j in range(1, groups):
            weight_in(j).wait_recv()
        for n in range(PIECES):
            from_sibling(n)

    for j in range(3):
        unit_z(j, me.m).start()

    @pl.when(foreign)
    def _():
        scenes.wait_recv()

    describe_scenes(ids_own, id_row, id_column, before)
    compute(0, 1, 2)

    @pl.when(foreign)
    def _():
        pass_on(0)

    compute(2, 1, 2)

    @pl.when(foreign)
    def _():
        pass_on(1)

    @pl.when(me.native)
    def _():
        from_sibling(0)

    compute(4, 1, 1)

    @pl.when(me.native)
    def _():
        from_sibling(1)

    compute(5, 2, 2)

    @pl.when(foreign)
    def _():
        pass_on(2)

    @pl.when(me.native)
    def _():
        from_sibling(2)

    own_copy = pltpu.make_async_copy(buf.at[pl.ds(pl.multiple_of(me.q * rows, 16), rows)], own, late_s.at[5])
    w_copy = pltpu.make_async_copy(w, w_out, late_s.at[6])
    own_copy.start()
    w_copy.start()
    compute(6, 2, 2)
    unit_own.wait()
    for j in range(3):
        unit_z(j, lax.rem(me.m + 3 - j, 4)).wait_recv()
        unit_z(j, me.m).wait_send()

    for j in range(3):
        source = lax.rem(me.m + 3 - j, 4)
        remote(b_ups.at[source], b_ups.at[source], b_s.at[j], b_r.at[j], around[j]).wait_recv()
        give_b_up(j).wait_send()

    @pl.when(me.native)
    def _():
        scenes.wait_send()

    @pl.when(foreign)
    def _():
        weight.wait_send()
        for j in range(1, groups):
            weight_share(j).wait_send()
        for n in range(PIECES):
            swap(n).wait_send()

    for n in range(PIECES):
        cross(me.q, n).wait_send()
        sib(me.q, n).wait_send()
        forward(cross_q, n).wait_send()
    for copy in padding + [own_copy, w_copy]:
        copy.wait()

    def finish_tile(t, _):
        for copy in outputs(t):
            copy.wait()
        return 0

    lax.fori_loop(0, tiles, finish_tile, 0)


def start(tokens, w_qkv, scene_ids, b_up, gain, shift, mine, ndp):
    rows = tokens.shape[0]
    total = 4 * rows
    heads = w_qkv.shape[1] // HEAD
    groups = ndp // 2
    w_qkv = w_qkv.reshape(3, groups, -1, D)
    units = (4,) + mine.shape
    wide = total + PAD
    shape = jax.ShapeDtypeStruct
    rowed = (heads, wide, LANES)
    k_cols, v_cols = (heads, HEAD, wide), (heads, HEAD + 16, wide)
    three = DMA((PIECES,))
    return pl.pallas_call(
        functools.partial(start_kernel, heads),
        name="start",
        cost_estimate=work(50),
        in_specs=[VMEM] * 6 + [ANY],
        out_specs=[ANY] * 3 + [VMEM] * 5 + [ANY] * 7,
        out_shape=[
            shape((total, D), BF16),
            shape((rows, D), BF16),
            shape(w_qkv.shape, BF16),
            shape(scene_ids.shape, jnp.int32),
            shape((1, wide), jnp.int32),
            shape((wide, 1), jnp.int32),
            shape((1, LANES), jnp.int32),
            shape((4, 1) + b_up.shape, F32),
            shape((total, D), BF16),
            shape(rowed, BF16),
            shape(rowed, BF16),
            shape(rowed, BF16),
            shape(k_cols, BF16),
            shape(v_cols, BF16),
            shape(units, BF16),
        ],
        scratch_shapes=[
            pltpu.VMEM((total, D), BF16),
            pltpu.VMEM(w_qkv.shape, BF16),
            pltpu.VMEM((total, D), BF16),
            pltpu.VMEM(rowed, BF16),
            pltpu.VMEM(rowed, BF16),
            pltpu.VMEM(rowed, BF16),
            pltpu.VMEM(k_cols, BF16),
            pltpu.VMEM(v_cols, BF16),
        ]
        + [three] * 8
        + [DMA((groups,))] * 2
        + [DMA] * 2
        + [DMA((3,))] * 2
        + [DMA((total // TILE, 7)), DMA((8,))]
        + [DMA((3,))] * 2,
        compiler_params=pltpu.CompilerParams(
            collective_id=1, has_side_effects=True, vmem_limit_bytes=60 << 20
        ),
    )(tokens, w_qkv, scene_ids, b_up, gain, shift, mine)


BLOCK = 256
STEP = 512


def blocks(total):
    return -(-total // BLOCK)


def block_range(i, numbers, before):
    lines = numbers.shape[0]
    per = BLOCK // LANES
    top, bottom = numbers[i * per, 0], numbers[jnp.minimum(i * per + per, lines) - 1, LANES - 1]
    bottom = jnp.where(i * per + per > lines, -1, bottom)
    low = jnp.where(top >= 0, before[0, jnp.maximum(top, 0)], i * BLOCK)
    high = jnp.where(bottom >= 0, before[0, jnp.maximum(bottom, 0) + 1], i * BLOCK + BLOCK)
    return low // LANES, (high + LANES - 1) // LANES


def list_steps(count, numbers, before, total, block_at, step_at, marks):
    stride = STEP // LANES

    def one_block(i, n):
        first, last = block_range(i, numbers, before)
        steps = (last - first + stride - 1) // stride

        def put(j, n):
            block_at[n] = i * (BLOCK // LANES)
            step_at[n] = first + j * stride
            marks[n] = jnp.where(j == 0, 1, 0) + jnp.where(j == steps - 1, 2, 0)
            return n + 1

        return lax.fori_loop(0, steps, put, n)

    n = lax.fori_loop(0, count, one_block, 0)
    for idle in range(2):
        block_at[n + idle] = 0
        step_at[n + idle] = total // LANES
        marks[n + idle] = 0
    return n


def step_lists(total):
    return [pltpu.SMEM((blocks(total) * (-(-total // STEP) + 1) + 2,), jnp.int32)] * 3


def attention_kernel(
    heads, total, numbers, before, idc, idr, q, k, vt, out, lse, block_at, step_at, marks, even, odd
):
    count = list_steps(blocks(total), numbers, before, total, block_at, step_at, marks)

    def place(i):
        rows = pl.ds(pl.multiple_of(block_at[i] * LANES, LANES), BLOCK)
        return rows, pl.ds(pl.multiple_of(step_at[i] * LANES, LANES), STEP)

    def score(i, buf, h):
        rows, cols = place(i)
        s = jnp.where(idc[cols, :] == idr[:, rows], dot(k[h, cols, :], q[h, rows, :], NT), MASKED)
        buf[h] = s
        return jnp.max(s, axis=0, keepdims=True)

    def step(i, now, after, carry):
        rows, cols = place(i)
        mark = marks[i]
        new = []
        for h in range(heads):
            top, acc, highest = carry[h]
            upcoming = score(i + 1, after, h)
            top = jnp.where(lax.rem(mark, 2) == 1, MASKED, top)
            above = jnp.maximum(top, highest)
            p = jnp.exp(now[h] - above).astype(BF16)
            acc = acc * jnp.exp(top - above) + dot(vt[h, :, cols], p)
            new.append((above, acc, upcoming))

        @pl.when(mark >= 2)
        def _():
            valid = jnp.where(idr[:, rows] >= 0, 1.0, 0.0)
            mixed = []
            for h in range(heads):
                top, acc, _ = new[h]
                row_total = acc[HEAD : HEAD + 1]
                mixed.append(acc[:HEAD] * (valid / row_total))
                lse[pl.ds(h, 1), rows] = top + jnp.log(row_total)
            out[rows, :] = jnp.concatenate(mixed, axis=0).T.astype(BF16)

        return tuple(new)

    low = jnp.full((1, BLOCK), MASKED, F32)
    start = tuple((low, jnp.zeros((vt.shape[1], BLOCK), F32), score(0, even, h)) for h in range(heads))

    def two_steps(n, carry):
        return step(2 * n + 1, odd, even, step(2 * n, even, odd, carry))

    lax.fori_loop(0, (count + 1) // 2, two_steps, start)


def attention(ids, q, k, vt):
    heads, wide, _ = q.shape
    total = wide - PAD
    rows = blocks(total) * BLOCK
    scores = pltpu.VMEM((heads, STEP, BLOCK), F32)
    return pl.pallas_call(
        functools.partial(attention_kernel, heads, total),
        name="attention",
        cost_estimate=work(31),
        in_specs=[SMEM] * 2 + [VMEM] * 5,
        out_specs=[VMEM, VMEM],
        out_shape=[
            jax.ShapeDtypeStruct((rows, heads * HEAD), BF16),
            jax.ShapeDtypeStruct((heads, wide), F32),
        ],
        scratch_shapes=step_lists(total) + [scores, scores],
        compiler_params=limit(56),
    )(*ids, q, k, vt)


def in_steps(first, last, body, carry):
    wide, narrow = 2 * BLOCK // LANES, BLOCK // LANES
    count = (last - first + narrow - 1) // narrow
    carry = lax.fori_loop(0, count // 2, lambda n, c: body(2 * BLOCK, first + n * wide, c), carry)
    return lax.fori_loop(0, count % 2, lambda n, c: body(BLOCK, first + (count - 1) * narrow, c), carry)


def attention_back_kernel(
    heads, total, numbers, before, idc, idr, q, k, v, kt, out, grad, lse, dproj, g, delta, dq
):
    wide = q.shape[1]
    width = heads * HEAD
    head_of = lax.broadcasted_iota(jnp.int32, (8, width), 1) // HEAD
    pick = jnp.where(head_of == lax.broadcasted_iota(jnp.int32, (8, width), 0), 1.0, 0.0).astype(BF16)
    none = jnp.zeros((TILE, LANES - HEAD), BF16)

    def prepare(i, _):
        rows = pl.ds(pl.multiple_of(i * TILE, LANES), TILE)
        grads = jnp.where(idc[rows, :] >= 0, grad[rows, :].astype(F32), 0.0)
        inner = grads * out[rows, :].astype(F32)
        high = inner.astype(BF16)
        rest = (inner - high.astype(F32)).astype(BF16)
        delta[:, rows] = dot(pick, high, NT) + dot(pick, rest, NT)
        grads = grads.astype(BF16)
        for h in range(heads):
            g[h, rows, :] = jnp.concatenate([grads[:, h * HEAD : (h + 1) * HEAD], none], axis=1)
            dq[h, :, rows] = jnp.zeros((HEAD, TILE), F32)
        return 0

    lax.fori_loop(0, total // TILE, prepare, 0)
    tail = wide - total
    delta[:, total:] = jnp.zeros((8, tail), F32)
    for h in range(heads):
        g[h, total:, :] = jnp.zeros((tail, LANES), BF16)
        dq[h, :, total:] = jnp.zeros((HEAD, tail), F32)

    def one_block(i, _):
        c0 = pl.multiple_of(i * BLOCK, LANES)
        cols = pl.ds(c0, BLOCK)
        mine = idc[cols, :]
        low, high = block_range(i, numbers, before)

        def queries(size, at, carry):
            rows = pl.ds(pl.multiple_of(at * LANES, LANES), size)
            allowed = mine == idr[:, rows]
            both = [
                (dot(k[h, cols, :], q[h, rows, :], NT), dot(v[h, cols, :], g[h, rows, :], NT)) for h in range(heads)
            ]
            new = []
            for h in range(heads):
                dk, dv = carry[h]
                s, dp = both[h]
                p = jnp.where(allowed, jnp.exp(s - lse[h : h + 1, rows]), 0.0)
                ds = (p * (dp - delta[h : h + 1, rows])).astype(BF16)
                dv = dv + dot(p.astype(BF16), g[h, rows, :])
                dk = dk + dot(ds, q[h, rows, :])
                dq[h, :, rows] += dot(kt[h, :, cols], ds)
                new.append((dk, dv))
            return tuple(new)

        zero = jnp.zeros((BLOCK, LANES), F32)
        done = in_steps(low, high, queries, tuple((zero, zero) for _ in range(heads)))
        for part in range(2):
            joined = jnp.concatenate([done[h][part][:, :HEAD] for h in range(heads)], axis=1)
            dproj[part + 1, cols, :] = joined.astype(BF16)
        return 0

    lax.fori_loop(0, blocks(total), one_block, 0)

    def finish(i, _):
        rows = pl.ds(pl.multiple_of(i * TILE, LANES), TILE)
        joined = jnp.concatenate([dq[h, :, rows] for h in range(heads)], axis=0)
        dproj[0, rows, :] = (joined * HEAD**-0.5).T.astype(BF16)
        return 0

    lax.fori_loop(0, total // TILE, finish, 0)


def attention_back(ids, q, k, v, kt, out, grad, lse):
    heads, wide, _ = q.shape
    total = wide - PAD
    return pl.pallas_call(
        functools.partial(attention_back_kernel, heads, total),
        name="attention_back",
        cost_estimate=work(51),
        in_specs=[SMEM] * 2 + [VMEM] * 9,
        out_specs=VMEM,
        out_shape=jax.ShapeDtypeStruct((3, blocks(total) * BLOCK, heads * HEAD), BF16),
        scratch_shapes=[
            pltpu.VMEM((heads, wide, LANES), BF16),
            pltpu.VMEM((8, wide), F32),
            pltpu.VMEM((heads, HEAD, wide), F32),
        ],
        compiler_params=limit(60),
    )(*ids, q, k, v, kt, out, grad, lse)


ROWS_MID = 288


def middle_kernel(
    attended, tok, cot, cot_came, b_out, gain, shift, b_up, b_down, *rest
):
    me = Place()
    groups = len(rest) - 25
    weights = rest[:groups]
    layer_out, grad_mid, grad_heads, cells = rest[groups : groups + 4]
    (
        att, grad_att, w, acc, vec, bup, sent, came, units,
        att_s, att_r, own_s, grad_s, grad_r, back_s, unit_s, push_s, push_r, sum_s, sum_r, cell_s,
    ) = rest[groups + 4 :]
    group = me.d // 2
    parts, piece, _ = weights[0].shape
    rows = tok.shape[0]
    tiles = rows // ROWS_MID
    width = att.shape[2]
    others = [lax.rem(me.q + k, 4) for k in range(1, 4)]
    greet([me.member(quarter) for quarter in others])

    def tile(t, quarter=0):
        return pl.ds(pl.multiple_of(quarter * rows + t * ROWS_MID, 16), ROWS_MID)

    def att_to(k, t):
        return remote(
            attended.at[tile(t, others[k])], att.at[me.q, tile(t)], att_s.at[k, t], att_r.at[k, t], me.member(others[k])
        )

    def att_from(k, t):
        source = others[2 - k]
        return remote(
            attended.at[tile(t)], att.at[source, tile(t)], att_s.at[k, t], att_r.at[k, t], me.member(source)
        )

    def att_own(t):
        return pltpu.make_async_copy(attended.at[tile(t, me.q)], att.at[me.q, tile(t)], own_s.at[t])

    def grad_to(k, t):
        return remote(
            grad_att.at[others[k], tile(t)], grad_heads.at[tile(t, me.q)], grad_s.at[k, t], grad_r.at[k, t], me.member(others[k])
        )

    def grad_from(k, t):
        source = others[2 - k]
        return remote(
            grad_att.at[source, tile(t)], grad_heads.at[tile(t, source)], grad_s.at[k, t], grad_r.at[k, t], me.member(source)
        )

    def grad_own(t):
        return pltpu.make_async_copy(grad_att.at[me.q, tile(t)], grad_heads.at[tile(t, me.q)], back_s.at[t])

    for t in range(tiles):
        for k in (1, 0, 2):
            att_to(k, t).start()
        att_own(t).start()

    def w_rows(j, core):
        source = 2 * lax.rem(group + groups - j, groups) + core
        return w.at[:, pl.ds(pl.multiple_of(source * piece, 16), piece)]

    def load(j):
        return pltpu.make_async_copy(weights[j], w_rows(j, me.c), unit_s.at[j])

    def push(j):
        return remote(weights[j], w_rows(j, me.c), push_s.at[j], push_r.at[j], me.sibling)

    def pushed(j):
        return remote(weights[j], w_rows(j, 1 - me.c), push_s.at[j], push_r.at[j], me.sibling)

    for j in range(groups):
        push(j).start()
        load(j).start()
    for ref in (acc, vec, bup):
        ref[...] = jnp.zeros_like(ref)
    for j in range(groups):
        load(j).wait()
        pushed(j).wait_recv()

    out_rows = slice(0, OUT_ROWS)
    down_rows = slice(OUT_ROWS, OUT_ROWS + UP_ROWS)
    up_rows = slice(OUT_ROWS + UP_ROWS, VEC_AT)

    def one_tile(t, _):
        here = tile(t)
        att_own(t).wait()
        for k in range(3):
            att_from(k, t).wait_recv()
        atts = [att[v, here, :] for v in range(parts)]
        middle = tok[here, :].astype(F32) + line(b_out)
        for v in range(parts):
            middle = middle + dot(atts[v], w[v, out_rows])
        unit, scale = normalise(middle)
        low = (unit * line(gain) + line(shift)).astype(BF16)
        cot_low = jnp.where(me.native, cot[here, :], cot_came[here, :])
        cot_full = cot_low.astype(F32)
        out = middle + line(b_down)
        grad_norm = jnp.zeros_like(middle)

        def products(v):
            return dot(low, w[v, up_rows], NT), dot(cot_low, w[v, down_rows], NT)

        upcoming = products(0)
        for v in range(parts):
            hidden, grad_active = upcoming
            if v + 1 < parts:
                upcoming = products(v + 1)
            hidden = hidden + b_up[v]
            below = 0.5 * (1.0 + lax.erf(hidden * 0.5**0.5))
            density = jnp.exp(-0.5 * hidden * hidden) * 0.3989422804014327
            active = (hidden * below).astype(BF16)
            grad_hidden = (grad_active * (below + hidden * density)).astype(BF16)
            out = out + dot(active, w[v, down_rows])
            grad_norm = grad_norm + dot(grad_hidden, w[v, up_rows])
            acc[v, down_rows] += dot(active, cot_low, TN)
            acc[v, up_rows] += dot(grad_hidden, low, TN)
            bup[v] += jnp.sum(grad_hidden.astype(F32), axis=0, keepdims=True)
        layer_out[here, :] = out.astype(BF16)
        scaled = grad_norm * line(gain)
        back = cot_full + scale * (
            scaled
            - jnp.mean(scaled, axis=-1, keepdims=True)
            - unit * jnp.mean(scaled * unit, axis=-1, keepdims=True)
        )
        grad_mid[here, :] = back
        back_low = back.astype(BF16)
        for v in range(parts):
            grad_att[v, here, :] = dot(back_low, w[v, out_rows], NT).astype(BF16)
        for k in (1, 0, 2):
            grad_to(k, t).start()
        grad_own(t).start()
        for v in range(parts):
            acc[v, out_rows] += dot(atts[v], back_low, TN)
        vec[0:1] += jnp.sum(grad_norm * unit, axis=0, keepdims=True)
        vec[1:2] += jnp.sum(grad_norm, axis=0, keepdims=True)
        vec[2:3] += jnp.sum(back, axis=0, keepdims=True)
        vec[3:4] += jnp.sum(cot_full, axis=0, keepdims=True)
        return 0

    lax.fori_loop(0, tiles, one_tile, 0)

    def sum_rows(i, core):
        return pl.ds(pl.multiple_of((2 * i + core) * piece, 16), piece)

    def give(i):
        return remote(sent.at[i], came.at[i], sum_s.at[i], sum_r.at[i], me.sibling)

    def keep(i):
        return pltpu.make_async_copy(units.at[i], cells.at[i], cell_s.at[i])

    for v in range(parts):
        acc[v, VEC_AT : VEC_AT + 8] = vec[...]
        acc[v, VEC_AT + 4 : VEC_AT + 5, :UP_ROWS] = bup[v]
    for i in range(groups):
        for v in range(parts):
            sent[i, v] = acc[v, sum_rows(i, 1 - me.c), :].astype(BF16)
        give(i).start()
    for i in range(groups):
        give(i).wait_recv()
        for v in range(parts):
            units[i, v] = (acc[v, sum_rows(i, me.c), :] + came[i, v].astype(F32)).astype(BF16)
        keep(i).start()
    for t in range(tiles):
        for k in range(3):
            grad_from(k, t).wait_recv()
            grad_to(k, t).wait_send()
            att_to(k, t).wait_send()
        grad_own(t).wait()
    for j in range(groups):
        push(j).wait_send()
        give(j).wait_send()
        keep(j).wait()


def middle_part(attended, tok, cot, cot_came, b_out, gain, shift, b_up, b_down, weights):
    rows = tok.shape[0]
    width = attended.shape[1]
    groups = len(weights)
    parts, piece, _ = weights[0].shape
    tiles = rows // ROWS_MID
    shape = jax.ShapeDtypeStruct
    halves = (groups, parts, piece, D)
    return pl.pallas_call(
        middle_kernel,
        name="middle_part",
        cost_estimate=work(50),
        in_specs=[ANY] + [VMEM] * 8 + [ANY] * groups,
        out_specs=[VMEM, VMEM, ANY, ANY],
        out_shape=[
            shape((rows, D), BF16),
            shape((rows, D), F32),
            shape((4 * rows, width), BF16),
            shape(halves, BF16),
        ],
        scratch_shapes=[
            pltpu.VMEM((parts, rows, width), BF16),
            pltpu.VMEM((parts, rows, width), BF16),
            pltpu.VMEM((parts, UNITS, D), BF16),
            pltpu.VMEM((parts, UNITS, D), F32),
            pltpu.VMEM((8, D), F32),
            pltpu.VMEM((parts, 1, UP_ROWS), F32),
            pltpu.VMEM(halves, BF16),
            pltpu.VMEM(halves, BF16),
            pltpu.VMEM(halves, BF16),
            DMA((3, tiles)),
            DMA((3, tiles)),
            DMA((tiles,)),
            DMA((3, tiles)),
            DMA((3, tiles)),
            DMA((tiles,)),
        ]
        + [DMA((groups,))] * 6,
        compiler_params=pltpu.CompilerParams(
            collective_id=2, has_side_effects=True, vmem_limit_bytes=60 << 20
        ),
    )(attended, tok, cot, cot_came, b_out, gain, shift, b_up, b_down, *weights)


def finish_kernel(
    dproj_in, normed_in, full_in, w, grad_mid, gain, cells, grad, vec_sum, d_w, sums,
    dproj, normed, full, part, theirs, sent, crossed, low, acc, w_part, w_in, w_z, vec, vz, vd, u_in, u_own,
    load_s, out_s, sib_s, sib_r, cross_s, cross_r, swap_s, swap_r, vz_s, vz_r, vd_s, vd_r,
    ws_s, ws_r, wz_s, wz_r, wg_s, wg_r, wf_s, wf_r, uz_s, uz_r, ug_s, ug_r, uf_s, uf_r,
):
    me = Place()
    foreign = jnp.logical_not(me.native)
    rows = grad_mid.shape[0]
    piece = rows // PIECES
    width = w.shape[1]
    ndp = vd.shape[0]
    groups, w_rows, _ = w_part.shape
    group = me.d // 2

    order = [2 * (1 - me.hf) + 1 - me.r, 2 * (1 - me.hf) + me.r, 2 * me.hf + 1 - me.r, 2 * me.hf + me.r]

    def span_of(k, p):
        return pl.ds(pl.multiple_of(order[k] * rows + p * piece, 16), piece)

    def loads(k, p):
        span = span_of(k, p)
        pairs = ((dproj_in.at[:, span], dproj.at[:, span]), (normed_in.at[span], normed.at[span]), (full_in.at[span], full.at[span]))
        return [pltpu.make_async_copy(src, dst, load_s.at[k, p, j]) for j, (src, dst) in enumerate(pairs)]

    for k in range(4):
        for p in range(PIECES):
            for copy in loads(k, p):
                copy.start()

    around = [(me.d, lax.rem(me.m + k, 4)) for k in range(1, 4)]
    along = [(lax.rem(me.d + k, ndp), me.m) for k in range(1, ndp)]
    greet([me.partner] + around + along)

    def to_sib(k, p):
        slot = k % 2
        return remote(part.at[k, p], theirs.at[slot, p], sib_s.at[slot, p], sib_r.at[slot, p], me.sibling)

    def to_cross(p):
        return remote(sent.at[p], crossed.at[p], cross_s.at[p], cross_r.at[p], me.cross)

    def to_partner(p):
        return remote(low.at[p], grad.at[p], swap_s.at[p], swap_r.at[p], me.partner)

    def keep(p):
        return pltpu.make_async_copy(low.at[p], grad.at[p], out_s.at[p])

    def unit_z(j):
        to = lax.rem(me.m + 1 + j, 4)
        return remote(cells.at[to], u_in.at[j], uz_s.at[j], uz_r.at[j], around[j])

    def unit_give(j):
        to = (2 * lax.rem(group + j, groups) + me.c, me.m)
        return remote(u_own, sums.at[me.d], ug_s.at[j], ug_r.at[j], to)

    def unit_give_in(j):
        source = 2 * lax.rem(group + groups - j, groups) + me.c
        return remote(u_own, sums.at[source], ug_s.at[j], ug_r.at[j], (source, me.m))

    def unit_forward(j):
        source = 2 * lax.rem(group + groups - j, groups) + me.c
        src = u_own if j == 0 else sums.at[source]
        return remote(src, sums.at[source], uf_s.at[j], uf_r.at[j], me.sibling)

    def unit_forward_in(j):
        source = 2 * lax.rem(group + groups - j, groups) + 1 - me.c
        return remote(u_own, sums.at[source], uf_s.at[j], uf_r.at[j], me.sibling)

    vec[...] = jnp.zeros_like(vec)

    def compute(k):
        def one(p, _):
            span = span_of(k, p)
            for copy in loads(k, p):
                copy.wait()
            total = jnp.zeros((piece, D), F32)
            for c in range(3):
                total = total + dot(dproj[c, span, :], w[c])
            part[k, p] = total.astype(BF16)

            @pl.when(me.native if k < 2 else foreign)
            def _():
                to_sib(k, p).start()

            return 0

        lax.fori_loop(0, PIECES, one, 0)

    def pass_across(k):
        for p in range(PIECES):
            to_sib(k, p).wait_recv()
            sent[p] = (part[k, p].astype(F32) + theirs[0, p].astype(F32)).astype(BF16)
            to_cross(p).start()

    def conclude(k, p):
        to_sib(k, p).wait_recv()
        to_cross(p).wait_recv()
        total = part[k, p].astype(F32) + theirs[1, p].astype(F32) + crossed[p].astype(F32)
        span = pl.ds(pl.multiple_of(me.q * rows + p * piece, 16), piece)
        unit, scale = normalise(full[span, :].astype(F32))
        vec[0:1] += jnp.sum(total * unit, axis=0, keepdims=True)
        vec[1:2] += jnp.sum(total, axis=0, keepdims=True)
        scaled = total * line(gain)
        result = grad_mid[p * piece : (p + 1) * piece, :] + scale * (
            scaled
            - jnp.mean(scaled, axis=-1, keepdims=True)
            - unit * jnp.mean(scaled * unit, axis=-1, keepdims=True)
        )
        low[p] = result.astype(BF16)

    def conclude_foreign(p):
        conclude(1, p)
        to_partner(p).start()

    compute(0)

    @pl.when(foreign)
    def _():
        pass_across(0)

    compute(1)
    compute(2)

    @pl.when(me.native)
    def _():
        pass_across(2)

    compute(3)
    for j in range(3):
        unit_z(j).start()

    for c in range(3):
        acc[c * width : (c + 1) * width, :] = dot(dproj[c], normed[...], TN)

    for i in range(groups):
        w_part[i] = acc[i * w_rows : (i + 1) * w_rows, :].astype(BF16)

    def other_group(k):
        return lax.rem(group + k, groups)

    def w_send(k):
        to = other_group(k)
        return remote(w_part.at[to], w_in.at[k], ws_s.at[k], ws_r.at[k], (2 * to + me.c, me.m))

    for k in range(1, groups):
        w_send(k).start()

    @pl.when(foreign)
    def _():
        conclude_foreign(0)
        conclude_foreign(1)

    w_sum = w_part[group].astype(F32)
    for k in range(1, groups):
        w_send(k).wait_recv()
        w_sum = w_sum + w_in[k].astype(F32)

    to_z = remote(w_z.at[0], w_z.at[1], wz_s, wz_r, (me.d, lax.rem(me.m + 2, 4)))

    def w_give(k):
        return remote(w_z.at[0], d_w.at[group], wg_s.at[k], wg_r.at[k], (2 * other_group(k) + me.c, me.m))

    def w_give_in(k):
        source = lax.rem(group + groups - k, groups)
        return remote(w_z.at[0], d_w.at[source], wg_s.at[k], wg_r.at[k], (2 * source + me.c, me.m))

    def w_forward(k):
        source = lax.rem(group + groups - k, groups)
        src = w_z.at[0] if k == 0 else d_w.at[source]
        return remote(src, d_w.at[source], wf_s.at[k], wf_r.at[k], me.sibling)

    w_keep = pltpu.make_async_copy(w_z.at[0], d_w.at[group], out_s.at[PIECES])
    unit_keep = pltpu.make_async_copy(u_own, sums.at[me.d], out_s.at[PIECES + 1])

    @pl.when(foreign)
    def _():
        w_z[0] = w_sum.astype(BF16)
        to_z.start()
        conclude_foreign(2)

    @pl.when(me.native)
    def _():
        to_z.wait_recv()
        w_z[0] = (w_sum + w_z[1].astype(F32)).astype(BF16)
        w_keep.start()
        for k in range(1, groups):
            w_give(k).start()
        w_forward(0).start()
        for p in range(PIECES):
            conclude(3, p)
            keep(p).start()

    vz[me.m] = vec[...]

    def around_copy(k):
        return remote(vz.at[me.m], vz.at[me.m], vz_s.at[k], vz_r.at[k], around[k])

    for k in range(3):
        around_copy(k).start()

    unit_sum = cells[me.m].astype(F32)
    for j in range(3):
        unit_z(j).wait_recv()
        unit_sum = unit_sum + u_in[j].astype(F32)
    u_own[...] = unit_sum.astype(BF16)
    unit_keep.start()
    for j in range(1, groups):
        unit_give(j).start()
    unit_forward(0).start()

    @pl.when(me.native)
    def _():
        for k in range(1, groups):
            w_give_in(k).wait_recv()
            w_forward(k).start()

    for k in range(3):
        source = lax.rem(me.m + 3 - k, 4)
        remote(vz.at[source], vz.at[source], vz_s.at[k], vz_r.at[k], around[k]).wait_recv()
    vd[me.d] = vz[0] + vz[1] + vz[2] + vz[3]

    def along_copy(k):
        return remote(vd.at[me.d], vd.at[me.d], vd_s.at[k], vd_r.at[k], along[k])

    for k in range(ndp - 1):
        along_copy(k).start()

    for j in range(1, groups):
        unit_give_in(j).wait_recv()
        unit_forward(j).start()
    for k in range(ndp - 1):
        source = lax.rem(me.d + ndp - 1 - k, ndp)
        remote(vd.at[source], vd.at[source], vd_s.at[k], vd_r.at[k], along[k]).wait_recv()
    total = vd[0]
    for i in range(1, ndp):
        total = total + vd[i]
    vec_sum[...] = total
    for j in range(groups):
        unit_forward_in(j).wait_recv()

    @pl.when(foreign)
    def _():
        for k in range(groups):
            source = lax.rem(group + groups - k, groups)
            remote(w_z.at[0], d_w.at[source], wf_s.at[k], wf_r.at[k], me.sibling).wait_recv()
        for p in range(PIECES):
            to_partner(p).wait_recv()
            to_partner(p).wait_send()
            to_sib(2, p).wait_send()
            to_sib(3, p).wait_send()
        to_z.wait_send()

    @pl.when(me.native)
    def _():
        for p in range(PIECES):
            keep(p).wait()
            to_sib(0, p).wait_send()
            to_sib(1, p).wait_send()
        for k in range(1, groups):
            w_give(k).wait_send()
        for k in range(groups):
            w_forward(k).wait_send()
        w_keep.wait()

    for p in range(PIECES):
        to_cross(p).wait_send()
    for k in range(1, groups):
        w_send(k).wait_send()
    for k in range(3):
        around_copy(k).wait_send()
        unit_z(k).wait_send()
    for k in range(ndp - 1):
        along_copy(k).wait_send()
    for j in range(groups):
        unit_forward(j).wait_send()
    for j in range(1, groups):
        unit_give(j).wait_send()
    unit_keep.wait()


def finish(dproj, normed, full, w, grad_mid, gain, cells, ndp):
    rows = grad_mid.shape[0]
    total = full.shape[0]
    piece = rows // PIECES
    pieces = (PIECES, piece, D)
    groups = ndp // 2
    columns = 3 * w.shape[1]
    cut = (groups, columns // groups, D)
    unit = cells.shape[1:]
    shape = jax.ShapeDtypeStruct
    return pl.pallas_call(
        finish_kernel,
        name="finish",
        cost_estimate=work(60),
        in_specs=[ANY] * 3 + [VMEM] * 4,
        out_specs=[ANY, VMEM, ANY, ANY],
        out_shape=[shape(pieces, BF16), shape((8, D), F32), shape(cut, BF16), shape((ndp,) + unit, BF16)],
        scratch_shapes=[
            pltpu.VMEM((3, total, w.shape[1]), BF16),
            pltpu.VMEM((total, D), BF16),
            pltpu.VMEM((total, D), BF16),
            pltpu.VMEM((4,) + pieces, BF16),
            pltpu.VMEM((2,) + pieces, BF16),
            pltpu.VMEM(pieces, BF16),
            pltpu.VMEM(pieces, BF16),
            pltpu.VMEM(pieces, BF16),
            pltpu.VMEM((columns, D), F32),
            pltpu.VMEM(cut, BF16),
            pltpu.VMEM(cut, BF16),
            pltpu.VMEM((2,) + cut[1:], BF16),
            pltpu.VMEM((8, D), F32),
            pltpu.VMEM((4, 8, D), F32),
            pltpu.VMEM((ndp, 8, D), F32),
            pltpu.VMEM((3,) + unit, BF16),
            pltpu.VMEM(unit, BF16),
            DMA((4, PIECES, 3)),
            DMA((PIECES + 2,)),
        ]
        + [DMA((2, PIECES))] * 2
        + [DMA((PIECES,))] * 4
        + [DMA((3,))] * 2
        + [DMA((ndp - 1,))] * 2
        + [DMA((groups,))] * 2
        + [DMA] * 2
        + [DMA((groups,))] * 4
        + [DMA((3,))] * 2
        + [DMA((groups,))] * 4,
        compiler_params=pltpu.CompilerParams(
            collective_id=4, has_side_effects=True, vmem_limit_bytes=60 << 20
        ),
    )(dproj, normed, full, w, grad_mid, gain, cells)


def outputs_kernel(
    width, layer, layer_came, grads, w_sums, unit_sums, vec_one,
    layer_out, tokens_grad, d_qkv, d_out, d_up, d_down, d_vecs, d_bup, d_ones, rows_of,
):
    me = Place()
    layer_out[...] = jnp.where(me.native, layer[...], layer_came[...])
    piece = grads.shape[1]
    for p in range(grads.shape[0]):
        tokens_grad[p * piece : (p + 1) * piece, :] = grads[p].astype(F32)
    groups, height, _ = w_sums.shape
    for i in range(groups):
        rows_of[i * height : (i + 1) * height, :] = w_sums[i].astype(F32)
    for c in range(3):
        d_qkv[c] = rows_of[c * width : (c + 1) * width, :]
    ndp, height, _ = unit_sums.shape
    for i in range(ndp):
        rows_of[i * height : (i + 1) * height, :] = unit_sums[i].astype(F32)
    d_out[...] = rows_of[:OUT_ROWS, :]
    d_down[...] = rows_of[OUT_ROWS : OUT_ROWS + UP_ROWS, :]
    d_up[...] = rows_of[OUT_ROWS + UP_ROWS : VEC_AT, :].T
    for i, ref in enumerate(d_vecs):
        ref[...] = rows_of[VEC_AT + i, :]
    d_bup[...] = rows_of[VEC_AT + 4, :UP_ROWS]
    for i, ref in enumerate(d_ones):
        ref[...] = vec_one[i, :]


def outputs(layer, layer_came, grads, w_sums, unit_sums, vec_one):
    rows = layer.shape[0]
    width = w_sums.shape[0] * w_sums.shape[1] // 3
    shape = lambda *s: jax.ShapeDtypeStruct(s, F32)

    def kernel(*refs):
        outs = refs[6:-1]
        outputs_kernel(width, *refs[:6], *outs[:6], outs[6:10], outs[10], outs[11:13], refs[-1])

    return pl.pallas_call(
        kernel,
        name="outputs",
        in_specs=[VMEM] * 6,
        out_specs=[VMEM] * 13,
        out_shape=[
            jax.ShapeDtypeStruct((rows, D), BF16),
            shape(rows, D),
            shape(3, width, D),
            shape(OUT_ROWS, D),
            shape(D, UP_ROWS),
            shape(UP_ROWS, D),
            shape(D),
            shape(D),
            shape(D),
            shape(D),
            shape(UP_ROWS),
            shape(D),
            shape(D),
        ],
        scratch_shapes=[pltpu.VMEM((UNITS, D), F32)],
        compiler_params=limit(48),
    )(layer, layer_came, grads, w_sums, unit_sums, vec_one)


def swap_pairs(ndp):
    return [
        (d * 4 + m, (d ^ 1) * 4 + (m + 2) % 4) for d in range(ndp) for m in range(4) if d % 2 != m // 2
    ]


def weight_piece(w_out, w_up, w_down, ndp):
    block = jnp.concatenate([w_out, w_down, w_up.T, jnp.zeros((UNITS - w_out.shape[0] - 2 * w_down.shape[0], D), BF16)])
    piece = UNITS // ndp
    return lax.dynamic_slice_in_dim(block, lax.axis_index("dp") * piece, piece, 0)


def from_other_pairs(block, ndp):
    groups = ndp // 2
    blocks_of = [block]
    for j in range(1, groups):
        pairs = [(d, 2 * ((d // 2 + j) % groups) + d % 2) for d in range(ndp)]
        blocks_of.append(lax.ppermute(block, "dp", pairs))
    return blocks_of


def sum_over_pairs(cells, ndp):
    cores = [[d for d in range(ndp) if d % 2 == core] for core in range(2)]
    return lax.psum_scatter(cells.reshape(-1, D), "dp", scatter_dimension=0, tiled=True, axis_index_groups=cores)


def shards(
    tokens,
    scene_ids,
    gain_one,
    shift_one,
    w_qkv,
    w_out,
    b_out,
    gain_two,
    shift_two,
    w_up,
    b_up,
    w_down,
    b_down,
    cotangent,
    ndp,
):
    both = ("dp", "mp")
    swap = swap_pairs(ndp)
    w_qkv = jnp.swapaxes(w_qkv, 1, 2)
    full, own_tok, w_mine, numbers, id_row, id_column, before, b_ups, normed, q, k, v, kt, vt, weights = start(
        tokens, w_qkv, scene_ids.reshape(-1, LANES), b_up, gain_one, shift_one, weight_piece(w_out, w_up, w_down, ndp), ndp
    )
    w_mine = w_mine.reshape(w_qkv.shape)
    ids = numbers, before, id_column, id_row
    weights = from_other_pairs(weights, ndp)
    sent_cot, q = lax.optimization_barrier((cotangent, q))
    cot_came = lax.ppermute(sent_cot, both, swap)
    attended, lse = attention(ids, q, k, vt)
    layer, grad_mid, grad_heads, cells = middle_part(
        attended, own_tok, cotangent, cot_came, b_out, gain_two, shift_two, b_ups, b_down, weights
    )
    sent_out, grad_heads = lax.optimization_barrier((layer, grad_heads))
    layer_came = lax.ppermute(sent_out, both, swap)
    cells = sum_over_pairs(cells, ndp)
    dproj = attention_back(ids, q, k, v, kt, attended, grad_heads, lse)
    cells, dproj = lax.optimization_barrier((cells, dproj))
    grads, vec_one, w_sums, unit_sums = finish(
        dproj, normed, full, w_mine, grad_mid, gain_one, cells.reshape(4, -1, D), ndp
    )
    (
        layer_out, tokens_grad, d_qkv, d_out, d_up, d_down, d_gain_two, d_shift_two, d_b_out, d_b_down, d_b_up, d_gain_one, d_shift_one,
    ) = outputs(layer, layer_came, grads, w_sums, unit_sums, vec_one)
    return (
        layer_out,
        tokens_grad,
        d_gain_one,
        d_shift_one,
        jnp.swapaxes(d_qkv, 1, 2),
        d_out,
        d_b_out,
        d_gain_two,
        d_shift_two,
        d_up,
        d_b_up,
        d_down,
        d_b_down,
    )


def solution(mesh):
    ndp = mesh.shape["dp"]
    return jax.shard_map(
        functools.partial(shards, ndp=ndp),
        mesh=mesh,
        in_specs=(
            P(("dp", "mp"), None),
            P("dp"),
            P(),
            P(),
            P(None, None, "mp"),
            P("mp", None),
            P(),
            P(),
            P(),
            P(None, "mp"),
            P("mp"),
            P("mp", None),
            P(),
            P(("dp", "mp"), None),
        ),
        out_specs=(
            P(("dp", "mp"), None),
            P(("dp", "mp"), None),
            P(),
            P(),
            P(None, None, "mp"),
            P("mp", None),
            P(),
            P(),
            P(),
            P(None, "mp"),
            P("mp"),
            P("mp", None),
            P(),
        ),
        check_vma=False,
    )
```

time: 360 us -> 327 us (0.908)
  local copies, waits for them, and re-layouts: 28.6 us -> 7.03 us
  Pallas kernels: 302 us -> 285 us
  waiting for transfers between devices: 2.12 us -> 6.72 us
    slice x7 -> x0, local copies, waits for them, and re-layouts: 9.15 us -> none  [the longest x1 2.79 us: shards(): sums[OUT_ROWS:OUT_ROWS + UP_ROWS]]
    pallas_call x1, Pallas kernels: 33.4 us -> 25.6 us  [attention(): pl.pallas_call(functools.partial(attention_kernel, heads, total), name='a...]
    pallas_call x1, Pallas kernels: 88.8 us -> 81.2 us  [finish(): pl.pallas_call(finish_kernel, name='finish', cost_estimate=work(60), in_s...]
    ppermute x2 -> x5, waiting for transfers between devices: 0.01 us -> 6.7 us  [the longest x3 4.8 us: from_other_pairs(): blocks_of.append(lax.ppermute(block, 'dp', pairs))]
    pallas_call x1, Pallas kernels: 59.1 us -> 53.1 us  [attention_back(): pl.pallas_call(functools.partial(attention_back_kernel, heads, total), na...]
    pallas_call x0 -> x1, Pallas kernels: none -> 5.31 us  [outputs(): pl.pallas_call(kernel, name='outputs', in_specs=[VMEM] * 6, out_specs=[VM...]
    reshape x7 -> x0, local copies, waits for them, and re-layouts: 4.74 us -> none  [the longest x6 4.17 us: shards(): line = lambda v: v.reshape(1, D)]
    select_n x4 -> x0, other arithmetic: 3.66 us -> none  [the longest x1 1.2 us: shards(): layer_out = jnp.where(native, layer_out, lax.ppermute(sent_out, both, swap))]
  transfers between devices with their start and end apart: 4 -> 6, of which waited for: 1 -> 2; matrix products, arithmetic and copies ran while one was open for 3% -> 0% of each run, Pallas kernels for 26% -> 49%
where the time goes in v4:
time: 327 us; the launch traced here: 324 us
  Pallas kernels  285 us (87%)
  between operations  14.2 us (4%)
  starting transfers between devices  8.85 us (3%)
  local copies, waits for them, and re-layouts  7.03 us (2%)
  waiting for transfers between devices  6.72 us (2%)
    pallas_call x1, Pallas kernels, finish(): pl.pallas_call(finish_kernel, name='finish', cost_estimate=work(60), in_s...  81.2 us
    pallas_call x1, Pallas kernels, start(): pl.pallas_call(functools.partial(start_kernel, heads), name='start', cost...  69.9 us
    pallas_call x1, Pallas kernels, attention_back(): pl.pallas_call(functools.partial(attention_back_kernel, heads, total), na...  53.1 us
    pallas_call x1, Pallas kernels, middle_part(): pl.pallas_call(middle_kernel, name='middle_part', cost_estimate=work(50),...  50.1 us
    pallas_call x1, Pallas kernels, attention(): pl.pallas_call(functools.partial(attention_kernel, heads, total), name='a...  25.6 us
    unnamed x21, local copies, waits for them, and re-layouts  6.94 us
  transfers between devices with their start and end apart: 6, of which 2 were waited for; matrix products, arithmetic and copies ran while one was open for 0% of the time, Pallas kernels for 49%

profile of v4, /device:TPU:1, one launch (start us, length us, event | category | flops | bytes accessed | tf_op | source)
XLA Modules:
  0.0 323.7 jit_solution(5098805306489842338)
XLA Ops:
  7.2 0.0 reduce-scatter.2.cloned.1.call-start
  7.2 1.4 copy.27
  8.6 0.1 pad_dynamic-slice_fusion.3
  8.7 1.7 fusion.2.mine
  10.4 69.9 %start.1 = (bf16[3456,768]{1,0:T(8,128)(2,1)}, bf16[864,768]{1,0:T(8,128)(2,1)}, bf16[3,4,48,768]{3,2,1,0:T(8,128)(2,1)}, s32[27,128]{1,0:T(8,128)}, s32[1,3968]...) custom-call(bf16[864,768]{1,0:T(8,128)(2,1)} %tok.1, ...), custom_call_target="tpu_custom_call" | custom-call | flops 49999998976 | bytes 150000000 | tf_op jit(solution)/shard_map/start/pallas_call | solution.py:388
  80.4 1.3 collective-permute-start.3
  81.7 0.2 collective-permute-start.2
  81.9 0.3 collective-permute-start.1
  82.2 2.2 collective-permute-start
  84.4 25.6 %attention.1 = (bf16[3584,192]{1,0:T(8,128)(2,1)}, f32[3,3968]{1,0:T(4,128)}) custom-call(s32[27,128]{1,0:T(8,128)} %get-tuple-element.57.numbers, s32[1,128]{1,0:T(1,128)} %get-tuple-element.58.before, s32[3968,1]{1,0:T(8,128)} %get-tuple-element.59.idc, s32[1,3968]{1,0:T(1,128)} %get-tuple-element.60.idr, bf16[3,3968,128]{2,1,0:T(8,128)(2,1)} %get-tuple-element.62.q, ...), custom_call_target="tpu_custom_call" | custom-call | flops 31000000512 | bytes 93000000 | tf_op jit(solution)/shard_map/attention/pallas_call | solution.py:533
  110.0 0.0 copy-start.8
  110.0 4.8 %collective-permute-done.1.rest_1_ = bf16[4,128,768]{2,1,0:T(8,128)(2,1)S(1)} collective-permute-done((bf16[4,128,768]{2,1,0:T(8,128)(2,1)}, bf16[4,128,768]{2,1,0:T(8,128)(2,1)S(1)}, u32[]{:S(2)}, u32[]{:S(2)}) %collective-permute-start.1) | collective-permute-done | bytes 786464 | tf_op jit(solution)/shard_map/ppermute | solution.py:1275
  114.8 1.9 collective-permute-done.cot_came
  116.7 1.1 copy-done.6
  117.8 50.1 %middle_part.1 = (bf16[864,768]{1,0:T(8,128)(2,1)}, f32[864,768]{1,0:T(8,128)}, bf16[3456,192]{1,0:T(8,128)(2,1)}, bf16[4,4,128,768]{3,2,1,0:T(8,128)(2,1)}) custom-call(bf16[3584,192]{1,0:T(8,128)(2,1)} %get-tuple-element.65.attended.out, bf16[864,768]{1,0:T(8,128)(2,1)} %get-tuple-element.66.tok, bf16[864,768]{1,0:T(8,128)(2,1)} %cot.1, ...), custom_call_target="tpu_custom_call" | custom-call | flops 49999998976 | bytes 150000000 | tf_op jit(solution)/shard_map/middle_part/pallas_call | solution.py:828
  167.9 0.0 reduce-scatter.2.cloned.1.call-update
  167.9 1.3 copy-done
  169.2 4.8 %collective-permute-start.4 = (bf16[864,768]{1,0:T(8,128)(2,1)S(1)}, bf16[864,768]{1,0:T(8,128)(2,1)S(1)}, u32[]{:S(2)}, u32[]{:S(2)}) collective-permute-start(bf16[864,768]{1,0:T(8,128)(2,1)S(1)} %copy-done), channel_id=1, source_target_pairs={{2,4},{3,5},{4,2},{5,3},{10,12},{11,13},{12,10},{13,11},{18,20},{1... | collective-permute-start | bytes 3981320 | tf_op jit(solution)/shard_map/ppermute | solution.py:1317
  174.0 53.1 %attention_back.1.dproj_in = bf16[3,3584,192]{2,1,0:T(8,128)(2,1)} custom-call(s32[27,128]{1,0:T(8,128)} %get-tuple-element.57.numbers, s32[1,128]{1,0:T(1,128)} %get-tuple-element.58.before, s32[3968,1]{1,0:T(8,128)} %get-tuple-element.59.idc, s32[1,3968]{1,0:T(1,128)} %get-tuple-element.60.idr, bf16[3,3968,128]{2,1,0:T(8,128)(2,1)} %get-tuple-element.62.q, ...), custom_call_target="tpu_custom_call" | custom-call | flops 51000000512 | bytes 153000000 | tf_op jit(solution)/shard_map/attention_back/pallas_call | solution.py:629
  227.1 81.2 %finish.1 = (bf16[3,288,768]{2,1,0:T(8,128)(2,1)}, f32[8,768]{1,0:T(8,128)}, bf16[4,144,768]{2,1,0:T(8,128)(2,1)}, bf16[8,128,768]{2,1,0:T(8,128)(2,1)}) custom-call(bf16[3,3584,192]{2,1,0:T(8,128)(2,1)} %attention_back.1.dproj_in, bf16[3456,768]{1,0:T(8,128)(2,1)} %get-tuple-element.79.normed_in, bf16[3456,768]{1,0:T(8,128)(2,1)} %get-tuple-element.80.full_in, ...), custom_call_target="tpu_custom_call" | custom-call | flops 60000002048 | bytes 180000000 | tf_op jit(solution)/shard_map/finish/pallas_call | solution.py:1154
  308.3 1.3 copy-done.1
  309.7 1.2 copy-done.2
  310.8 0.7 copy-done.3
  311.6 5.3 %outputs.1 = (bf16[864,768]{1,0:T(8,128)(2,1)}, f32[864,768]{1,0:T(8,128)}, f32[3,192,768]{2,1,0:T(8,128)}, f32[192,768]{1,0:T(8,128)}, f32[768,384]{1,0:T(8,128...) custom-call(bf16[864,768]{1,0:T(8,128)(2,1)S(1)} %copy-done, ...), custom_call_target="tpu_custom_call" | custom-call | tf_op jit(solution)/shard_map/outputs/pallas_call | solution.py:1233
  (19 shorter events, 0.0 us)
Async XLA Ops:
  7.2 1.5 copy-start.4
  7.2 219.9 %reduce-scatter.2.cloned.1.call-start = ((), (), s32[]{:S(2)}) async-start(), calls=%async_computation.1 | async-start | bytes 3932160 | tf_op jit(solution)/shard_map/reduce_scatter | solution.py:1281
  10.4 71.8 %copy-start.5 = (bf16[864,768]{1,0:T(8,128)(2,1)S(1)}, bf16[864,768]{1,0:T(8,128)(2,1)}, u32[]{:S(2)}) copy-start(bf16[864,768]{1,0:T(8,128)(2,1)} %cot.1) | copy-start | bytes 3981316
  80.4 29.6 %collective-permute-start.3 = (bf16[4,128,768]{2,1,0:T(8,128)(2,1)}, bf16[4,128,768]{2,1,0:T(8,128)(2,1)S(1)}, u32[]{:S(2)}, u32[]{:S(2)}) collective-permute-start(bf16[4,128,768]{2,1,0:T(8,128)(2,1)} %get-tuple-element.69.rest_0_), channel_id=1, source_target_pairs={{0,24},{4,28},{8,0},{12,4},{16,8},{20,12},{24,16},{28,20},{1,25},{... | collective-permute-start | bytes 2359304 | tf_op jit(solution)/shard_map/ppermute | solution.py:1275
  81.7 28.3 %collective-permute-start.2 = (bf16[4,128,768]{2,1,0:T(8,128)(2,1)}, bf16[4,128,768]{2,1,0:T(8,128)(2,1)S(1)}, u32[]{:S(2)}, u32[]{:S(2)}) collective-permute-start(bf16[4,128,768]{2,1,0:T(8,128)(2,1)} %get-tuple-element.69.rest_0_), channel_id=1, source_target_pairs={{0,16},{4,20},{8,24},{12,28},{16,0},{20,4},{24,8},{28,12},{1,17},{... | collective-permute-start | bytes 2359304 | tf_op jit(solution)/shard_map/ppermute | solution.py:1275
  81.9 32.9 %collective-permute-start.1 = (bf16[4,128,768]{2,1,0:T(8,128)(2,1)}, bf16[4,128,768]{2,1,0:T(8,128)(2,1)S(1)}, u32[]{:S(2)}, u32[]{:S(2)}) collective-permute-start(bf16[4,128,768]{2,1,0:T(8,128)(2,1)} %get-tuple-element.69.rest_0_), channel_id=1, source_target_pairs={{0,8},{4,12},{8,16},{12,20},{16,24},{20,28},{24,0},{28,4},{1,9},{5... | collective-permute-start | bytes 2359304 | tf_op jit(solution)/shard_map/ppermute | solution.py:1275
  82.2 34.5 %collective-permute-start = (bf16[864,768]{1,0:T(8,128)(2,1)S(1)}, bf16[864,768]{1,0:T(8,128)(2,1)S(1)}, u32[]{:S(2)}, u32[]{:S(2)}) collective-permute-start(bf16[864,768]{1,0:T(8,128)(2,1)S(1)} %copy-done.5), channel_id=1, source_target_pairs={{2,4},{3,5},{4,2},{5,3},{10,12},{11,13},{12,10},{13,11},{18,20},{1... | collective-permute-start | bytes 3981320 | tf_op jit(solution)/shard_map/ppermute | solution.py:1311
  110.0 6.7 %copy-start.7 = (bf16[4,128,768]{2,1,0:T(8,128)(2,1)}, bf16[4,128,768]{2,1,0:T(8,128)(2,1)S(1)}, u32[]{:S(2)}) copy-start(bf16[4,128,768]{2,1,0:T(8,128)(2,1)S(1)} %collective-permute-done.3.rest_3_) | copy-start | bytes 2359300
  110.0 6.7 %copy-start.8 = (bf16[4,128,768]{2,1,0:T(8,128)(2,1)}, bf16[4,128,768]{2,1,0:T(8,128)(2,1)S(1)}, u32[]{:S(2)}) copy-start(bf16[4,128,768]{2,1,0:T(8,128)(2,1)S(1)} %collective-permute-done.2.rest_2_) | copy-start | bytes 2359300
  114.8 1.9 copy-start.9
  116.7 1.1 copy-start.6
  167.9 1.3 copy-start
  169.2 139.1 %collective-permute-start.4 = (bf16[864,768]{1,0:T(8,128)(2,1)S(1)}, bf16[864,768]{1,0:T(8,128)(2,1)S(1)}, u32[]{:S(2)}, u32[]{:S(2)}) collective-permute-start(bf16[864,768]{1,0:T(8,128)(2,1)S(1)} %copy-done), channel_id=1, source_target_pairs={{2,4},{3,5},{4,2},{5,3},{10,12},{11,13},{12,10},{13,11},{18,20},{1... | collective-permute-start | bytes 3981320 | tf_op jit(solution)/shard_map/ppermute | solution.py:1317
  308.3 1.3 copy-start.1
  309.7 1.2 copy-start.2
  310.8 0.7 copy-start.3
Sparse Core Ops, SparseCore 0:
  168.0 42.1 reduce-scatter.1

commit v5 on v4

--- a/solution.py
+++ b/solution.py
@@ -77,7 +77,8 @@
     )
 
 
-PIECES = 3
+STAGES = 3
+PIECES = 6
 TILE = 384
 SCENES = 4
 
@@ -274,6 +275,9 @@
     for copy in padding:
         copy.start()
 
+    def stage(n):
+        return range(n * PIECES // STAGES, (n + 1) * PIECES // STAGES)
+
     @pl.when(me.native)
     def _():
         for n in range(PIECES):
@@ -303,33 +307,39 @@
 
     @pl.when(foreign)
     def _():
-        pass_on(0)
+        for n in stage(0):
+            pass_on(n)
 
     compute(2, 1, 2)
 
     @pl.when(foreign)
     def _():
-        pass_on(1)
+        for n in stage(1):
+            pass_on(n)
 
     @pl.when(me.native)
     def _():
-        from_sibling(0)
+        for n in stage(0):
+            from_sibling(n)
 
     compute(4, 1, 1)
 
     @pl.when(me.native)
     def _():
-        from_sibling(1)
+        for n in stage(1):
+            from_sibling(n)
 
     compute(5, 2, 2)
 
     @pl.when(foreign)
     def _():
-        pass_on(2)
+        for n in stage(2):
+            pass_on(n)
 
     @pl.when(me.native)
     def _():
-        from_sibling(2)
+        for n in stage(2):
+            from_sibling(n)
 
     own_copy = pltpu.make_async_copy(buf.at[pl.ds(pl.multiple_of(me.q * rows, 16), rows)], own, late_s.at[5])
     w_copy = pltpu.make_async_copy(w, w_out, late_s.at[6])
@@ -553,13 +563,20 @@
 
 
 def attention_back_kernel(
-    heads, total, numbers, before, idc, idr, q, k, v, kt, out, grad, lse, dproj, g, delta, dq
+    heads, total, numbers, before, idc, idr, q_in, k_in, v_in, kt_in, out, grad, lse, dproj,
+    q, k, v, kt, made, g, delta, dq, in_s, out_s,
 ):
     wide = q.shape[1]
     width = heads * HEAD
     head_of = lax.broadcasted_iota(jnp.int32, (8, width), 1) // HEAD
     pick = jnp.where(head_of == lax.broadcasted_iota(jnp.int32, (8, width), 0), 1.0, 0.0).astype(BF16)
     none = jnp.zeros((TILE, LANES - HEAD), BF16)
+    arriving = [
+        pltpu.make_async_copy(src, dst, in_s.at[i])
+        for i, (src, dst) in enumerate(((q_in, q), (k_in, k), (v_in, v), (kt_in, kt)))
+    ]
+    for copy in arriving:
+        copy.start()
 
     def prepare(i, _):
         rows = pl.ds(pl.multiple_of(i * TILE, LANES), TILE)
@@ -580,6 +597,13 @@
     for h in range(heads):
         g[h, total:, :] = jnp.zeros((tail, LANES), BF16)
         dq[h, :, total:] = jnp.zeros((HEAD, tail), F32)
+
+    for copy in arriving:
+        copy.wait()
+
+    def give(i):
+        cols = pl.ds(pl.multiple_of(i * BLOCK, LANES), BLOCK)
+        return pltpu.make_async_copy(made.at[1:3, cols], dproj.at[1:3, cols], out_s.at[i])
 
     def one_block(i, _):
         c0 = pl.multiple_of(i * BLOCK, LANES)
@@ -609,7 +633,8 @@
         done = in_steps(low, high, queries, tuple((zero, zero) for _ in range(heads)))
         for part in range(2):
             joined = jnp.concatenate([done[h][part][:, :HEAD] for h in range(heads)], axis=1)
-            dproj[part + 1, cols, :] = joined.astype(BF16)
+            made[part + 1, cols, :] = joined.astype(BF16)
+        give(i).start()
         return 0
 
     lax.fori_loop(0, blocks(total), one_block, 0)
@@ -617,10 +642,19 @@
     def finish(i, _):
         rows = pl.ds(pl.multiple_of(i * TILE, LANES), TILE)
         joined = jnp.concatenate([dq[h, :, rows] for h in range(heads)], axis=0)
-        dproj[0, rows, :] = (joined * HEAD**-0.5).T.astype(BF16)
+        made[0, rows, :] = (joined * HEAD**-0.5).T.astype(BF16)
+        give_q(i).start()
         return 0
 
+    def give_q(i):
+        rows = pl.ds(pl.multiple_of(i * TILE, LANES), TILE)
+        return pltpu.make_async_copy(made.at[0, rows], dproj.at[0, rows], out_s.at[blocks(total) + i])
+
     lax.fori_loop(0, total // TILE, finish, 0)
+    for i in range(blocks(total)):
+        give(i).wait()
+    for i in range(total // TILE):
+        give_q(i).wait()
 
 
 def attention_back(ids, q, k, v, kt, out, grad, lse):
@@ -630,13 +664,20 @@
         functools.partial(attention_back_kernel, heads, total),
         name="attention_back",
         cost_estimate=work(51),
-        in_specs=[SMEM] * 2 + [VMEM] * 9,
-        out_specs=VMEM,
+        in_specs=[SMEM] * 2 + [VMEM] * 2 + [ANY] * 4 + [VMEM] * 3,
+        out_specs=ANY,
         out_shape=jax.ShapeDtypeStruct((3, blocks(total) * BLOCK, heads * HEAD), BF16),
         scratch_shapes=[
+            pltpu.VMEM(q.shape, BF16),
+            pltpu.VMEM(k.shape, BF16),
+            pltpu.VMEM(v.shape, BF16),
+            pltpu.VMEM(kt.shape, BF16),
+            pltpu.VMEM((3, blocks(total) * BLOCK, heads * HEAD), BF16),
             pltpu.VMEM((heads, wide, LANES), BF16),
             pltpu.VMEM((8, wide), F32),
             pltpu.VMEM((heads, HEAD, wide), F32),
+            DMA((4,)),
+            DMA((blocks(total) + total // TILE,)),
         ],
         compiler_params=limit(60),
     )(*ids, q, k, v, kt, out, grad, lse)
@@ -856,9 +897,12 @@
         ]
         + [DMA((groups,))] * 6,
         compiler_params=pltpu.CompilerParams(
-            collective_id=2, has_side_effects=True, vmem_limit_bytes=60 << 20
+            collective_id=2, has_side_effects=True, vmem_limit_bytes=48 << 20
         ),
     )(attended, tok, cot, cot_came, b_out, gain, shift, b_up, b_down, *weights)
+
+
+CUTS = 3
 
 
 def finish_kernel(
@@ -870,7 +914,7 @@
     me = Place()
     foreign = jnp.logical_not(me.native)
     rows = grad_mid.shape[0]
-    piece = rows // PIECES
+    piece = rows // CUTS
     width = w.shape[1]
     ndp = vd.shape[0]
     groups, w_rows, _ = w_part.shape
@@ -887,7 +931,7 @@
         return [pltpu.make_async_copy(src, dst, load_s.at[k, p, j]) for j, (src, dst) in enumerate(pairs)]
 
     for k in range(4):
-        for p in range(PIECES):
+        for p in range(CUTS):
             for copy in loads(k, p):
                 copy.start()
 
@@ -947,10 +991,10 @@
 
             return 0
 
-        lax.fori_loop(0, PIECES, one, 0)
+        lax.fori_loop(0, CUTS, one, 0)
 
     def pass_across(k):
-        for p in range(PIECES):
+        for p in range(CUTS):
             to_sib(k, p).wait_recv()
             sent[p] = (part[k, p].astype(F32) + theirs[0, p].astype(F32)).astype(BF16)
             to_cross(p).start()
@@ -1010,8 +1054,8 @@
 
     @pl.when(foreign)
     def _():
-        conclude_foreign(0)
-        conclude_foreign(1)
+        for p in range(2 * CUTS // 3):
+            conclude_foreign(p)
 
     w_sum = w_part[group].astype(F32)
     for k in range(1, groups):
@@ -1032,14 +1076,15 @@
         src = w_z.at[0] if k == 0 else d_w.at[source]
         return remote(src, d_w.at[source], wf_s.at[k], wf_r.at[k], me.sibling)
 
-    w_keep = pltpu.make_async_copy(w_z.at[0], d_w.at[group], out_s.at[PIECES])
-    unit_keep = pltpu.make_async_copy(u_own, sums.at[me.d], out_s.at[PIECES + 1])
+    w_keep = pltpu.make_async_copy(w_z.at[0], d_w.at[group], out_s.at[CUTS])
+    unit_keep = pltpu.make_async_copy(u_own, sums.at[me.d], out_s.at[CUTS + 1])
 
     @pl.when(foreign)
     def _():
         w_z[0] = w_sum.astype(BF16)
         to_z.start()
-        conclude_foreign(2)
+        for p in range(2 * CUTS // 3, CUTS):
+            conclude_foreign(p)
 
     @pl.when(me.native)
     def _():
@@ -1049,7 +1094,7 @@
         for k in range(1, groups):
             w_give(k).start()
         w_forward(0).start()
-        for p in range(PIECES):
+        for p in range(CUTS):
             conclude(3, p)
             keep(p).start()
 
@@ -1106,7 +1151,7 @@
         for k in range(groups):
             source = lax.rem(group + groups - k, groups)
             remote(w_z.at[0], d_w.at[source], wf_s.at[k], wf_r.at[k], me.sibling).wait_recv()
-        for p in range(PIECES):
+        for p in range(CUTS):
             to_partner(p).wait_recv()
             to_partner(p).wait_send()
             to_sib(2, p).wait_send()
@@ -1115,7 +1160,7 @@
 
     @pl.when(me.native)
     def _():
-        for p in range(PIECES):
+        for p in range(CUTS):
             keep(p).wait()
             to_sib(0, p).wait_send()
             to_sib(1, p).wait_send()
@@ -1125,7 +1170,7 @@
             w_forward(k).wait_send()
         w_keep.wait()
 
-    for p in range(PIECES):
+    for p in range(CUTS):
         to_cross(p).wait_send()
     for k in range(1, groups):
         w_send(k).wait_send()
@@ -1144,8 +1189,8 @@
 def finish(dproj, normed, full, w, grad_mid, gain, cells, ndp):
     rows = grad_mid.shape[0]
     total = full.shape[0]
-    piece = rows // PIECES
-    pieces = (PIECES, piece, D)
+    piece = rows // CUTS
+    pieces = (CUTS, piece, D)
     groups = ndp // 2
     columns = 3 * w.shape[1]
     cut = (groups, columns // groups, D)
@@ -1176,11 +1221,11 @@
             pltpu.VMEM((ndp, 8, D), F32),
             pltpu.VMEM((3,) + unit, BF16),
             pltpu.VMEM(unit, BF16),
-            DMA((4, PIECES, 3)),
-            DMA((PIECES + 2,)),
+            DMA((4, CUTS, 3)),
+            DMA((CUTS + 2,)),
         ]
-        + [DMA((2, PIECES))] * 2
-        + [DMA((PIECES,))] * 4
+        + [DMA((2, CUTS))] * 2
+        + [DMA((CUTS,))] * 4
         + [DMA((3,))] * 2
         + [DMA((ndp - 1,))] * 2
         + [DMA((groups,))] * 2
@@ -1195,50 +1240,69 @@
 
 
 def outputs_kernel(
-    width, layer, layer_came, grads, w_sums, unit_sums, vec_one,
-    layer_out, tokens_grad, d_qkv, d_out, d_up, d_down, d_vecs, d_bup, d_ones, rows_of,
+    layer, layer_came, grads, w_sums, unit_sums, vec_one,
+    layer_out, tokens_grad, d_qkv, d_out, d_up, d_down, d_gain_two, d_shift_two, d_b_out, d_b_down, d_b_up, d_gain_one, d_shift_one,
+    layer_s, came_s, grads_s, w_s, unit_s, grads_f, w_f, unit_f, up_f, in_s, out_s,
 ):
     me = Place()
-    layer_out[...] = jnp.where(me.native, layer[...], layer_came[...])
-    piece = grads.shape[1]
-    for p in range(grads.shape[0]):
-        tokens_grad[p * piece : (p + 1) * piece, :] = grads[p].astype(F32)
-    groups, height, _ = w_sums.shape
-    for i in range(groups):
-        rows_of[i * height : (i + 1) * height, :] = w_sums[i].astype(F32)
-    for c in range(3):
-        d_qkv[c] = rows_of[c * width : (c + 1) * width, :]
-    ndp, height, _ = unit_sums.shape
-    for i in range(ndp):
-        rows_of[i * height : (i + 1) * height, :] = unit_sums[i].astype(F32)
-    d_out[...] = rows_of[:OUT_ROWS, :]
-    d_down[...] = rows_of[OUT_ROWS : OUT_ROWS + UP_ROWS, :]
-    d_up[...] = rows_of[OUT_ROWS + UP_ROWS : VEC_AT, :].T
-    for i, ref in enumerate(d_vecs):
-        ref[...] = rows_of[VEC_AT + i, :]
-    d_bup[...] = rows_of[VEC_AT + 4, :UP_ROWS]
-    for i, ref in enumerate(d_ones):
-        ref[...] = vec_one[i, :]
+    arriving = [
+        pltpu.make_async_copy(src, dst, in_s.at[i])
+        for i, (src, dst) in enumerate(
+            ((unit_sums, unit_s), (w_sums, w_s), (grads, grads_s), (layer, layer_s), (layer_came, came_s))
+        )
+    ]
+    for copy in arriving:
+        copy.start()
+    leaving = []
+
+    def leave(src, dst):
+        copy = pltpu.make_async_copy(src, dst, out_s.at[len(leaving)])
+        copy.start()
+        leaving.append(copy)
+
+    def flatten(pieces, flat):
+        count, height, _ = pieces.shape
+        for i in range(count):
+            flat[i * height : (i + 1) * height, :] = pieces[i].astype(F32)
+
+    arriving[0].wait()
+    flatten(unit_s, unit_f)
+    leave(unit_f.at[:OUT_ROWS], d_out)
+    leave(unit_f.at[OUT_ROWS : OUT_ROWS + UP_ROWS], d_down)
+    up_f[...] = unit_f[OUT_ROWS + UP_ROWS : VEC_AT, :].T
+    leave(up_f, d_up)
+    arriving[1].wait()
+    flatten(w_s, w_f)
+    leave(w_f, d_qkv)
+    arriving[2].wait()
+    flatten(grads_s, grads_f)
+    leave(grads_f, tokens_grad)
+    for i in (3, 4):
+        arriving[i].wait()
+    layer_s[...] = jnp.where(me.native, layer_s[...], came_s[...])
+    leave(layer_s, layer_out)
+    for i, ref in enumerate((d_gain_two, d_shift_two, d_b_out, d_b_down)):
+        ref[...] = unit_f[VEC_AT + i, :]
+    d_b_up[...] = unit_f[VEC_AT + 4, :UP_ROWS]
+    d_gain_one[...] = vec_one[0, :]
+    d_shift_one[...] = vec_one[1, :]
+    for copy in leaving:
+        copy.wait()
 
 
 def outputs(layer, layer_came, grads, w_sums, unit_sums, vec_one):
     rows = layer.shape[0]
-    width = w_sums.shape[0] * w_sums.shape[1] // 3
+    columns = w_sums.shape[0] * w_sums.shape[1]
     shape = lambda *s: jax.ShapeDtypeStruct(s, F32)
-
-    def kernel(*refs):
-        outs = refs[6:-1]
-        outputs_kernel(width, *refs[:6], *outs[:6], outs[6:10], outs[10], outs[11:13], refs[-1])
-
     return pl.pallas_call(
-        kernel,
+        outputs_kernel,
         name="outputs",
-        in_specs=[VMEM] * 6,
-        out_specs=[VMEM] * 13,
+        in_specs=[ANY] * 5 + [VMEM],
+        out_specs=[ANY] * 6 + [VMEM] * 7,
         out_shape=[
             jax.ShapeDtypeStruct((rows, D), BF16),
             shape(rows, D),
-            shape(3, width, D),
+            shape(columns, D),
             shape(OUT_ROWS, D),
             shape(D, UP_ROWS),
             shape(UP_ROWS, D),
@@ -1250,8 +1314,20 @@
             shape(D),
             shape(D),
         ],
-        scratch_shapes=[pltpu.VMEM((UNITS, D), F32)],
-        compiler_params=limit(48),
+        scratch_shapes=[
+            pltpu.VMEM(layer.shape, BF16),
+            pltpu.VMEM(layer.shape, BF16),
+            pltpu.VMEM(grads.shape, BF16),
+            pltpu.VMEM(w_sums.shape, BF16),
+            pltpu.VMEM(unit_sums.shape, BF16),
+            pltpu.VMEM((rows, D), F32),
+            pltpu.VMEM((columns, D), F32),
+            pltpu.VMEM((UNITS, D), F32),
+            pltpu.VMEM((D, UP_ROWS), F32),
+            DMA((5,)),
+            DMA((6,)),
+        ],
+        compiler_params=limit(60),
     )(layer, layer_came, grads, w_sums, unit_sums, vec_one)
 
 
@@ -1329,7 +1405,7 @@
         tokens_grad,
         d_gain_one,
         d_shift_one,
-        jnp.swapaxes(d_qkv, 1, 2),
+        jnp.swapaxes(d_qkv.reshape(w_qkv.shape), 1, 2),
         d_out,
         d_b_out,
         d_gain_two,

time: 327 us -> 324 us (level); the launches traced: 324 us -> 328 us
  Pallas kernels: 285 us -> 289 us
    pallas_call x1, Pallas kernels: 81.2 us -> 95.4 us  [finish(): pl.pallas_call(finish_kernel, name='finish', cost_estimate=work(60), in_s...]
    pallas_call x1, Pallas kernels: 53.1 us -> 43.6 us  [attention_back(): pl.pallas_call(functools.partial(attention_back_kernel, heads, total), na...]
    unnamed x21 -> x25, local copies, waits for them, and re-layouts: 6.94 us -> 4.64 us
where the time goes in v5:
time: 324 us; the launch traced here: 328 us
  Pallas kernels  289 us (89%)
  between operations  14.3 us (4%)
  starting transfers between devices  9.76 us (3%)
  waiting for transfers between devices  9.07 us (3%)
  local copies, waits for them, and re-layouts  4.73 us (1%)
    pallas_call x1, Pallas kernels, finish(): pl.pallas_call(finish_kernel, name='finish', cost_estimate=work(60), in_s...  95.4 us
    pallas_call x1, Pallas kernels, start(): pl.pallas_call(functools.partial(start_kernel, heads), name='start', cost...  71.4 us
    pallas_call x1, Pallas kernels, middle_part(): pl.pallas_call(middle_kernel, name='middle_part', cost_estimate=work(50),...  48.4 us
    pallas_call x1, Pallas kernels, attention_back(): pl.pallas_call(functools.partial(attention_back_kernel, heads, total), na...  43.6 us
    pallas_call x1, Pallas kernels, attention(): pl.pallas_call(functools.partial(attention_kernel, heads, total), name='a...  23.5 us
    ppermute x3, waiting for transfers between devices, from_other_pairs(): blocks_of.append(lax.ppermute(block, 'dp', pairs))  8.06 us
    pallas_call x1, Pallas kernels, outputs(): pl.pallas_call(outputs_kernel, name='outputs', in_specs=[ANY] * 5 + [VMEM...  6.68 us
  transfers between devices with their start and end apart: 6, of which 2 were waited for; matrix products, arithmetic and copies ran while one was open for 0% of the time, Pallas kernels for 49%

profile of v5, /device:TPU:1, one launch (start us, length us, event | category | flops | bytes accessed | tf_op | source)
XLA Modules:
  0.0 328.5 jit_solution(2196699787377086929)
XLA Ops:
  7.2 0.0 reduce-scatter.2.cloned.1.call-start
  7.2 1.4 copy.27
  8.6 0.1 pad_dynamic-slice_fusion.3
  8.7 1.7 fusion.2.mine
  10.4 71.4 %start.1 = (bf16[3456,768]{1,0:T(8,128)(2,1)}, bf16[864,768]{1,0:T(8,128)(2,1)}, bf16[3,4,48,768]{3,2,1,0:T(8,128)(2,1)}, s32[27,128]{1,0:T(8,128)}, s32[1,3968]...) custom-call(bf16[864,768]{1,0:T(8,128)(2,1)} %tok.1, ...), custom_call_target="tpu_custom_call" | custom-call | flops 49999998976 | bytes 150000000 | tf_op jit(solution)/shard_map/start/pallas_call | solution.py:398
  81.8 1.3 collective-permute-start.3
  83.1 0.2 collective-permute-start.2
  83.3 0.3 collective-permute-start.1
  83.6 1.9 collective-permute-start
  85.6 0.0 copy-start.3
  85.6 0.0 copy-start.4
  85.6 23.5 %attention.1 = (bf16[3584,192]{1,0:T(8,128)(2,1)}, f32[3,3968]{1,0:T(4,128)}) custom-call(s32[27,128]{1,0:T(8,128)} %get-tuple-element.57.numbers, s32[1,128]{1,0:T(1,128)} %get-tuple-element.58.before, s32[3968,1]{1,0:T(8,128)} %get-tuple-element.59.idc, s32[1,3968]{1,0:T(1,128)} %get-tuple-element.60.idr, bf16[3,3968,128]{2,1,0:T(8,128)(2,1)} %get-tuple-element.62.q.q_in, ...), custom_call_target="tpu_custom_call" | custom-call | flops 31000000512 | bytes 93000000 | tf_op jit(solution)/shard_map/attention/pallas_call | solution.py:543
  109.1 8.1 %collective-permute-done.1.rest_1_ = bf16[4,128,768]{2,1,0:T(8,128)(2,1)S(1)} collective-permute-done((bf16[4,128,768]{2,1,0:T(8,128)(2,1)}, bf16[4,128,768]{2,1,0:T(8,128)(2,1)S(1)}, u32[]{:S(2)}, u32[]{:S(2)}) %collective-permute-start.1) | collective-permute-done | bytes 786464 | tf_op jit(solution)/shard_map/ppermute | solution.py:1351
  117.2 1.0 collective-permute-done.cot_came
  118.1 1.1 copy-done.11
  119.2 48.4 %middle_part.1 = (bf16[864,768]{1,0:T(8,128)(2,1)S(1)}, f32[864,768]{1,0:T(8,128)}, bf16[3456,192]{1,0:T(8,128)(2,1)}, bf16[4,4,128,768]{3,2,1,0:T(8,128)(2,1)}) custom-call(bf16[3584,192]{1,0:T(8,128)(2,1)} %get-tuple-element.65.attended.out, bf16[864,768]{1,0:T(8,128)(2,1)S(1)} %copy-done.6, bf16[864,768]{1,0:T(8,128)(2,1)} %cot.1, ...), custom_call_target="tpu_custom_call" | custom-call | flops 49999998976 | bytes 150000000 | tf_op jit(solution)/shard_map/middle_part/pallas_call | solution.py:869
  167.7 0.0 reduce-scatter.2.cloned.1.call-update
  167.7 1.1 copy-done
  168.8 6.0 %collective-permute-start.4 = (bf16[864,768]{1,0:T(8,128)(2,1)S(1)}, bf16[864,768]{1,0:T(8,128)(2,1)S(1)}, u32[]{:S(2)}, u32[]{:S(2)}) collective-permute-start(bf16[864,768]{1,0:T(8,128)(2,1)S(1)} %get-tuple-element.72.layer), channel_id=1, source_target_pairs={{2,4},{3,5},{4,2},{5,3},{10,12},{11,13},{12,10},{13,11},{18,20},{1... | collective-permute-start | bytes 3981320 | tf_op jit(solution)/shard_map/ppermute | solution.py:1393
  174.8 43.6 %attention_back.1.dproj_in = bf16[3,3584,192]{2,1,0:T(8,128)(2,1)} custom-call(s32[27,128]{1,0:T(8,128)} %get-tuple-element.57.numbers, s32[1,128]{1,0:T(1,128)} %get-tuple-element.58.before, s32[3968,1]{1,0:T(8,128)} %get-tuple-element.59.idc, s32[1,3968]{1,0:T(1,128)} %get-tuple-element.60.idr, bf16[3,3968,128]{2,1,0:T(8,128)(2,1)} %get-tuple-element.62.q.q_in, ...), custom_call_target="tpu_custom_call" | custom-call | flops 51000000512 | bytes 153000000 | tf_op jit(solution)/shard_map/attention_back/pallas_call | solution.py:663
  218.4 0.0 reduce-scatter.2.cloned.1.call-done
  218.4 95.4 %finish.1 = (bf16[3,288,768]{2,1,0:T(8,128)(2,1)}, f32[8,768]{1,0:T(8,128)}, bf16[4,144,768]{2,1,0:T(8,128)(2,1)}, bf16[8,128,768]{2,1,0:T(8,128)(2,1)}) custom-call(bf16[3,3584,192]{2,1,0:T(8,128)(2,1)} %attention_back.1.dproj_in, bf16[3456,768]{1,0:T(8,128)(2,1)} %get-tuple-element.79.normed_in, bf16[3456,768]{1,0:T(8,128)(2,1)} %get-tuple-element.80.full_in, ...), custom_call_target="tpu_custom_call" | custom-call | flops 60000002048 | bytes 180000000 | tf_op jit(solution)/shard_map/finish/pallas_call | solution.py:1199
  313.9 1.1 copy-done.8
  314.9 6.7 %outputs.1 = (bf16[864,768]{1,0:T(8,128)(2,1)}, f32[864,768]{1,0:T(8,128)}, f32[576,768]{1,0:T(8,128)}, f32[192,768]{1,0:T(8,128)}, f32[768,384]{1,0:T(8,128)}, ...) custom-call(bf16[864,768]{1,0:T(8,128)(2,1)} %copy-done, ...), custom_call_target="tpu_custom_call" | custom-call | tf_op jit(solution)/shard_map/outputs/pallas_call | solution.py:1297
  (23 shorter events, 0.1 us)
Async XLA Ops:
  7.2 1.5 copy-start.9
  7.2 211.2 %reduce-scatter.2.cloned.1.call-start = ((), (), s32[]{:S(2)}) async-start(), calls=%async_computation.1 | async-start | bytes 3932160 | tf_op jit(solution)/shard_map/reduce_scatter | solution.py:1357
  10.4 73.2 %copy-start.10 = (bf16[864,768]{1,0:T(8,128)(2,1)S(1)}, bf16[864,768]{1,0:T(8,128)(2,1)}, u32[]{:S(2)}) copy-start(bf16[864,768]{1,0:T(8,128)(2,1)} %cot.1) | copy-start | bytes 3981316
  81.8 27.3 %collective-permute-start.3 = (bf16[4,128,768]{2,1,0:T(8,128)(2,1)}, bf16[4,128,768]{2,1,0:T(8,128)(2,1)S(1)}, u32[]{:S(2)}, u32[]{:S(2)}) collective-permute-start(bf16[4,128,768]{2,1,0:T(8,128)(2,1)} %get-tuple-element.69.rest_0_), channel_id=1, source_target_pairs={{0,24},{4,28},{8,0},{12,4},{16,8},{20,12},{24,16},{28,20},{1,25},{... | collective-permute-start | bytes 2359304 | tf_op jit(solution)/shard_map/ppermute | solution.py:1351
  83.1 26.0 %collective-permute-start.2 = (bf16[4,128,768]{2,1,0:T(8,128)(2,1)}, bf16[4,128,768]{2,1,0:T(8,128)(2,1)S(1)}, u32[]{:S(2)}, u32[]{:S(2)}) collective-permute-start(bf16[4,128,768]{2,1,0:T(8,128)(2,1)} %get-tuple-element.69.rest_0_), channel_id=1, source_target_pairs={{0,16},{4,20},{8,24},{12,28},{16,0},{20,4},{24,8},{28,12},{1,17},{... | collective-permute-start | bytes 2359304 | tf_op jit(solution)/shard_map/ppermute | solution.py:1351
  83.3 33.9 %collective-permute-start.1 = (bf16[4,128,768]{2,1,0:T(8,128)(2,1)}, bf16[4,128,768]{2,1,0:T(8,128)(2,1)S(1)}, u32[]{:S(2)}, u32[]{:S(2)}) collective-permute-start(bf16[4,128,768]{2,1,0:T(8,128)(2,1)} %get-tuple-element.69.rest_0_), channel_id=1, source_target_pairs={{0,8},{4,12},{8,16},{12,20},{16,24},{20,28},{24,0},{28,4},{1,9},{5... | collective-permute-start | bytes 2359304 | tf_op jit(solution)/shard_map/ppermute | solution.py:1351
  83.6 34.5 %collective-permute-start = (bf16[864,768]{1,0:T(8,128)(2,1)S(1)}, bf16[864,768]{1,0:T(8,128)(2,1)S(1)}, u32[]{:S(2)}, u32[]{:S(2)}) collective-permute-start(bf16[864,768]{1,0:T(8,128)(2,1)S(1)} %copy-done.10), channel_id=1, source_target_pairs={{2,4},{3,5},{4,2},{5,3},{10,12},{11,13},{12,10},{13,11},{18,20},{1... | collective-permute-start | bytes 3981320 | tf_op jit(solution)/shard_map/ppermute | solution.py:1387
  85.5 33.7 %copy-start.1 = (bf16[4,128,768]{2,1,0:T(8,128)(2,1)S(1)}, bf16[4,128,768]{2,1,0:T(8,128)(2,1)}, u32[]{:S(2)}) copy-start(bf16[4,128,768]{2,1,0:T(8,128)(2,1)} %get-tuple-element.69.rest_0_) | copy-start | bytes 2359300
  85.6 33.6 %copy-start.2 = (f32[768]{0:T(1024)S(1)}, f32[768]{0:T(1024)}, u32[]{:S(2)}) copy-start(f32[768]{0:T(1024)} %b_out.1) | copy-start | bytes 9220
  85.6 33.6 %copy-start.3 = (f32[768]{0:T(1024)S(1)}, f32[768]{0:T(1024)}, u32[]{:S(2)}) copy-start(f32[768]{0:T(1024)} %gain.4) | copy-start | bytes 9220
  85.6 33.6 %copy-start.4 = (f32[768]{0:T(1024)S(1)}, f32[768]{0:T(1024)}, u32[]{:S(2)}) copy-start(f32[768]{0:T(1024)} %shift.3) | copy-start | bytes 9220
  85.6 33.6 %copy-start.5 = (f32[768]{0:T(1024)S(1)}, f32[768]{0:T(1024)}, u32[]{:S(2)}) copy-start(f32[768]{0:T(1024)} %b_down.1) | copy-start | bytes 9220
  85.6 33.6 %copy-start.6 = (bf16[864,768]{1,0:T(8,128)(2,1)S(1)}, bf16[864,768]{1,0:T(8,128)(2,1)}, u32[]{:S(2)}) copy-start(bf16[864,768]{1,0:T(8,128)(2,1)} %get-tuple-element.66.tok) | copy-start | bytes 3981316
  85.6 33.6 %copy-start.7 = (f32[4,1,384]{2,1,0:T(1,128)S(1)}, f32[4,1,384]{2,1,0:T(1,128)}, u32[]{:S(2)}) copy-start(f32[4,1,384]{2,1,0:T(1,128)} %get-tuple-element.68.b_up) | copy-start | bytes 18436
  118.1 1.1 copy-start.11
  167.7 1.1 copy-start
  168.8 145.1 %collective-permute-start.4 = (bf16[864,768]{1,0:T(8,128)(2,1)S(1)}, bf16[864,768]{1,0:T(8,128)(2,1)S(1)}, u32[]{:S(2)}, u32[]{:S(2)}) collective-permute-start(bf16[864,768]{1,0:T(8,128)(2,1)S(1)} %get-tuple-element.72.layer), channel_id=1, source_target_pairs={{2,4},{3,5},{4,2},{5,3},{10,12},{11,13},{12,10},{13,11},{18,20},{1... | collective-permute-start | bytes 3981320 | tf_op jit(solution)/shard_map/ppermute | solution.py:1393
  313.9 1.1 copy-start.8
Sparse Core Ops, SparseCore 0:
  167.8 44.9 reduce-scatter.1
